TPU v7x, 32 devices: a whole 2x2x4 slice. The times are simulated.
32 devices in a mesh: dp: 8 (over y, x, core), fsdp: 4 (over z).
Axes of the slice: x: 2, y: 2, z: 4, core: 2. Of those that a mesh axis runs over, the one named last changes fastest.
Arguments:
- hidden_in: bfloat16 [16, 1024, 1536], P('dp', 'fsdp'), may hold values from -6 to 6
- cotangent: bfloat16 [16, 1024, 1536], P('dp', 'fsdp'), may hold values from -6 to 6
- in_proj: bfloat16 [1536, 6448], P(('dp', 'fsdp')), may hold values from -0.15625 to 0.15625
- out_proj: bfloat16 [3072, 1536], P(('dp', 'fsdp')), may hold values from -0.109375 to 0.109375
- conv_params: bfloat16 [5, 3328], P(None, ('dp', 'fsdp')), may hold values from -0.5 to 0.5
- pre_gain: bfloat16 [1536], P(('dp', 'fsdp')), may hold values from 0.5 to 1.5
- gated_gain: bfloat16 [3072], P(('dp', 'fsdp')), may hold values from 0.5 to 1.5
- head_params: float32 [3, 48], replicated, may hold values from -6 to 2, as said below
Outputs:
- hidden_out: bfloat16 [16, 1024, 1536], P('dp', 'fsdp')
- grad_in: bfloat16 [16, 1024, 1536], P('dp', 'fsdp')
- in_proj_grad: float32 [1536, 6448], P(('dp', 'fsdp'))
- out_proj_grad: float32 [3072, 1536], P(('dp', 'fsdp'))
- conv_grad: float32 [5, 3328], P(None, ('dp', 'fsdp'))
- pre_gain_grad: float32 [1536], P(('dp', 'fsdp'))
- gated_gain_grad: float32 [3072], P(('dp', 'fsdp'))
- head_grad: float32 [3, 48], replicated
Inputs may be any that keep to these rules, and one draw needn't show every extreme that they name: `head_params`: row 0 holds each head's log decay coefficient (the decay rate is minus its exponential), row 1 each head's step bias, row 2 each head's skip coefficient.
All inputs are finite; a program needn't handle non-finite values.
Results may differ from a plain program's by a relative error of at most 0.0063.
The roundings to bfloat16 on the way count: a program that leaves them out, or rounds other values in their place, can miss the bound.
Values may be sent and summed in bfloat16 or wider, within the bound.
No kernel may reach another device: no remote copies, remote signals or barrier semaphores. Data moves between devices by JAX's collectives and lax.ppermute only.
A program may use at most 160 MiB of HBM per device.

v0:
```python
import jax
import jax.numpy as jnp
from jax import lax
from jax.experimental import pallas as pl
from jax.experimental.pallas import tpu as pltpu
from jax.sharding import Mesh
from jax.sharding import PartitionSpec as P

HEADS = 48
HEADDIM = 64
STATE = 128
CONV = 4
INNER = 3072
XBC = 3328
HALF = INNER // 2
LANES = 128
SEGS = 4
LIGHT = pl.CostEstimate(flops=1024, bytes_accessed=1024, transcendentals=0)
VMEM_LIMIT = 48 * 1024 * 1024
LOG2E = 1.4426950408889634

epsilon = 1e-05
f32 = jnp.float32
bf16 = jnp.bfloat16


def own_columns(array, core):
    chips = lax.axis_size("chip")
    width = array.shape[-1] // (2 * chips)
    parted = array.reshape(array.shape[:-1] + (chips, 2, width))
    picked = lax.dynamic_index_in_dim(parted, core, axis=parted.ndim - 2, keepdims=False)
    return picked.reshape(array.shape[:-1] + (chips * width,))


def to_partner(array):
    return lax.ppermute(array, "core", [(0, 1), (1, 0)])


def in_core_order(mine, theirs, core, axis):
    first = jnp.where(core == 0, mine, theirs)
    second = jnp.where(core == 0, theirs, mine)
    return jnp.stack([first, second], axis=axis)


def chip_dims():
    return (lax.axis_size("chip") // 2, 2, lax.axis_size("seg"))


def chip_place():
    chip = lax.axis_index("chip")
    return (chip // 2, chip % 2, lax.axis_index("seg"))


def moved(array, dim, by):
    sizes = chip_dims()
    index = lambda at: (at[0] * sizes[1] + at[1]) * sizes[2] + at[2]
    pairs = []
    for a in range(sizes[0]):
        for b in range(sizes[1]):
            for z in range(sizes[2]):
                to = [a, b, z]
                to[dim] = (to[dim] + by) % sizes[dim]
                pairs.append((index((a, b, z)), index(to)))
    return lax.ppermute(array, ("chip", "seg"), pairs)


def tie(*values):
    return lax.optimization_barrier(values)


def gather_step(data, dim):
    return [data] + [moved(data, dim, by) for by in range(1, chip_dims()[dim])]


def exchanged(array, by):
    line = lax.axis_size("seg")
    return lax.ppermute(array, "seg", [(at, at ^ by) for at in range(line)])


def plane_steps():
    a, b, _ = chip_dims()
    steps = [(at // b, at % b) for at in range(1, a * b)]
    return sorted(steps, key=lambda by: bool(by[0] and by[1]))


def near_steps():
    a, b, _ = chip_dims()
    return plane_steps()[: a + b - 2]


def far_steps():
    a, b, _ = chip_dims()
    return plane_steps()[a + b - 2 :]


def moved_plane(array, by_a, by_b):
    a, b, z = chip_dims()
    pairs = [
        ((at_a * b + at_b) * z + at_z, ((at_a + by_a) % a * b + (at_b + by_b) % b) * z + at_z)
        for at_a in range(a)
        for at_b in range(b)
        for at_z in range(z)
    ]
    return lax.ppermute(array, ("chip", "seg"), pairs)


def gather_plane(data, steps):
    return [moved_plane(data, *by) for by in steps]


def placed_kernel(plan, place_ref, *refs):
    sources, target, sems = refs[:-2], refs[-2], refs[-1]
    copies = []
    for source, lead, at, paired in plan:
        spot = [lax.rem(place_ref[dim] + (size - back), size) for dim, (back, size) in enumerate(at)]
        spot.append(place_ref[2 + lead])
        to = target.at[spot[0], spot[1], :, spot[2]] if paired else target.at[spot[0], spot[1], spot[2]]
        copies.append(pltpu.make_async_copy(sources[source].at[lead], to, sems.at[len(copies)]))
    for copy in copies:
        copy.start()
    for copy in copies:
        copy.wait()


def whole_matrix(gathered, paired, by_bits=False):
    a, b, z = chip_dims()
    at_a, at_b, at_z = chip_place()
    spots = [at_z ^ back if by_bits else (at_z + z - back) % z for back in range(z)]
    plan = [
        (source, back, ((by[0], a), (by[1], b)), paired)
        for source, by in enumerate([(0, 0)] + plane_steps())
        for back in range(z)
    ]
    block = gathered[0].shape[1:]
    shape = (a, b, 2, z) + block[1:] if paired else (a, b, z) + block
    anywhere = pl.BlockSpec(memory_space=pl.ANY)
    whole = pl.pallas_call(
        lambda *refs: placed_kernel(plan, *refs),
        out_shape=jax.ShapeDtypeStruct(shape, bf16),
        in_specs=[pl.BlockSpec(memory_space=pltpu.SMEM)] + [anywhere] * len(gathered),
        out_specs=pl.BlockSpec(memory_space=pltpu.VMEM),
        scratch_shapes=[pltpu.SemaphoreType.DMA((len(plan),))],
        compiler_params=pltpu.CompilerParams(vmem_limit_bytes=VMEM_LIMIT),
        cost_estimate=LIGHT,
    )(jnp.stack([at_a, at_b, *spots]).astype(jnp.int32), *gathered)
    return whole.reshape(-1, shape[-1])


def total(terms):
    result = terms[0].astype(f32)
    for term in terms[1:]:
        result = result + term.astype(f32)
    return result


def reduce_send(terms, axis, dim, wire):
    place, size = chip_place()[dim], chip_dims()[dim]
    pick = lambda at: [lax.dynamic_index_in_dim(term, at, axis=axis, keepdims=False) for term in terms]
    received = [moved(total(pick((place + by) % size)).astype(wire), dim, by) for by in range(1, size)]
    return pick(place), received


def plane_part(partials, by_a, by_b):
    (at_a, at_b, _), (a, b, _) = chip_place(), chip_dims()
    chip = (at_a + by_a) % a * b + (at_b + by_b) % b
    flat = [partial.reshape((a * b,) + partial.shape[2:]) for partial in partials]
    return jnp.concatenate([lax.dynamic_index_in_dim(array, chip, axis=0, keepdims=False) for array in flat], axis=-1)


def reduce_plane(partials, steps):
    return [moved_plane(plane_part(partials, *by), *by) for by in steps]


def reduce_z(firsts):
    joined = jnp.concatenate([total(kept + received) for kept, received in firsts], axis=-1)
    return [reduce_send([joined], 0, 2, bf16)]


def reduce_end(third):
    return total(third[0][0] + third[0][1])


def arrivals(parts):
    return [received for _, received in parts]


def arrived(parts, received):
    return [(kept, new) for (kept, _), new in zip(parts, received)]


def line_perm(turn, back):
    line = lax.axis_size("seg")
    parts = line // SEGS
    pairs = []
    for core in range(2):
        for place in range(line):
            half, odd = divmod(place % SEGS, 2)
            source = core * line + place
            target = odd * line + (2 * core + (half ^ turn)) * parts + place // SEGS
            pairs.append((target, source) if back else (source, target))
    return pairs


def swapped(pair, turn):
    return [jnp.where(turn == 0, pair[0], pair[1]), jnp.where(turn == 0, pair[1], pair[0])]


def send_sequence(array, place):
    pieces = swapped([array[0], array[1]], (place % SEGS) // 2)
    return [lax.ppermute(piece, ("core", "seg"), line_perm(turn, False)) for turn, piece in enumerate(pieces)]


def order_sequence(got, place):
    parts = lax.axis_size("seg") // SEGS
    return jnp.stack(swapped(got, (place // parts) % 2))


def send_back(ordered, place):
    parts = lax.axis_size("seg") // SEGS
    pieces = swapped([ordered[0], ordered[1]], (place // parts) % 2)
    return [lax.ppermute(piece, ("core", "seg"), line_perm(turn, True)) for turn, piece in enumerate(pieces)]


def order_back(got, place):
    return jnp.stack(swapped(got, (place % SEGS) // 2))


def part_pairs(step):
    line = lax.axis_size("seg")
    parts = line // SEGS
    return [(i, i + step) for i in range(line) if 0 <= i + step < line and i // parts == (i + step) // parts]


def entering(decay, state, step):
    parts = lax.axis_size("seg") // SEGS
    total = jnp.zeros_like(state)
    for _ in range(parts - 1):
        total = lax.ppermute(decay * total + state, "seg", part_pairs(step))
    return total


def borrowed(array, step):
    parts = lax.axis_size("seg") // SEGS
    if parts == 1:
        return jnp.zeros_like(array)
    return lax.ppermute(array, "seg", part_pairs(step))


def spilled(grad, edge, taps):
    if lax.axis_size("seg") == SEGS:
        return grad
    edge = borrowed(edge, -1)
    spill = jnp.stack(
        [
            sum(taps[k] * edge[CONV - 1 - k - early] for k in range(CONV - early))
            for early in range(CONV - 1, 0, -1)
        ]
    )
    at = grad.shape[0] - CONV + 1
    return grad.at[at:].set((grad[at:].astype(f32) + spill).astype(bf16))


def dot(a, b, contract):
    return lax.dot_general(a, b, (contract, ((), ())), preferred_element_type=f32)


def normed_kernel(slabs, core_ref, mine_ref, other_ref, gain_ref, normed_ref, turned_ref):
    own = lax.rem(pl.program_id(0), 2) == core_ref[0]
    hidden = jnp.where(own, mine_ref[0], other_ref[0]).astype(f32)
    scale = lax.rsqrt(jnp.mean(hidden * hidden, axis=1, keepdims=True) + epsilon)
    normed = hidden * scale * gain_ref[...]
    normed_ref[...] = normed.astype(bf16)
    turned = normed.T.astype(bf16)
    for to, at, size in slabs:
        turned_ref[to : to + size] = turned[at : at + size]


def normed_tokens(core, mine, other, gain, rows):
    segs, seg_len, width = 2 * mine.shape[0], mine.shape[1], mine.shape[2]
    a, b, z = chip_dims()
    group = 2 * z * rows
    inside = rows % 16 == 0
    slabs = [(0, 0, width)]
    if inside:
        slabs = [
            (chip * group + (at * 2 + core_at) * rows, chip * group + (core_at * z + at) * rows, rows)
            for chip in range(a * b)
            for core_at in range(2)
            for at in range(z)
        ]
    normed, turned = pl.pallas_call(
        lambda *refs: normed_kernel(slabs, *refs),
        grid_spec=pltpu.PrefetchScalarGridSpec(
            num_scalar_prefetch=1,
            grid=(segs,),
            in_specs=[
                pl.BlockSpec((1, seg_len, width), lambda i, core: (i // 2, 0, 0)),
                pl.BlockSpec((1, seg_len, width), lambda i, core: (i // 2, 0, 0)),
                pl.BlockSpec((1, width), lambda i, core: (0, 0)),
            ],
            out_specs=(
                pl.BlockSpec((seg_len, width), lambda i, core: (i, 0)),
                pl.BlockSpec((width, seg_len), lambda i, core: (0, i)),
            ),
        ),
        out_shape=(
            jax.ShapeDtypeStruct((segs * seg_len, width), bf16),
            jax.ShapeDtypeStruct((width, segs * seg_len), bf16),
        ),
        compiler_params=pltpu.CompilerParams(dimension_semantics=("arbitrary",), vmem_limit_bytes=VMEM_LIMIT),
        cost_estimate=LIGHT,
    )(core.reshape(1).astype(jnp.int32), mine, other, gain.reshape(1, width))
    if not inside:
        turned = turned.reshape(a, b, 2, z, rows, -1).transpose(0, 1, 3, 2, 4, 5).reshape(turned.shape)
    return normed, turned


def mixed_kernel(gated_ref, scale_ref, gain_ref, mixed_ref, turned_ref):
    mixed = gated_ref[...] * scale_ref[...] * gain_ref[...]
    mixed_ref[...] = mixed.astype(bf16)
    turned_ref[...] = mixed.T.astype(bf16)


def mixed_tokens(gated, scale, gain, seg_len):
    length, width = gated.shape
    return pl.pallas_call(
        mixed_kernel,
        grid=(length // seg_len,),
        in_specs=[
            pl.BlockSpec((seg_len, width), lambda i: (i, 0)),
            pl.BlockSpec((seg_len, 1), lambda i: (i, 0)),
            pl.BlockSpec((1, width), lambda i: (0, 0)),
        ],
        out_specs=(
            pl.BlockSpec((seg_len, width), lambda i: (i, 0)),
            pl.BlockSpec((width, seg_len), lambda i: (0, i)),
        ),
        out_shape=(
            jax.ShapeDtypeStruct((length, width), bf16),
            jax.ShapeDtypeStruct((width, length), bf16),
        ),
        compiler_params=pltpu.CompilerParams(dimension_semantics=("arbitrary",), vmem_limit_bytes=VMEM_LIMIT),
        cost_estimate=LIGHT,
    )(gated, scale, gain.reshape(1, width))


def columns_of(pair):
    return pl.ds(pair * LANES, LANES)


def low_half(shape):
    return lax.broadcasted_iota(jnp.int32, shape, len(shape) - 1) < HEADDIM


def pair_columns(array, pair, low):
    rows = array.shape[0]
    first = jnp.broadcast_to(array[:, 2 * pair : 2 * pair + 1], (rows, LANES))
    second = jnp.broadcast_to(array[:, 2 * pair + 1 : 2 * pair + 2], (rows, LANES))
    return jnp.where(low, first, second)


def conv_parts(current, before, taps):
    rows = current.shape[0]
    padded = jnp.concatenate([before, current], axis=0)
    seen = [padded[8 - CONV + 1 + k : 8 - CONV + 1 + k + rows] for k in range(CONV - 1)] + [current]
    total = taps[CONV : CONV + 1]
    for k in range(CONV):
        total = total + taps[k : k + 1] * seen[k]
    return total, seen


def step_terms(raw, head, seg_len):
    shifted = raw + head[1:2]
    step = jnp.maximum(shifted, 0.0) + jnp.log1p(jnp.exp(-jnp.abs(shifted)))
    log_decay = step * head[0:1]
    at_or_before = lax.broadcasted_iota(jnp.int32, (seg_len, seg_len), 0) >= lax.broadcasted_iota(
        jnp.int32, (seg_len, seg_len), 1
    )
    sums = lax.dot_general(
        jnp.where(at_or_before, 1.0, 0.0), log_decay, (((1,), (0,)), ((), ())),
        precision=lax.Precision.HIGHEST, preferred_element_type=f32,
    )
    return shifted, step, log_decay, sums * LOG2E


def forward_kernel(
    proj_ref, taps_ref, head_ref, skip_ref, rim_ref, init_ref,
    values_ref, prior_ref, final_ref, last_ref, state_ref, tail_ref,
):
    seg_len = proj_ref.shape[0]
    half = seg_len // 2

    @pl.when(pl.program_id(0) == 0)
    def _():
        state_ref[...] = init_ref[...]
        tail_ref[...] = rim_ref[...]

    def activated(begin):
        at = pl.ds(begin, LANES)
        total, _ = conv_parts(proj_ref[:, at], tail_ref[:, at], taps_ref[:, at])
        return total * jax.nn.sigmoid(total)

    b_low = activated(HALF).astype(bf16)
    b_turned = activated(HALF).T.astype(bf16)
    c_low = activated(HALF + STATE).astype(bf16)
    _, step, _, sums = step_terms(proj_ref[:, HALF + 2 * STATE :], head_ref, seg_len)
    sums_turned, step_turned = sums.T, step.T
    scores = dot(c_low, b_low, ((1,), (1,)))
    kept = lax.broadcasted_iota(jnp.int32, (half, half), 0) >= lax.broadcasted_iota(jnp.int32, (half, half), 1)
    first_scores = jnp.where(kept, scores[:half, :half], 0.0)
    later_scores = scores[half:, :half]
    second_scores = jnp.where(kept, scores[half:, half:], 0.0)
    low = low_half((seg_len, LANES))
    last_ref[...] = jnp.broadcast_to(sums[seg_len - 1 :], last_ref.shape)

    for pair in range(HEADS // 4):
        at = columns_of(pair)
        x_values = activated(pair * LANES)
        x_low = x_values.astype(bf16)
        sums_pair = pair_columns(sums, pair, low)
        last_pair = sums_pair[seg_len - 1 :]
        carry = jnp.exp2(last_pair - sums_pair) * pair_columns(step, pair, low)
        scaled_x = (carry * x_low.astype(f32)).astype(bf16)
        prior = state_ref[:, at]
        prior_low = prior.astype(bf16)
        prior_ref[0, :, at] = prior_low
        from_state = jnp.exp2(sums_pair) * dot(c_low, prior_low, ((1,), (0,)))
        state_ref[:, at] = jnp.exp2(last_pair) * prior + dot(b_turned, scaled_x, ((1,), (0,)))
        early, late = 0.0, 0.0
        for side in range(2):
            head = 2 * pair + side
            x_side = jnp.where(low if side == 0 else ~low, x_values, 0.0).astype(bf16)
            at_token = jnp.broadcast_to(sums[:, head : head + 1], (seg_len, half))
            at_source, source_step = sums_turned[head : head + 1], step_turned[head : head + 1]
            first = jnp.exp2(jnp.minimum(at_token[:half] - at_source[:, :half], 0.0)) * first_scores
            first = (first * source_step[:, :half]).astype(bf16)
            later = jnp.exp2(at_token[half:] - at_source[:, :half]) * later_scores
            later = (later * source_step[:, :half]).astype(bf16)
            second = jnp.exp2(jnp.minimum(at_token[half:] - at_source[:, half:], 0.0)) * second_scores
            second = (second * source_step[:, half:]).astype(bf16)
            early = early + dot(first, x_side[:half], ((1,), (0,)))
            late = late + dot(jnp.concatenate([later, second], axis=1), x_side, ((1,), (0,)))
        intra = jnp.concatenate([early, late], axis=0)
        values_ref[:, at] = intra + from_state + skip_ref[:, at] * x_values

    tail_ref[...] = proj_ref[seg_len - 8 :, : HALF + 2 * STATE]
    final_ref[...] = state_ref[...]


def full_block(shape):
    return pl.BlockSpec(shape, lambda *_: (0,) * len(shape))


def scan_forward(proj, taps, head, skip, rim, init, seg_len):
    segs = proj.shape[0] // seg_len
    wide = HALF + 2 * STATE
    return pl.pallas_call(
        forward_kernel,
        grid=(segs,),
        out_shape=(
            jax.ShapeDtypeStruct((proj.shape[0], HALF), f32),
            jax.ShapeDtypeStruct((segs, STATE, HALF), bf16),
            jax.ShapeDtypeStruct((STATE, HALF), f32),
            jax.ShapeDtypeStruct((segs * 8, LANES), f32),
        ),
        in_specs=[
            pl.BlockSpec((seg_len, proj.shape[1]), lambda i: (i, 0)),
            full_block((8, wide)),
            full_block((8, LANES)),
            full_block((1, HALF)),
            full_block((8, wide)),
            full_block((STATE, HALF)),
        ],
        out_specs=(
            pl.BlockSpec((seg_len, HALF), lambda i: (i, 0)),
            pl.BlockSpec((1, STATE, HALF), lambda i: (i, 0, 0)),
            full_block((STATE, HALF)),
            pl.BlockSpec((8, LANES), lambda i: (i, 0)),
        ),
        scratch_shapes=[pltpu.VMEM((STATE, HALF), f32), pltpu.VMEM((8, wide), f32)],
        compiler_params=pltpu.CompilerParams(
            dimension_semantics=("arbitrary",), vmem_limit_bytes=VMEM_LIMIT
        ),
        cost_estimate=LIGHT,
    )(proj, taps, head, skip, rim, init)


def split_dot(array, other):
    high = array.astype(bf16)
    rest = (array - high.astype(f32)).astype(bf16)
    return dot(high, other, ((1,), (0,))) + dot(rest, other, ((1,), (0,)))


def backward_kernel(
    group, proj_ref, before_ref, taps_ref, rim_ref, shared_ref, shared_before_ref, shared_taps_ref, shared_rim_ref,
    head_ref, skip_ref, end_ref, prior_ref, values_ref, grad_ref, core_ref,
    grad_x_ref, mine_ref, theirs_ref, grad_raw_ref, taps_grad_ref, skip_grad_ref, head_grad_ref, edge_ref, start_ref,
    later_ref, local_ref, scaled_ref, grad_state_ref, inner_ref, source_ref, carry_ref, decay_ref,
):
    seg_len = proj_ref.shape[0]
    half = seg_len // 2
    turn = pl.program_id(0)

    @pl.when(turn == 0)
    def _():
        later_ref[...] = end_ref[...]
        edge_ref[...] = jnp.zeros_like(edge_ref)
        taps_grad_ref[...] = jnp.zeros_like(taps_grad_ref)
        skip_grad_ref[...] = jnp.zeros_like(skip_grad_ref)
        head_grad_ref[...] = jnp.zeros_like(head_grad_ref)

    first_segment = turn == pl.num_programs(0) - 1

    def conv_at(at, current, ahead, taps, rim):
        before = jnp.where(first_segment, rim[:, at], ahead[:, at])
        return conv_parts(current[:, at], before, taps[:, at])

    def activated(begin):
        total, _ = conv_at(pl.ds(begin, LANES), shared_ref, shared_before_ref, shared_taps_ref, shared_rim_ref)
        return total * jax.nn.sigmoid(total)

    b_values = activated(0)
    c_values = activated(STATE)
    b_low, c_low, c_turned = b_values.astype(bf16), c_values.astype(bf16), c_values.T.astype(bf16)
    shifted, step, log_decay, sums = step_terms(shared_ref[:, 2 * STATE :], head_ref, seg_len)
    sums_turned = sums.T
    scores = dot(b_low, c_low, ((1,), (1,)))
    kept = lax.broadcasted_iota(jnp.int32, (half, half), 0) <= lax.broadcasted_iota(jnp.int32, (half, half), 1)
    first_scores = jnp.where(kept, scores[:half, :half], 0.0)
    later_scores = scores[:half, half:]
    second_scores = jnp.where(kept, scores[half:, half:], 0.0)
    low = low_half((seg_len, LANES))
    first_grad, later_grad, second_grad = 0.0, 0.0, 0.0

    pairs = grad_ref.shape[1] // LANES
    for pair in range(pairs):
        at = columns_of(pair)
        total, seen = conv_at(at, proj_ref, before_ref, taps_ref, rim_ref)
        sigmoid = jax.nn.sigmoid(total)
        x_values = total * sigmoid
        x_low = x_values.astype(bf16)
        x_wide = x_low.astype(f32)
        sums_pair = pair_columns(sums, group * pairs + pair, low)
        step_pair = pair_columns(step, group * pairs + pair, low)
        last_pair = sums_pair[seg_len - 1 :]
        gap = jnp.exp2(last_pair - sums_pair)
        scaled_ref[:, at] = (gap * step_pair * x_wide).astype(bf16)
        grad_values = grad_ref[:, at]
        grad_state_ref[:, at] = (grad_values * jnp.exp2(sums_pair)).astype(bf16)
        later = later_ref[:, at]
        later_low = later.astype(bf16)
        local_ref[:, at] = later_low
        prior = prior_ref[0, :, at]
        decay_ref[:, at] = jnp.broadcast_to(
            jnp.sum(later * prior.astype(f32), axis=0, keepdims=True), (8, LANES)
        )
        grad_prior = dot(c_turned, grad_state_ref[:, at], ((1,), (0,)))
        later_ref[:, at] = jnp.exp2(last_pair) * later + grad_prior
        grad_scaled = dot(b_low, later_low, ((1,), (0,)))
        stepped = (step_pair * x_wide).astype(bf16)
        early, late = 0.0, 0.0
        for side in range(2):
            head = 2 * (group * pairs + pair) + side
            grad_low = jnp.where(low if side == 0 else ~low, grad_values, 0.0).astype(bf16)
            at_source = jnp.broadcast_to(sums[:, head : head + 1], (seg_len, half))
            at_token = sums_turned[head : head + 1]
            grad_weights = dot(stepped, grad_low, ((1,), (1,)))
            first = jnp.exp2(jnp.minimum(at_token[:, :half] - at_source[:half], 0.0))
            after = jnp.exp2(at_token[:, half:] - at_source[:half])
            second = jnp.exp2(jnp.minimum(at_token[:, half:] - at_source[half:], 0.0))
            first_grad = first_grad + first * grad_weights[:half, :half]
            later_grad = later_grad + after * grad_weights[:half, half:]
            second_grad = second_grad + second * grad_weights[half:, half:]
            upper = jnp.concatenate([first * first_scores, after * later_scores], axis=1).astype(bf16)
            early = early + dot(upper, grad_low, ((1,), (0,)))
            late = late + dot((second * second_scores).astype(bf16), grad_low[half:], ((1,), (0,)))
        inner = jnp.concatenate([early, late], axis=0)
        skip = skip_ref[:, at]
        skip_grad_ref[:, at] += jnp.sum(grad_values * x_values, axis=0, keepdims=True)
        inner_ref[:, at] = grad_values * (values_ref[:, at] - skip * x_values)
        source_ref[:, at] = x_wide * inner
        carry_ref[:, at] = x_wide * grad_scaled
        grad_x = skip * grad_values + step_pair * (inner + gap * grad_scaled)
        grad_total = grad_x * (sigmoid * (1.0 + total * (1.0 - sigmoid)))
        for k in range(CONV):
            taps_grad_ref[k : k + 1, at] += jnp.sum(grad_total * seen[k], axis=0, keepdims=True)
        taps_grad_ref[CONV : CONV + 1, at] += jnp.sum(grad_total, axis=0, keepdims=True)
        extended = jnp.concatenate([grad_total, edge_ref[:, at]], axis=0)
        edge_ref[:, at] = grad_total[:8]
        taps = taps_ref[:, at]
        grad_conv = taps[CONV - 1 : CONV] * grad_total
        for k in range(CONV - 1):
            grad_conv = grad_conv + taps[k : k + 1] * extended[CONV - 1 - k : CONV - 1 - k + seg_len]
        grad_x_ref[:, at] = grad_conv.astype(bf16)

    width = grad_ref.shape[1]
    channel = lax.broadcasted_iota(jnp.int32, (width, LANES), 0) // HEADDIM + group * width // HEADDIM
    heads = jnp.where(channel == lax.broadcasted_iota(jnp.int32, (width, LANES), 1), 1.0, 0.0).astype(bf16)
    tail = jnp.exp2(sums[seg_len - 1 :] - sums)
    source_grad = split_dot(source_ref[...], heads)
    step_grad = source_grad + tail * split_dot(carry_ref[...], heads)
    used = step * step_grad
    sum_grad = split_dot(inner_ref[...], heads) - used
    at_last = jnp.sum(used - step * source_grad, axis=0, keepdims=True)
    at_last = at_last + split_dot(decay_ref[...], heads)[:1] * jnp.exp2(sums[seg_len - 1 :])
    is_last = lax.broadcasted_iota(jnp.int32, (seg_len, LANES), 0) == seg_len - 1
    sum_grad = sum_grad + jnp.where(is_last, at_last, 0.0)
    at_or_after = lax.broadcasted_iota(jnp.int32, (seg_len, seg_len), 0) <= lax.broadcasted_iota(
        jnp.int32, (seg_len, seg_len), 1
    )
    log_grad = lax.dot_general(
        jnp.where(at_or_after, 1.0, 0.0), sum_grad, (((1,), (0,)), ((), ())),
        precision=lax.Precision.HIGHEST, preferred_element_type=f32,
    )
    grad_raw = (step_grad + head_ref[0:1] * log_grad) * jax.nn.sigmoid(shifted)
    grad_raw_ref[...] = grad_raw
    head_grad_ref[CONV + 1 : CONV + 2] += jnp.sum(log_grad * log_decay, axis=0, keepdims=True)
    head_grad_ref[CONV + 2 : CONV + 3] += jnp.sum(grad_raw, axis=0, keepdims=True)

    first_low = jnp.where(kept, first_grad, 0.0)
    second_low = jnp.where(kept, second_grad, 0.0)
    grad_scores = jnp.concatenate(
        [
            jnp.concatenate([first_low, later_grad], axis=1),
            jnp.concatenate([jnp.zeros_like(first_low), second_low], axis=1),
        ],
        axis=0,
    )
    start_ref[...] = later_ref[...]
    grad_b = dot(scaled_ref[...], local_ref[...], ((1,), (1,))) + dot(
        grad_scores.astype(bf16), c_low, ((1,), (0,))
    )
    grad_c = dot(grad_state_ref[...], prior_ref[0], ((1,), (1,))) + dot(
        grad_scores.T.astype(bf16), b_low, ((1,), (0,))
    )
    first = core_ref[0] == 0
    mine_ref[...] = jnp.where(first, grad_b, grad_c)
    theirs_ref[...] = jnp.where(first, grad_c, grad_b)


GROUPS = 1


def scan_backward(group, core, proj, taps, head, skip, rim, end, prior, values, grad_values, seg_len):
    length = proj.shape[0]
    segs = length // seg_len
    width, shared = HALF // GROUPS, proj.shape[1] - HALF
    back = lambda width, at=0: pl.BlockSpec((seg_len, width), lambda i: (segs - 1 - i, at))
    row_ahead = lambda i: jnp.maximum((segs - 1 - i) * (seg_len // 8) - 1, 0)
    ahead = lambda width, at: pl.BlockSpec((8, width), lambda i: (row_ahead(i), at))
    column = lambda rows, width, at: pl.BlockSpec((rows, width), lambda i: (0, at))
    both = HALF // shared
    return pl.pallas_call(
        lambda *refs: backward_kernel(group, *refs),
        grid=(segs,),
        out_shape=(
            jax.ShapeDtypeStruct((length, width), bf16),
            jax.ShapeDtypeStruct((length, STATE), f32),
            jax.ShapeDtypeStruct((length, STATE), f32),
            jax.ShapeDtypeStruct((length, LANES), f32),
            jax.ShapeDtypeStruct((8, width), f32),
            jax.ShapeDtypeStruct((1, width), f32),
            jax.ShapeDtypeStruct((8, LANES), f32),
            jax.ShapeDtypeStruct((8, width), f32),
            jax.ShapeDtypeStruct((STATE, width), f32),
        ),
        in_specs=[
            back(width, group),
            ahead(width, group),
            column(8, width, group),
            column(8, width, group),
            back(shared, both),
            ahead(shared, both),
            column(8, shared, both),
            column(8, shared, both),
            full_block((8, LANES)),
            column(1, width, group),
            column(STATE, width, group),
            pl.BlockSpec((1, STATE, width), lambda i: (segs - 1 - i, 0, group)),
            back(width, group),
            back(width, group),
            pl.BlockSpec(memory_space=pltpu.SMEM),
        ],
        out_specs=(
            back(width),
            back(STATE),
            back(STATE),
            back(LANES),
            full_block((8, width)),
            full_block((1, width)),
            full_block((8, LANES)),
            full_block((8, width)),
            full_block((STATE, width)),
        ),
        scratch_shapes=[
            pltpu.VMEM((STATE, width), f32),
            pltpu.VMEM((STATE, width), bf16),
            pltpu.VMEM((seg_len, width), bf16),
            pltpu.VMEM((seg_len, width), bf16),
            pltpu.VMEM((seg_len, width), f32),
            pltpu.VMEM((seg_len, width), f32),
            pltpu.VMEM((seg_len, width), f32),
            pltpu.VMEM((8, width), f32),
        ],
        compiler_params=pltpu.CompilerParams(
            dimension_semantics=("arbitrary",), vmem_limit_bytes=VMEM_LIMIT
        ),
        cost_estimate=LIGHT,
    )(
        proj, proj, taps, rim, proj, proj, taps, rim, head, skip, end, prior, values, grad_values,
        core.reshape(1).astype(jnp.int32),
    )


def half_kernel(transposed, count, core_ref, *refs):
    inputs, mine_ref, theirs_ref = refs[: 2 * count], refs[-2], refs[-1]
    total = refs[2 * count][...] if len(refs) > 2 * count + 2 else 0.0
    for left, right in zip(inputs[:count], inputs[count:]):
        total = total + dot(left[...], right[...], ((1,), (1 if transposed else 0,)))
    own = lax.rem(pl.program_id(0), 2) == core_ref[0]

    @pl.when(own)
    def _():
        mine_ref[0] = total

    @pl.when(jnp.logical_not(own))
    def _():
        theirs_ref[0] = total.astype(bf16)


def half_products(core, terms, seg_len, width, transposed, base=()):
    length = terms[0][0].shape[0]
    left = [pl.BlockSpec((seg_len, array.shape[1]), lambda i, core: (i, 0)) for array, _, _ in terms]
    right = []
    for array, matrix, at in terms:
        if transposed:
            right.append(pl.BlockSpec((width, array.shape[1]), lambda i, core, at=at: (0, at(core[0]))))
        else:
            right.append(pl.BlockSpec(matrix.shape, lambda i, core: (0, 0)))
    depth = sum(array.shape[1] for array, _, _ in terms)
    mine, theirs = pl.pallas_call(
        lambda *refs: half_kernel(transposed, len(terms), *refs),
        grid_spec=pltpu.PrefetchScalarGridSpec(
            num_scalar_prefetch=1,
            grid=(length // seg_len,),
            in_specs=left + right + [pl.BlockSpec((seg_len, width), lambda i, core: (i, 0)) for _ in base],
            out_specs=[pl.BlockSpec((1, seg_len, width), lambda i, core: (i // 2, 0, 0))] * 2,
        ),
        out_shape=(
            jax.ShapeDtypeStruct((length // seg_len // 2, seg_len, width), f32),
            jax.ShapeDtypeStruct((length // seg_len // 2, seg_len, width), bf16),
        ),
        compiler_params=pltpu.CompilerParams(dimension_semantics=("arbitrary",), vmem_limit_bytes=VMEM_LIMIT),
        cost_estimate=LIGHT,
    )(core.reshape(1).astype(jnp.int32), *[array for array, _, _ in terms], *[matrix for _, matrix, _ in terms], *base)
    return mine, theirs


def shared_kernel(core_ref, proj_ref, rim_ref, taps_ref, mine_ref, other_ref, grad_ref, taps_grad_ref, edge_ref):
    total, seen = conv_parts(proj_ref[...], rim_ref[...], taps_ref[...])
    sigmoid = jax.nn.sigmoid(total)
    grad_total = mine_ref[...] + other_ref[...]
    grad_total = grad_total * (sigmoid * (1.0 + total * (1.0 - sigmoid)))
    sums = [jnp.sum(grad_total * part, axis=0, keepdims=True) for part in seen]
    sums = sums + [jnp.sum(grad_total, axis=0, keepdims=True), jnp.zeros((8 - CONV - 1, LANES), f32)]
    taps_grad_ref[...] = jnp.concatenate(sums, axis=0)
    edge_ref[...] = grad_total[:8]
    taps = taps_ref[...]
    extended = jnp.concatenate([grad_total, jnp.zeros((8, LANES), f32)], axis=0)
    grad_conv = taps[CONV - 1 : CONV] * grad_total
    for k in range(CONV - 1):
        grad_conv = grad_conv + taps[k : k + 1] * extended[CONV - 1 - k : CONV - 1 - k + grad_total.shape[0]]
    grad_ref[...] = grad_conv.astype(bf16)


def shared_backward(core, proj, rim, taps, mine, other):
    length = proj.shape[0]
    picked = lambda rows: pl.BlockSpec((rows, LANES), lambda i, core: (0, HALF // LANES + core[0]))
    whole = lambda rows: pl.BlockSpec((rows, LANES), lambda i, core: (0, 0))
    return pl.pallas_call(
        shared_kernel,
        grid_spec=pltpu.PrefetchScalarGridSpec(
            num_scalar_prefetch=1,
            grid=(1,),
            in_specs=[picked(length), picked(8), picked(8), whole(length), whole(length)],
            out_specs=(whole(length), whole(8), whole(8)),
        ),
        out_shape=(
            jax.ShapeDtypeStruct((length, LANES), bf16),
            jax.ShapeDtypeStruct((8, LANES), f32),
            jax.ShapeDtypeStruct((8, LANES), f32),
        ),
        compiler_params=pltpu.CompilerParams(vmem_limit_bytes=VMEM_LIMIT),
        cost_estimate=LIGHT,
    )(core.reshape(1).astype(jnp.int32), proj, rim, taps, mine, other)


def per_device(hidden_in, cotangent, in_proj, out_proj, conv_params, pre_gain, gated_gain, head_params):
    chips, line = lax.axis_size("chip"), lax.axis_size("seg")
    core, place = lax.axis_index("core"), lax.axis_index("seg")
    rows, model_width = in_proj.shape[0], hidden_in.shape[2]
    heads = HEADS // 2

    conv_width, gain_width = conv_params.shape[1], gated_gain.shape[0]
    used = HALF + 2 * STATE + heads
    spare = -used % LANES
    small = jnp.zeros((rows, spare), bf16)
    small = small.at[: CONV + 1, :conv_width].set(conv_params)
    small = small.at[CONV + 1, :rows].set(pre_gain)
    small = small.at[CONV + 2, :gain_width].set(gated_gain)

    def conv_side(which):
        return jnp.concatenate(
            [
                own_columns(in_proj[:, INNER : 2 * INNER], which),
                in_proj[:, 2 * INNER : INNER + XBC],
                own_columns(in_proj[:, INNER + XBC :], which),
                small,
            ],
            axis=1,
        )

    def gate_side(which):
        return own_columns(in_proj[:, :INNER], which)

    conv_swap = to_partner(conv_side(1 - core))
    conv_block = in_core_order(conv_side(core), conv_swap, core, 0)
    conv_z = gather_step(conv_block, 2)
    gate_swap = to_partner(gate_side(1 - core))
    gate_block = in_core_order(gate_side(core), gate_swap, core, 0)
    conv_z, hidden_in, gate_block = tie(conv_z, hidden_in, gate_block)
    conv_own = jnp.stack(conv_z)
    conv_near = gather_plane(conv_own, near_steps())
    hidden_got = send_sequence(hidden_in, place)
    conv_own, conv_near, hidden_got, gate_block = tie(conv_own, conv_near, hidden_got, gate_block)
    hidden_half = order_sequence(hidden_got, place)
    conv_far = gather_plane(conv_own, far_steps())
    gate_z = gather_step(gate_block, 2)
    hidden_other = to_partner(hidden_half)
    conv_far, gate_z, hidden_other, out_proj = tie(conv_far, gate_z, hidden_other, out_proj)
    out_own = out_proj[None]
    out_other = exchanged(out_own, 1)
    gate_own = jnp.stack(gate_z)
    gate_near = gather_plane(gate_own, near_steps())
    conv_all = whole_matrix([conv_own, *conv_near, *conv_far], True)

    small_all = conv_all.reshape(chips, 2, line, rows, -1)[..., used:].astype(f32)
    taps_full = small_all[..., : CONV + 1, :conv_width].transpose(3, 0, 1, 2, 4).reshape(CONV + 1, XBC)
    taps = jnp.concatenate([own_columns(taps_full[:, :INNER], core), taps_full[:, INNER:]], axis=1)
    gain_pre = small_all[..., CONV + 1, :rows].reshape(model_width)
    gain_gate = lax.dynamic_index_in_dim(
        small_all[..., CONV + 2, :gain_width], core, axis=1, keepdims=False
    ).reshape(HALF)
    params = own_columns(head_params, core)

    seg_len = hidden_half.shape[1]
    tokens = SEGS * seg_len
    normed, normed_turned = normed_tokens(core, hidden_half, hidden_other, gain_pre, rows)
    projected = dot(normed, conv_all, ((1,), (0,)))
    projected, gate_own, gate_near, out_own, out_other = tie(projected, gate_own, gate_near, out_own, out_other)
    gate_far = gather_plane(gate_own, far_steps())
    out_own = jnp.concatenate([out_own, out_other])
    out_others = []
    for bit in range(1, (line - 1).bit_length()):
        out_others.append(exchanged(out_own, 2**bit))
        if 2 ** (bit + 1) < line:
            out_own, out_others = jnp.concatenate([out_own, out_others[-1]]), []

    taps = jnp.pad(taps, ((0, 8 - CONV - 1), (0, projected.shape[1] - taps.shape[1])))
    head = jnp.pad(jnp.stack([-jnp.exp(params[0]), params[1]]), ((0, 6), (0, LANES - heads)))
    skip = jnp.repeat(params[2], HEADDIM).reshape(1, HALF)
    wide = HALF + 2 * STATE
    rim = borrowed(projected[tokens - 8 :], 1)
    nothing = jnp.zeros((STATE, HALF), f32)
    values, prior, final, last = scan_forward(projected, taps, head, skip, rim, nothing, seg_len)
    if line > SEGS:
        last = jnp.sum(last.reshape(SEGS, 8, LANES)[:, 0, :heads], axis=0)
        decay = jnp.repeat(jnp.exp2(last), HEADDIM)
        begin = entering(decay, final, 1)
        values, prior, _, _ = scan_forward(projected, taps, head, skip, rim, begin, seg_len)

    values, gate_far, out_others, cotangent = tie(values, gate_far, out_others, cotangent)
    cot_got = send_sequence(cotangent, place)
    out_own = jnp.concatenate([out_own, *out_others])
    out_all = gather_plane(out_own, plane_steps())
    gate_matrix = whole_matrix([gate_own, *gate_near, *gate_far], True)
    gate_input = dot(normed, gate_matrix, ((1,), (0,)))

    silu_gate = jax.nn.silu(gate_input)
    gated = values * silu_gate
    squares = jnp.sum(gated * gated, axis=1)
    squares_other = to_partner(squares)
    scale = lax.rsqrt((squares + squares_other) / INNER + epsilon)[:, None]
    mixed, mixed_turned = mixed_tokens(gated, scale, gain_gate, seg_len)
    mixed_turned, out_all, cot_got = tie(mixed_turned, out_all, cot_got)
    cot_half = order_sequence(cot_got, place)
    cot_other = to_partner(cot_half)
    cot = in_core_order(cot_half, cot_other, core, 1)
    upstream = cot.reshape(tokens, model_width)
    by_owner = lambda grad: grad.astype(bf16).reshape(chip_dims() + (-1, grad.shape[1]))
    out_grad = by_owner(dot(mixed_turned, upstream, ((1,), (0,))))
    out_got_near = reduce_plane([out_grad], near_steps())
    out_matrix = whole_matrix([out_own, *out_all], False, True)
    branch, branch_sent = half_products(core, [(mixed, out_matrix, None)], seg_len, model_width, False)
    branch_sent, upstream = tie(branch_sent, upstream)
    branch_other = to_partner(branch_sent)
    grad_mixed = dot(upstream, out_matrix, ((1,), (1,)))
    grad_mixed, out_got_near, out_grad = tie(grad_mixed, out_got_near, out_grad)
    out_got_far = reduce_plane([out_grad], far_steps())
    unit = gated * scale
    gain_grad = grad_mixed * gain_gate
    along = jnp.sum(gain_grad * unit, axis=1)
    along_other = to_partner(along)
    along_other, branch_other = tie(along_other, branch_other)
    hidden_out = send_back((hidden_half.astype(f32) + branch + branch_other.astype(f32)).astype(bf16), place)
    along = ((along + along_other) / INNER)[:, None]
    gate_gain_grad = jnp.sum(grad_mixed * unit, axis=0)
    grad_gated = scale * (gain_grad - unit * along)
    grad_values = grad_gated * silu_gate
    sigmoid = jax.nn.sigmoid(gate_input)
    grad_gate = (grad_gated * values * (sigmoid * (1.0 + gate_input * (1.0 - sigmoid)))).astype(bf16)
    gate_grad = by_owner(dot(normed_turned, grad_gate, ((1,), (0,))))
    gate_grad, grad_values, out_got_far = tie(gate_grad, grad_values, out_got_far)
    gate_got = reduce_plane([gate_grad], plane_steps())
    scan = lambda later: scan_backward(
        0, core, projected, taps, head, skip, rim, later, prior, values, grad_values, seg_len
    )
    if line > SEGS:
        nothing = entering(decay, scan(nothing)[-1], -1)
    back = scan(nothing)
    back, gate_got, hidden_out, grad_gate = tie(back, gate_got, hidden_out, grad_gate)
    ((early_kept, early_got),) = reduce_z(
        [
            ([plane_part([out_grad], 0, 0)], [*out_got_near, *out_got_far]),
            ([plane_part([gate_grad], 0, 0)], gate_got),
        ]
    )
    grad_x, mine, theirs, grad_raw, x_taps_grad, skip_grad, head_sums, x_edge, _ = back
    grad_x = spilled(grad_x, x_edge, taps[:, :HALF])
    other = to_partner(theirs)
    x_grad = by_owner(dot(normed_turned, grad_x, ((1,), (0,))))
    other, x_grad = tie(other, x_grad)
    grad_state, state_taps_grad, state_edge = shared_backward(core, projected, rim, taps, mine, other)
    grad_state = spilled(grad_state, state_edge, lax.dynamic_slice_in_dim(taps, HALF + core * STATE, STATE, axis=1))
    grad_raw = grad_raw.astype(bf16)
    rest_grad = by_owner(dot(normed_turned, jnp.concatenate([grad_state, grad_raw], axis=1), ((1,), (0,))))
    rest_grad, x_grad, grad_gate = tie(rest_grad, x_grad, grad_gate)
    conv_near = reduce_plane([x_grad, rest_grad], near_steps())
    base = dot(grad_gate, gate_matrix, ((1,), (1,)))
    terms = [
        (grad_x, conv_all, lambda core: 0),
        (grad_state, conv_all, lambda core: HALF // LANES + core),
        (grad_raw, conv_all, lambda core: (HALF + 2 * STATE) // LANES),
    ]
    grad_normed, sent_normed = half_products(core, terms, seg_len, model_width, True, (base,))
    row = lax.broadcasted_iota(jnp.int32, (8, 1), 0)
    small = x_taps_grad + jnp.where(row == CONV + 1, gate_gain_grad, 0.0) + jnp.where(row == CONV + 2, skip_grad, 0.0)
    small = jnp.concatenate([small, state_taps_grad + head_sums], axis=1)
    sent_normed, early_got, conv_near, small, x_grad, rest_grad = tie(
        sent_normed, early_got, conv_near, small, x_grad, rest_grad
    )
    conv_far = reduce_plane([x_grad, rest_grad], far_steps())
    other_normed = to_partner(sent_normed)
    wide_hidden = hidden_half.astype(f32)
    hidden_scale = lax.rsqrt(jnp.mean(wide_hidden * wide_hidden, axis=-1, keepdims=True) + epsilon)
    grad_normed = (grad_normed + other_normed.astype(f32)) * gain_pre
    hidden_unit = wide_hidden * hidden_scale
    along = jnp.mean(grad_normed * hidden_unit, axis=-1, keepdims=True)
    grad_hidden = hidden_scale * (grad_normed - hidden_unit * along)
    grad_in = (cot_half.astype(f32) + grad_hidden).astype(bf16)
    grad_in, conv_far = tie(send_back(grad_in, place), conv_far)
    late = reduce_z([([plane_part([x_grad, rest_grad], 0, 0)], [*conv_near, *conv_far])])
    for dim in range(3):
        small = small + sum(moved(small, dim, by) for by in range(1, chip_dims()[dim]))
    small_other = to_partner(small)
    late_got, small_other = tie(arrivals(late), small_other)
    early_share = total([*early_kept, *early_got])
    out_share = early_share[:, :model_width]
    paired = lambda share: share.astype(bf16).reshape(2, rows, -1)
    gate_share, conv_share = paired(early_share[:, model_width:]), paired(reduce_end(arrived(late, late_got)))

    def mine_and_partner(share):
        keep = lax.dynamic_index_in_dim(share, core, axis=0, keepdims=False)
        give = lax.dynamic_index_in_dim(share, 1 - core, axis=0, keepdims=False)
        return keep, to_partner(give)

    both = in_core_order(small, small_other, core, 0)
    natural = lambda array, width: array.reshape(2, -1, chips, width).transpose(1, 2, 0, 3).reshape(-1, 2 * chips * width)
    device = (lax.axis_index("chip") * 2 + core) * line + place
    columns = natural(both[:, :, :HALF], HALF // chips)
    taps_all = jnp.concatenate([columns, both[0, :, HALF:], both[1, :, HALF:]], axis=1)[: CONV + 1]
    taps_share = lax.dynamic_slice_in_dim(taps_all, device * conv_width, conv_width, axis=1)
    gain_share = lax.dynamic_slice_in_dim(columns[CONV + 1], device * gain_width, gain_width, axis=0)
    head_total = jnp.concatenate(
        [
            natural(both[:, CONV + 1 : CONV + 3, HALF : HALF + heads], heads // chips),
            jnp.sum(columns[CONV + 2].reshape(1, HEADS, HEADDIM), axis=2),
        ]
    )

    def interleave(mine, theirs):
        width = mine.shape[1] // chips
        both = in_core_order(mine.reshape(rows, chips, width), theirs.reshape(rows, chips, width), core, 2)
        return both.reshape(rows, -1)

    keep_gate, got_gate = mine_and_partner(gate_share)
    keep, got = mine_and_partner(conv_share)
    state_end = HALF + STATE
    in_share = jnp.concatenate(
        [
            interleave(keep_gate, got_gate),
            interleave(keep[:, :HALF], got[:, :HALF]),
            in_core_order(keep[:, HALF:state_end], got[:, HALF:state_end], core, 1).reshape(rows, -1),
            interleave(keep[:, state_end : state_end + heads], got[:, state_end : state_end + heads]),
        ],
        axis=1,
    ).astype(f32)
    pre_share = jnp.sum(in_proj.astype(f32) * in_share, axis=1) / pre_gain.astype(f32)
    hidden_out, grad_in = order_back(hidden_out, place), order_back(grad_in, place)
    return (hidden_out, grad_in, in_share, out_share, taps_share, pre_share, gain_share, head_total)


def solution(mesh):
    devices = mesh.devices
    cores = Mesh(devices.reshape(devices.shape[0] // 2, 2, devices.shape[1]), ("chip", "core", "seg"))
    dp, both = ("chip", "core"), ("chip", "core", "seg")
    tokens = P(dp, "seg", None)
    return jax.shard_map(
        per_device,
        mesh=cores,
        in_specs=(tokens, tokens, P(both, None), P(both, None), P(None, both), P(both), P(both), P()),
        out_specs=(tokens, tokens, P(both, None), P(both, None), P(None, both), P(both), P(both), P()),
        check_vma=False,
    )
```

profile of v0, /device:TPU:1, one launch (start us, length us, event | category | flops | bytes accessed | tf_op | source)
XLA Modules:
  0.0 558.9 jit_solution(17950188805620565569)
XLA Ops:
  14.7 7.2 %collective-permute-done.3 = bf16[2,48,1920]{2,1,0:T(8,128)(2,1)S(1)} collective-permute-done((bf16[2,48,1920]{2,1,0:T(8,128)(2,1)S(1)}, bf16[2,48,1920]{2,1,0:T(8,128)(2,1)S(1)}, u32[]{:S(2)}, u32[]{:S(2)}) %collective-permute-start.3) | collective-permute-done | bytes 368672 | tf_op jit(solution)/shard_map/ppermute | solution.py:64
  21.9 23.5 %collective-permute-done.2 = bf16[2,48,1920]{2,1,0:T(8,128)(2,1)S(1)} collective-permute-done((bf16[2,48,1920]{2,1,0:T(8,128)(2,1)S(1)}, bf16[2,48,1920]{2,1,0:T(8,128)(2,1)S(1)}, u32[]{:S(2)}, u32[]{:S(2)}) %collective-permute-start.2) | collective-permute-done | bytes 368672 | tf_op jit(solution)/shard_map/ppermute | solution.py:64
  50.7 6.2 %collective-permute-start.7 = (bf16[256,1536]{1,0:T(8,128)(2,1)}, bf16[256,1536]{1,0:T(8,128)(2,1)}, u32[]{:S(2)}, u32[]{:S(2)}) collective-permute-start(bf16[256,1536]{1,0:T(8,128)(2,1)} %get-tuple-element.288), channel_id=1, source_target_pairs={{0,0},{1,4},{2,1},{3,5},{4,2},{5,6},{6,3},{7,7},{8,8},{9,12},{10,9... | collective-permute-start | bytes 2359304 | tf_op jit(solution)/shard_map/ppermute | solution.py:210
  56.9 15.6 %collective-permute-done.8 = bf16[256,1536]{1,0:T(8,128)(2,1)} collective-permute-done((bf16[256,1536]{1,0:T(8,128)(2,1)}, bf16[256,1536]{1,0:T(8,128)(2,1)}, u32[]{:S(2)}, u32[]{:S(2)}) %collective-permute-start.8) | collective-permute-done | bytes 786464 | tf_op jit(solution)/shard_map/ppermute | solution.py:210
  72.6 8.5 %collective-permute-done.7 = bf16[256,1536]{1,0:T(8,128)(2,1)} collective-permute-done((bf16[256,1536]{1,0:T(8,128)(2,1)}, bf16[256,1536]{1,0:T(8,128)(2,1)}, u32[]{:S(2)}, u32[]{:S(2)}) %collective-permute-start.7) | collective-permute-done | bytes 786464 | tf_op jit(solution)/shard_map/ppermute | solution.py:210
  85.6 9.8 %collective-permute-start.11 = (bf16[2,48,1536]{2,1,0:T(8,128)(2,1)S(1)}, bf16[2,48,1536]{2,1,0:T(8,128)(2,1)}, u32[]{:S(2)}, u32[]{:S(2)}) collective-permute-start(bf16[2,48,1536]{2,1,0:T(8,128)(2,1)S(1)} %pad_maximum_fusion.12), channel_id=1, source_target_pairs={{0,2},{1,3},{2,0},{3,1},{8,10},{9,11},{10,8},{11,9},{16,18},{17,19... | collective-permute-start | bytes 884744 | tf_op jit(solution)/shard_map/ppermute | solution.py:64
  95.9 5.3 collective-permute-done.12
  101.2 19.8 %collective-permute-done.11 = bf16[2,48,1536]{2,1,0:T(8,128)(2,1)} collective-permute-done((bf16[2,48,1536]{2,1,0:T(8,128)(2,1)S(1)}, bf16[2,48,1536]{2,1,0:T(8,128)(2,1)}, u32[]{:S(2)}, u32[]{:S(2)}) %collective-permute-start.11) | collective-permute-done | bytes 294944 | tf_op jit(solution)/shard_map/ppermute | solution.py:64
  125.8 5.5 collective-permute-start.16
  131.3 5.4 shard_map.143
  138.2 5.7 %shard_map.144 = (bf16[1024,1536]{1,0:T(8,128)(2,1)}, bf16[1536,1024]{1,0:T(8,128)(2,1)}) custom-call(s32[1]{0:T(128)} %bitcast.refs_0_.refs_14_.core_ref, bf16[2,256,1536]{2,1,0:T(8,128)(2,1)S(1)} %pad_maximum_fusion.1.refs_1_, bf16[2,256,1536]{2,1,0:T(8,128)(2,1)} %collective-permute-done.13.refs_2_, f32[1,1536]{1,0:T(1,128)S(1)} %reshape_reshape_squeeze.3.refs_3_), custom_call_target="tpu_custom_call" | custom-call | flops 1024 | bytes 1024 | tf_op jit(solution)/shard_map/pallas_call | solution.py:291
  143.9 12.0 %fusion.47.proj_ref.refs_0_.refs_1_.refs_4_.refs_5_ = f32[1024,1920]{1,0:T(8,128)} fusion(bf16[1024,1536]{1,0:T(8,128)(2,1)} %get-tuple-element.157, bf16[1536,1920]{1,0:T(8,128)(2,1)} %bitcast.238), kind=kOutput, calls=%fused_computation.189 | convolution fusion | flops 6039797760 | bytes 16908288 | tf_op jit(solution)/shard_map/dot_general | solution.py:264
  160.0 22.1 %shard_map.145 = (f32[1024,1536]{1,0:T(8,128)}, bf16[4,128,1536]{2,1,0:T(8,128)(2,1)S(1)}, f32[128,1536]{1,0:T(8,128)}, f32[32,128]{1,0:T(8,128)}) custom-call(f32[1024,1920]{1,0:T(8,128)} %fusion.47.proj_ref.refs_0_.refs_1_.refs_4_.refs_5_, f32[8,1920]{1,0:T(8,128)S(1)} %select_maximum_fusion.taps_ref.refs_2_.refs_6_, ...), custom_call_target="tpu_custom_call" | custom-call | flops 1024 | bytes 1024 | tf_op jit(solution)/shard_map/pallas_call | solution.py:457
  196.2 11.9 %multiply_reduce_fusion.2 = (f32[1024]{0:T(1024)S(1)}, f32[1024,1536]{1,0:T(8,128)}, f32[1024,1536]{1,0:T(8,128)}) fusion(f32[1024,1536]{1,0:T(8,128)S(1)} %bitcast.245, bf16[1024,1536]{1,0:T(8,128)(2,1)} %get-tuple-element.157, bf16[1536,1536]{1,0:T(8,128)(2,1)} %bitcast.255), kind=kOutput, calls=%fused_computation.15 | convolution fusion | flops 4842847232 | bytes 26742784 | tf_op jit(solution)/shard_map/dot_general | solution.py:264
  217.1 5.6 %shard_map.147 = (bf16[1024,1536]{1,0:T(8,128)(2,1)S(1)}, bf16[1536,1024]{1,0:T(8,128)(2,1)}) custom-call(f32[1024,1536]{1,0:T(8,128)} %get-tuple-element.251.gated_ref, f32[1024,1]{1,0:T(8,128)S(1)} %copy.56.scale_ref, f32[1,1536]{1,0:T(1,128)S(1)} %reshape_reshape.15.gain_ref), custom_call_target="tpu_custom_call" | custom-call | flops 1024 | bytes 1024 | tf_op jit(solution)/shard_map/pallas_call | solution.py:326
  222.7 7.0 %collective-permute-done.24 = bf16[256,1536]{1,0:T(8,128)(2,1)} collective-permute-done((bf16[256,1536]{1,0:T(8,128)(2,1)}, bf16[256,1536]{1,0:T(8,128)(2,1)}, u32[]{:S(2)}, u32[]{:S(2)}) %collective-permute-start.24) | collective-permute-done | bytes 786464 | tf_op jit(solution)/shard_map/ppermute | solution.py:210
  229.7 8.6 %collective-permute-done.23 = bf16[256,1536]{1,0:T(8,128)(2,1)} collective-permute-done((bf16[256,1536]{1,0:T(8,128)(2,1)}, bf16[256,1536]{1,0:T(8,128)(2,1)}, u32[]{:S(2)}, u32[]{:S(2)}) %collective-permute-start.23) | collective-permute-done | bytes 786464 | tf_op jit(solution)/shard_map/ppermute | solution.py:210
  254.7 5.3 convolution_convert_fusion.2
  269.2 8.6 %shard_map.149 = (f32[2,256,1536]{2,1,0:T(8,128)S(1)}, bf16[2,256,1536]{2,1,0:T(8,128)(2,1)S(1)}) custom-call(s32[1]{0:T(128)} %bitcast.refs_0_.refs_14_.core_ref, bf16[1024,1536]{1,0:T(8,128)(2,1)} %copy-done, bf16[1536,1536]{1,0:T(8,128)(2,1)} %bitcast.246), custom_call_target="tpu_custom_call" | custom-call | flops 1024 | bytes 1024 | tf_op jit(solution)/shard_map/pallas_call | solution.py:741
  278.8 7.4 %fusion.48 = f32[1024,1536]{1,0:T(8,128)S(1)} fusion(bf16[1024,1536]{1,0:T(8,128)(2,1)S(1)} %bitcast.262, bf16[1536,1536]{1,0:T(8,128)(2,1)} %bitcast.247), kind=kOutput, calls=%fused_computation.190 | convolution fusion | flops 4831838208 | bytes 14155776 | tf_op jit(solution)/shard_map/dot_general | solution.py:264
  296.5 10.6 %fusion.11 = (f32[1024,1536]{1,0:T(8,128)}, bf16[1024,1536]{1,0:T(8,128)(2,1)S(1)}) fusion(f32[1024]{0:T(1024)S(1)} %add_multiply_fusion.1, f32[1024,1536]{1,0:T(8,128)S(1)} %bitcast.243, f32[1024,1536]{1,0:T(8,128)} %copy-done.5, f32[1536]{0:T(1024)S(1)} %mul.138, f32[1024]{0:T(1024)S(1)} %add_rsqrt_fusion, f32[1024,1536]{1,0:T(8,128)} %get-tuple-element.320, ...), kind=kLoop, calls=%fused_computation.33 | loop fusion | flops 26738688 | bytes 34617344 | tf_op jit(solution)/shard_map/mul | solution.py:919
  310.1 5.5 convolution_convert_fusion.1
  315.5 9.2 %collective-permute-done.30 = bf16[4,96,1536]{2,1,0:T(8,128)(2,1)S(1)} collective-permute-done((bf16[4,96,1536]{2,1,0:T(8,128)(2,1)S(1)}, bf16[4,96,1536]{2,1,0:T(8,128)(2,1)S(1)}, u32[]{:S(2)}, u32[]{:S(2)}) %collective-permute-start.30) | collective-permute-done | bytes 1179680 | tf_op jit(solution)/shard_map/ppermute | solution.py:104
  331.5 8.4 %collective-permute-start.34 = (bf16[256,1536]{1,0:T(8,128)(2,1)S(1)}, bf16[256,1536]{1,0:T(8,128)(2,1)S(1)}, u32[]{:S(2)}, u32[]{:S(2)}) collective-permute-start(bf16[256,1536]{1,0:T(8,128)(2,1)S(1)} %get-tuple-element.280), channel_id=1, source_target_pairs={{0,0},{4,1},{1,2},{5,3},{2,4},{6,5},{3,6},{7,7},{8,8},{12,9},{9,10... | collective-permute-start | bytes 2359304 | tf_op jit(solution)/shard_map/ppermute | solution.py:221
  340.0 48.9 %shard_map.150 = (bf16[1024,1536]{1,0:T(8,128)(2,1)}, f32[1024,128]{1,0:T(8,128)S(1)}, f32[1024,128]{1,0:T(8,128)S(1)}, f32[1024,128]{1,0:T(8,128)S(1)}, f32[8,1...) custom-call(f32[1024,1920]{1,0:T(8,128)} %fusion.47.proj_ref.refs_0_, ...), custom_call_target="tpu_custom_call" | custom-call | flops 1024 | bytes 1024 | tf_op jit(solution)/shard_map/pallas_call | solution.py:653
  399.3 6.8 %convolution_convert_fusion = bf16[1536,1536]{1,0:T(8,128)(2,1)} fusion(bf16[1536,1024]{1,0:T(8,128)(2,1)S(1)} %copy-done.50, bf16[1024,1536]{1,0:T(8,128)(2,1)S(1)} %copy-done.22), kind=kOutput, calls=%fused_computation | convolution fusion | flops 4834197504 | bytes 11010048 | tf_op jit(solution)/shard_map/dot_general | solution.py:264
  417.9 7.1 %fusion.49.refs_7_ = f32[1024,1536]{1,0:T(8,128)} fusion(bf16[1024,1536]{1,0:T(8,128)(2,1)S(1)} %copy-done.26, bf16[1536,1536]{1,0:T(8,128)(2,1)S(1)} %bitcast.258), kind=kOutput, calls=%fused_computation.191 | convolution fusion | flops 4831838208 | bytes 14155776 | tf_op jit(solution)/shard_map/dot_general | solution.py:264
  426.3 12.0 %shard_map.152 = (f32[2,256,1536]{2,1,0:T(8,128)S(1)}, bf16[2,256,1536]{2,1,0:T(8,128)(2,1)}) custom-call(s32[1]{0:T(128)} %bitcast.refs_0_.refs_14_.core_ref, bf16[1024,1536]{1,0:T(8,128)(2,1)} %get-tuple-element.203.refs_1_, bf16[1024,128]{1,0:T(8,128)(2,1)S(1)} %get-tuple-element.207.refs_2_, bf16[1024,128]{1,0:T(8,128)(2,1)S(1)} %convert_element_type.162.refs_3_, ...), custom_call_target="tpu_custom_call" | custom-call | flops 1024 | bytes 1024 | tf_op jit(solution)/shard_map/pallas_call | solution.py:741
  438.3 10.9 %collective-permute-done.38 = bf16[96,3072]{1,0:T(8,128)(2,1)} collective-permute-done((bf16[96,3072]{1,0:T(8,128)(2,1)}, bf16[96,3072]{1,0:T(8,128)(2,1)}, u32[]{:S(2)}, u32[]{:S(2)}) %collective-permute-start.38) | collective-permute-done | bytes 589856 | tf_op jit(solution)/shard_map/ppermute | solution.py:64
  478.3 24.1 %collective-permute-done.52 = f32[8,1664]{1,0:T(8,128)S(1)} collective-permute-done((f32[8,1664]{1,0:T(8,128)}, f32[8,1664]{1,0:T(8,128)S(1)}, u32[]{:S(2)}, u32[]{:S(2)}) %collective-permute-start.52) | collective-permute-done | bytes 53280 | tf_op jit(solution)/shard_map/ppermute | solution.py:64
  503.5 6.7 %collective-permute-done.43 = bf16[256,1536]{1,0:T(8,128)(2,1)S(1)} collective-permute-done((bf16[256,1536]{1,0:T(8,128)(2,1)S(1)}, bf16[256,1536]{1,0:T(8,128)(2,1)S(1)}, u32[]{:S(2)}, u32[]{:S(2)}) %collective-permute-start.43) | collective-permute-done | bytes 786464 | tf_op jit(solution)/shard_map/ppermute | solution.py:221
  526.2 23.9 %collective-permute-done.48 = bf16[96,1792]{1,0:T(8,128)(2,1)S(1)} collective-permute-done((bf16[96,1792]{1,0:T(8,128)(2,1)S(1)}, bf16[96,1792]{1,0:T(8,128)(2,1)S(1)}, u32[]{:S(2)}, u32[]{:S(2)}) %collective-permute-start.48) | collective-permute-done | bytes 344096 | tf_op jit(solution)/shard_map/ppermute | solution.py:64
  (383 shorter events, 181.2 us)
Async XLA Ops:
  14.2 31.2 %collective-permute-start.2 = (bf16[2,48,1920]{2,1,0:T(8,128)(2,1)S(1)}, bf16[2,48,1920]{2,1,0:T(8,128)(2,1)S(1)}, u32[]{:S(2)}, u32[]{:S(2)}) collective-permute-start(bf16[2,48,1920]{2,1,0:T(8,128)(2,1)S(1)} %pad_maximum_fusion.11), channel_id=1, source_target_pairs={{0,2},{1,3},{2,0},{3,1},{8,10},{9,11},{10,8},{11,9},{16,18},{17,19... | collective-permute-start | bytes 1105928 | tf_op jit(solution)/shard_map/ppermute | solution.py:64
  14.2 31.2 %collective-permute-start.1 = (bf16[2,48,1920]{2,1,0:T(8,128)(2,1)S(1)}, bf16[2,48,1920]{2,1,0:T(8,128)(2,1)S(1)}, u32[]{:S(2)}, u32[]{:S(2)}) collective-permute-start(bf16[2,48,1920]{2,1,0:T(8,128)(2,1)S(1)} %pad_maximum_fusion.11), channel_id=1, source_target_pairs={{0,1},{1,2},{2,3},{3,0},{8,9},{9,10},{10,11},{11,8},{16,17},{17,18... | collective-permute-start | bytes 1105928 | tf_op jit(solution)/shard_map/ppermute | solution.py:64
  45.6 35.5 %collective-permute-start.6 = (bf16[4,2,48,1920]{3,2,1,0:T(8,128)(2,1)S(1)}, bf16[4,2,48,1920]{3,2,1,0:T(8,128)(2,1)S(1)}, u32[]{:S(2)}, u32[]{:S(2)}) collective-permute-start(bf16[4,2,48,1920]{3,2,1,0:T(8,128)(2,1)S(1)} %pad_maximum_fusion.5.refs_1_), channel_id=1, source_target_pairs={{0,16},{1,17},{2,18},{3,19},{8,24},{9,25},{10,26},{11,27},{16,0},{... | collective-permute-start | bytes 4423688 | tf_op jit(solution)/shard_map/ppermute | solution.py:104
  46.9 34.2 %collective-permute-start.5 = (bf16[4,2,48,1920]{3,2,1,0:T(8,128)(2,1)S(1)}, bf16[4,2,48,1920]{3,2,1,0:T(8,128)(2,1)}, u32[]{:S(2)}, u32[]{:S(2)}) collective-permute-start(bf16[4,2,48,1920]{3,2,1,0:T(8,128)(2,1)S(1)} %pad_maximum_fusion.5.refs_1_), channel_id=1, source_target_pairs={{0,8},{1,9},{2,10},{3,11},{8,0},{9,1},{10,2},{11,3},{16,24},{17,25... | collective-permute-start | bytes 4423688 | tf_op jit(solution)/shard_map/ppermute | solution.py:104
  50.7 30.4 %collective-permute-start.7 = (bf16[256,1536]{1,0:T(8,128)(2,1)}, bf16[256,1536]{1,0:T(8,128)(2,1)}, u32[]{:S(2)}, u32[]{:S(2)}) collective-permute-start(bf16[256,1536]{1,0:T(8,128)(2,1)} %get-tuple-element.288), channel_id=1, source_target_pairs={{0,0},{1,4},{2,1},{3,5},{4,2},{5,6},{6,3},{7,7},{8,8},{9,12},{10,9... | collective-permute-start | bytes 2359304 | tf_op jit(solution)/shard_map/ppermute | solution.py:210
  84.0 37.0 %collective-permute-start.13 = (bf16[2,256,1536]{2,1,0:T(8,128)(2,1)S(1)}, bf16[2,256,1536]{2,1,0:T(8,128)(2,1)}, u32[]{:S(2)}, u32[]{:S(2)}) collective-permute-start(bf16[2,256,1536]{2,1,0:T(8,128)(2,1)S(1)} %pad_maximum_fusion.1.refs_1_), channel_id=1, source_target_pairs={{0,4},{4,0},{1,5},{5,1},{2,6},{6,2},{3,7},{7,3},{8,12},{12,8},{9,1... | collective-permute-start | bytes 4718600 | tf_op jit(solution)/shard_map/ppermute | solution.py:36
  85.2 35.9 %collective-permute-start.9 = (bf16[4,2,48,1920]{3,2,1,0:T(8,128)(2,1)S(1)}, bf16[4,2,48,1920]{3,2,1,0:T(8,128)(2,1)}, u32[]{:S(2)}, u32[]{:S(2)}) collective-permute-start(bf16[4,2,48,1920]{3,2,1,0:T(8,128)(2,1)S(1)} %pad_maximum_fusion.5.refs_1_), channel_id=1, source_target_pairs={{0,24},{1,25},{2,26},{3,27},{8,16},{9,17},{10,18},{11,19},{16,8},{... | collective-permute-start | bytes 4423688 | tf_op jit(solution)/shard_map/ppermute | solution.py:104
  85.6 35.4 %collective-permute-start.11 = (bf16[2,48,1536]{2,1,0:T(8,128)(2,1)S(1)}, bf16[2,48,1536]{2,1,0:T(8,128)(2,1)}, u32[]{:S(2)}, u32[]{:S(2)}) collective-permute-start(bf16[2,48,1536]{2,1,0:T(8,128)(2,1)S(1)} %pad_maximum_fusion.12), channel_id=1, source_target_pairs={{0,2},{1,3},{2,0},{3,1},{8,10},{9,11},{10,8},{11,9},{16,18},{17,19... | collective-permute-start | bytes 884744 | tf_op jit(solution)/shard_map/ppermute | solution.py:64
  123.4 32.5 %collective-permute-start.15 = (bf16[4,2,48,1536]{3,2,1,0:T(8,128)(2,1)}, bf16[4,2,48,1536]{3,2,1,0:T(8,128)(2,1)}, u32[]{:S(2)}, u32[]{:S(2)}) collective-permute-start(bf16[4,2,48,1536]{3,2,1,0:T(8,128)(2,1)} %pad_maximum_fusion.9.refs_1_), channel_id=1, source_target_pairs={{0,16},{1,17},{2,18},{3,19},{8,24},{9,25},{10,26},{11,27},{16,0},{... | collective-permute-start | bytes 3538952 | tf_op jit(solution)/shard_map/ppermute | solution.py:104
  124.6 31.3 %collective-permute-start.14 = (bf16[4,2,48,1536]{3,2,1,0:T(8,128)(2,1)}, bf16[4,2,48,1536]{3,2,1,0:T(8,128)(2,1)}, u32[]{:S(2)}, u32[]{:S(2)}) collective-permute-start(bf16[4,2,48,1536]{3,2,1,0:T(8,128)(2,1)} %pad_maximum_fusion.9.refs_1_), channel_id=1, source_target_pairs={{0,8},{1,9},{2,10},{3,11},{8,0},{9,1},{10,2},{11,3},{16,24},{17,25... | collective-permute-start | bytes 3538952 | tf_op jit(solution)/shard_map/ppermute | solution.py:104
  125.8 30.1 %collective-permute-start.16 = (bf16[1,96,1536]{2,1,0:T(8,128)(2,1)}, bf16[1,96,1536]{2,1,0:T(8,128)(2,1)S(1)}, u32[]{:S(2)}, u32[]{:S(2)}) collective-permute-start(bf16[1,96,1536]{2,1,0:T(8,128)(2,1)} %bitcast.27), channel_id=1, source_target_pairs={{0,1},{1,0},{2,3},{3,2},{4,5},{5,4},{6,7},{7,6},{8,9},{9,8},{10,11... | collective-permute-start | bytes 884744 | tf_op jit(solution)/shard_map/ppermute | solution.py:77
  155.9 32.4 %collective-permute-start.17 = (bf16[4,2,48,1536]{3,2,1,0:T(8,128)(2,1)}, bf16[4,2,48,1536]{3,2,1,0:T(8,128)(2,1)}, u32[]{:S(2)}, u32[]{:S(2)}) collective-permute-start(bf16[4,2,48,1536]{3,2,1,0:T(8,128)(2,1)} %pad_maximum_fusion.9.refs_1_), channel_id=1, source_target_pairs={{0,24},{1,25},{2,26},{3,27},{8,16},{9,17},{10,18},{11,19},{16,8},{... | collective-permute-start | bytes 3538952 | tf_op jit(solution)/shard_map/ppermute | solution.py:104
  159.8 28.5 %collective-permute-start.18 = (bf16[2,96,1536]{2,1,0:T(8,128)(2,1)S(1)}, bf16[2,96,1536]{2,1,0:T(8,128)(2,1)S(1)}, u32[]{:S(2)}, u32[]{:S(2)}) collective-permute-start(bf16[2,96,1536]{2,1,0:T(8,128)(2,1)S(1)} %pad_maximum_fusion.10), channel_id=1, source_target_pairs={{0,2},{1,3},{2,0},{3,1},{4,6},{5,7},{6,4},{7,5},{8,10},{9,11},{10,... | collective-permute-start | bytes 1769480 | tf_op jit(solution)/shard_map/ppermute | solution.py:77
  188.3 50.0 %collective-permute-start.22 = (bf16[4,96,1536]{2,1,0:T(8,128)(2,1)S(1)}, bf16[4,96,1536]{2,1,0:T(8,128)(2,1)}, u32[]{:S(2)}, u32[]{:S(2)}) collective-permute-start(bf16[4,96,1536]{2,1,0:T(8,128)(2,1)S(1)} %constant_dynamic-update-slice_fusion.refs_1_), channel_id=1, source_target_pairs={{0,24},{1,25},{2,26},{3,27},{8,16},{9,17},{10,18},{11,19},{16,8},{... | collective-permute-start | bytes 3538952 | tf_op jit(solution)/shard_map/ppermute | solution.py:104
  188.4 52.5 %collective-permute-start.21 = (bf16[4,96,1536]{2,1,0:T(8,128)(2,1)S(1)}, bf16[4,96,1536]{2,1,0:T(8,128)(2,1)}, u32[]{:S(2)}, u32[]{:S(2)}) collective-permute-start(bf16[4,96,1536]{2,1,0:T(8,128)(2,1)S(1)} %constant_dynamic-update-slice_fusion.refs_1_), channel_id=1, source_target_pairs={{0,16},{1,17},{2,18},{3,19},{8,24},{9,25},{10,26},{11,27},{16,0},{... | collective-permute-start | bytes 3538952 | tf_op jit(solution)/shard_map/ppermute | solution.py:104
  188.9 52.0 %collective-permute-start.20 = (bf16[4,96,1536]{2,1,0:T(8,128)(2,1)S(1)}, bf16[4,96,1536]{2,1,0:T(8,128)(2,1)}, u32[]{:S(2)}, u32[]{:S(2)}) collective-permute-start(bf16[4,96,1536]{2,1,0:T(8,128)(2,1)S(1)} %constant_dynamic-update-slice_fusion.refs_1_), channel_id=1, source_target_pairs={{0,8},{1,9},{2,10},{3,11},{8,0},{9,1},{10,2},{11,3},{16,24},{17,25... | collective-permute-start | bytes 3538952 | tf_op jit(solution)/shard_map/ppermute | solution.py:104
  296.2 28.5 %collective-permute-start.30 = (bf16[4,96,1536]{2,1,0:T(8,128)(2,1)S(1)}, bf16[4,96,1536]{2,1,0:T(8,128)(2,1)S(1)}, u32[]{:S(2)}, u32[]{:S(2)}) collective-permute-start(bf16[4,96,1536]{2,1,0:T(8,128)(2,1)S(1)} %dynamic-slice_bitcast_fusion.7), channel_id=1, source_target_pairs={{0,24},{1,25},{2,26},{3,27},{8,16},{9,17},{10,18},{11,19},{16,8},{... | collective-permute-start | bytes 3538952 | tf_op jit(solution)/shard_map/ppermute | solution.py:104
  326.9 64.6 %collective-permute-start.33 = (bf16[4,96,1536]{2,1,0:T(8,128)(2,1)}, bf16[4,96,1536]{2,1,0:T(8,128)(2,1)S(1)}, u32[]{:S(2)}, u32[]{:S(2)}) collective-permute-start(bf16[4,96,1536]{2,1,0:T(8,128)(2,1)} %get-tuple-element.261), channel_id=1, source_target_pairs={{0,24},{1,25},{2,26},{3,27},{8,16},{9,17},{10,18},{11,19},{16,8},{... | collective-permute-start | bytes 3538952 | tf_op jit(solution)/shard_map/ppermute | solution.py:104
  327.1 64.4 %collective-permute-start.32 = (bf16[4,96,1536]{2,1,0:T(8,128)(2,1)}, bf16[4,96,1536]{2,1,0:T(8,128)(2,1)S(1)}, u32[]{:S(2)}, u32[]{:S(2)}) collective-permute-start(bf16[4,96,1536]{2,1,0:T(8,128)(2,1)} %get-tuple-element.262), channel_id=1, source_target_pairs={{0,16},{1,17},{2,18},{3,19},{8,24},{9,25},{10,26},{11,27},{16,0},{... | collective-permute-start | bytes 3538952 | tf_op jit(solution)/shard_map/ppermute | solution.py:104
  328.1 63.4 %collective-permute-start.31 = (bf16[4,96,1536]{2,1,0:T(8,128)(2,1)}, bf16[4,96,1536]{2,1,0:T(8,128)(2,1)S(1)}, u32[]{:S(2)}, u32[]{:S(2)}) collective-permute-start(bf16[4,96,1536]{2,1,0:T(8,128)(2,1)} %get-tuple-element.263), channel_id=1, source_target_pairs={{0,8},{1,9},{2,10},{3,11},{8,0},{9,1},{10,2},{11,3},{16,24},{17,25... | collective-permute-start | bytes 3538952 | tf_op jit(solution)/shard_map/ppermute | solution.py:104
  329.7 61.8 %collective-permute-start.35 = (bf16[256,1536]{1,0:T(8,128)(2,1)S(1)}, bf16[256,1536]{1,0:T(8,128)(2,1)S(1)}, u32[]{:S(2)}, u32[]{:S(2)}) collective-permute-start(bf16[256,1536]{1,0:T(8,128)(2,1)S(1)} %get-tuple-element.279), channel_id=1, source_target_pairs={{1,0},{5,1},{0,2},{4,3},{3,4},{7,5},{2,6},{6,7},{9,8},{13,9},{8,10... | collective-permute-start | bytes 2359304 | tf_op jit(solution)/shard_map/ppermute | solution.py:221
  331.5 60.0 %collective-permute-start.34 = (bf16[256,1536]{1,0:T(8,128)(2,1)S(1)}, bf16[256,1536]{1,0:T(8,128)(2,1)S(1)}, u32[]{:S(2)}, u32[]{:S(2)}) collective-permute-start(bf16[256,1536]{1,0:T(8,128)(2,1)S(1)} %get-tuple-element.280), channel_id=1, source_target_pairs={{0,0},{4,1},{1,2},{5,3},{2,4},{6,5},{3,6},{7,7},{8,8},{12,9},{9,10... | collective-permute-start | bytes 2359304 | tf_op jit(solution)/shard_map/ppermute | solution.py:221
  396.5 41.8 %collective-permute-start.39 = (bf16[96,3072]{1,0:T(8,128)(2,1)}, bf16[96,3072]{1,0:T(8,128)(2,1)}, u32[]{:S(2)}, u32[]{:S(2)}) collective-permute-start(bf16[96,3072]{1,0:T(8,128)(2,1)} %get-tuple-element.258), channel_id=1, source_target_pairs={{0,3},{1,0},{2,1},{3,2},{8,11},{9,8},{10,9},{11,10},{16,19},{17,16... | collective-permute-start | bytes 1769480 | tf_op jit(solution)/shard_map/ppermute | solution.py:64
  396.5 41.8 %collective-permute-start.37 = (bf16[96,3072]{1,0:T(8,128)(2,1)}, bf16[96,3072]{1,0:T(8,128)(2,1)}, u32[]{:S(2)}, u32[]{:S(2)}) collective-permute-start(bf16[96,3072]{1,0:T(8,128)(2,1)} %get-tuple-element.259), channel_id=1, source_target_pairs={{0,1},{1,2},{2,3},{3,0},{8,9},{9,10},{10,11},{11,8},{16,17},{17,18... | collective-permute-start | bytes 1769480 | tf_op jit(solution)/shard_map/ppermute | solution.py:64
  398.0 51.2 %collective-permute-start.38 = (bf16[96,3072]{1,0:T(8,128)(2,1)}, bf16[96,3072]{1,0:T(8,128)(2,1)}, u32[]{:S(2)}, u32[]{:S(2)}) collective-permute-start(bf16[96,3072]{1,0:T(8,128)(2,1)} %get-tuple-element.260), channel_id=1, source_target_pairs={{0,2},{1,3},{2,0},{3,1},{8,10},{9,11},{10,8},{11,9},{16,18},{17,19... | collective-permute-start | bytes 1769480 | tf_op jit(solution)/shard_map/ppermute | solution.py:64
  415.1 34.1 %collective-permute-start.40 = (bf16[4,96,1792]{2,1,0:T(8,128)(2,1)}, bf16[4,96,1792]{2,1,0:T(8,128)(2,1)}, u32[]{:S(2)}, u32[]{:S(2)}) collective-permute-start(bf16[4,96,1792]{2,1,0:T(8,128)(2,1)} %pad_maximum_fusion.6), channel_id=1, source_target_pairs={{0,8},{1,9},{2,10},{3,11},{8,0},{9,1},{10,2},{11,3},{16,24},{17,25... | collective-permute-start | bytes 4128776 | tf_op jit(solution)/shard_map/ppermute | solution.py:104
  416.7 32.6 %collective-permute-start.41 = (bf16[4,96,1792]{2,1,0:T(8,128)(2,1)}, bf16[4,96,1792]{2,1,0:T(8,128)(2,1)}, u32[]{:S(2)}, u32[]{:S(2)}) collective-permute-start(bf16[4,96,1792]{2,1,0:T(8,128)(2,1)} %pad_maximum_fusion.7), channel_id=1, source_target_pairs={{0,16},{1,17},{2,18},{3,19},{8,24},{9,25},{10,26},{11,27},{16,0},{... | collective-permute-start | bytes 4128776 | tf_op jit(solution)/shard_map/ppermute | solution.py:104
  459.3 44.2 %collective-permute-start.45 = (bf16[4,96,1792]{2,1,0:T(8,128)(2,1)}, bf16[4,96,1792]{2,1,0:T(8,128)(2,1)}, u32[]{:S(2)}, u32[]{:S(2)}) collective-permute-start(bf16[4,96,1792]{2,1,0:T(8,128)(2,1)} %pad_maximum_fusion.8), channel_id=1, source_target_pairs={{0,24},{1,25},{2,26},{3,27},{8,16},{9,17},{10,18},{11,19},{16,8},{... | collective-permute-start | bytes 4128776 | tf_op jit(solution)/shard_map/ppermute | solution.py:104
  471.7 31.8 %collective-permute-start.44 = (bf16[256,1536]{1,0:T(8,128)(2,1)}, bf16[256,1536]{1,0:T(8,128)(2,1)S(1)}, u32[]{:S(2)}, u32[]{:S(2)}) collective-permute-start(bf16[256,1536]{1,0:T(8,128)(2,1)} %get-tuple-element.273), channel_id=1, source_target_pairs={{1,0},{5,1},{0,2},{4,3},{3,4},{7,5},{2,6},{6,7},{9,8},{13,9},{8,10... | collective-permute-start | bytes 2359304 | tf_op jit(solution)/shard_map/ppermute | solution.py:221
  475.0 35.2 %collective-permute-start.43 = (bf16[256,1536]{1,0:T(8,128)(2,1)S(1)}, bf16[256,1536]{1,0:T(8,128)(2,1)S(1)}, u32[]{:S(2)}, u32[]{:S(2)}) collective-permute-start(bf16[256,1536]{1,0:T(8,128)(2,1)S(1)} %get-tuple-element.274), channel_id=1, source_target_pairs={{0,0},{4,1},{1,2},{5,3},{2,4},{6,5},{3,6},{7,7},{8,8},{12,9},{9,10... | collective-permute-start | bytes 2359304 | tf_op jit(solution)/shard_map/ppermute | solution.py:221
  514.5 35.6 %collective-permute-start.48 = (bf16[96,1792]{1,0:T(8,128)(2,1)S(1)}, bf16[96,1792]{1,0:T(8,128)(2,1)S(1)}, u32[]{:S(2)}, u32[]{:S(2)}) collective-permute-start(bf16[96,1792]{1,0:T(8,128)(2,1)S(1)} %get-tuple-element.269), channel_id=1, source_target_pairs={{0,2},{1,3},{2,0},{3,1},{8,10},{9,11},{10,8},{11,9},{16,18},{17,19... | collective-permute-start | bytes 1032200 | tf_op jit(solution)/shard_map/ppermute | solution.py:64
  519.6 30.5 %collective-permute-start.47 = (bf16[96,1792]{1,0:T(8,128)(2,1)S(1)}, bf16[96,1792]{1,0:T(8,128)(2,1)S(1)}, u32[]{:S(2)}, u32[]{:S(2)}) collective-permute-start(bf16[96,1792]{1,0:T(8,128)(2,1)S(1)} %get-tuple-element.270), channel_id=1, source_target_pairs={{0,1},{1,2},{2,3},{3,0},{8,9},{9,10},{10,11},{11,8},{16,17},{17,18... | collective-permute-start | bytes 1032200 | tf_op jit(solution)/shard_map/ppermute | solution.py:64
  (85 other events, 836.6 us)
where the time goes:
time: 567 us; the launch traced here: 559 us
  waiting for transfers between devices  190 us (34%)
  Pallas kernels  121 us (21%)
  starting transfers between devices  87.4 us (15%)
  other arithmetic  61.6 us (11%)
  matrix products  58.9 us (10%)
  local copies, waits for them, and re-layouts  37.1 us (7%)
    ppermute x17, waiting for transfers between devices, moved(): return lax.ppermute(array, ('chip', 'seg'), pairs)  118 us
    dot_general x8, matrix products, dot(): lax.dot_general(a, b, (contract, ((), ())), preferred_element_type=f32)  58.9 us
    pallas_call x1, Pallas kernels, scan_backward(): pl.pallas_call(lambda *refs: backward_kernel(group, *refs), grid=(segs,),...  48.9 us
    ppermute x4, waiting for transfers between devices, send_sequence(): lax.ppermute(piece, ('core', 'seg'), line_perm(turn, False))  39.8 us
    ppermute x17, starting transfers between devices, moved(): return lax.ppermute(array, ('chip', 'seg'), pairs)  28.6 us
    pallas_call x1, Pallas kernels, scan_forward(): pl.pallas_call(forward_kernel, grid=(segs,), out_shape=(jax.ShapeDtypeStr...  22.1 us
    pallas_call x2, Pallas kernels, half_products(): pl.pallas_call(lambda *refs: half_kernel(transposed, len(terms), *refs),...  20.6 us
    ppermute x18, starting transfers between devices, moved_plane(): return lax.ppermute(array, ('chip', 'seg'), pairs)  16.8 us
  transfers between devices with their start and end apart: 57, of which 20 were waited for; matrix products, arithmetic and copies ran while one was open for 21% of the time, Pallas kernels for 22%

commit v1 on v0

--- a/solution.py
+++ b/solution.py
@@ -369,6 +369,16 @@
     return total, seen
 
 
+def exact_sums(chosen, array):
+    chosen = jnp.where(chosen, 1.0, 0.0).astype(bf16)
+    result = 0.0
+    for _ in range(3):
+        part = array.astype(bf16)
+        array = array - part.astype(f32)
+        result = result + dot(chosen, part, ((1,), (0,)))
+    return result
+
+
 def step_terms(raw, head, seg_len):
     shifted = raw + head[1:2]
     step = jnp.maximum(shifted, 0.0) + jnp.log1p(jnp.exp(-jnp.abs(shifted)))
@@ -376,10 +386,7 @@
     at_or_before = lax.broadcasted_iota(jnp.int32, (seg_len, seg_len), 0) >= lax.broadcasted_iota(
         jnp.int32, (seg_len, seg_len), 1
     )
-    sums = lax.dot_general(
-        jnp.where(at_or_before, 1.0, 0.0), log_decay, (((1,), (0,)), ((), ())),
-        precision=lax.Precision.HIGHEST, preferred_element_type=f32,
-    )
+    sums = exact_sums(at_or_before, log_decay)
     return shifted, step, log_decay, sums * LOG2E
 
 
@@ -608,10 +615,7 @@
     at_or_after = lax.broadcasted_iota(jnp.int32, (seg_len, seg_len), 0) <= lax.broadcasted_iota(
         jnp.int32, (seg_len, seg_len), 1
     )
-    log_grad = lax.dot_general(
-        jnp.where(at_or_after, 1.0, 0.0), sum_grad, (((1,), (0,)), ((), ())),
-        precision=lax.Precision.HIGHEST, preferred_element_type=f32,
-    )
+    log_grad = exact_sums(at_or_after, sum_grad)
     grad_raw = (step_grad + head_ref[0:1] * log_grad) * jax.nn.sigmoid(shifted)
     grad_raw_ref[...] = grad_raw
     head_grad_ref[CONV + 1 : CONV + 2] += jnp.sum(log_grad * log_decay, axis=0, keepdims=True)
@@ -885,6 +889,7 @@
     out_all = gather_plane(out_own, plane_steps())
     gate_matrix = whole_matrix([gate_own, *gate_near, *gate_far], True)
     gate_input = dot(normed, gate_matrix, ((1,), (0,)))
+    gate_input, cot_first = tie(gate_input, cot_got[0])
 
     silu_gate = jax.nn.silu(gate_input)
     gated = values * silu_gate
@@ -892,8 +897,8 @@
     squares_other = to_partner(squares)
     scale = lax.rsqrt((squares + squares_other) / INNER + epsilon)[:, None]
     mixed, mixed_turned = mixed_tokens(gated, scale, gain_gate, seg_len)
-    mixed_turned, out_all, cot_got = tie(mixed_turned, out_all, cot_got)
-    cot_half = order_sequence(cot_got, place)
+    mixed_turned, out_all, cot_second = tie(mixed_turned, out_all, cot_got[1])
+    cot_half = order_sequence([cot_first, cot_second], place)
     cot_other = to_partner(cot_half)
     cot = in_core_order(cot_half, cot_other, core, 1)
     upstream = cot.reshape(tokens, model_width)
@@ -959,7 +964,6 @@
     sent_normed, early_got, conv_near, small, x_grad, rest_grad = tie(
         sent_normed, early_got, conv_near, small, x_grad, rest_grad
     )
-    conv_far = reduce_plane([x_grad, rest_grad], far_steps())
     other_normed = to_partner(sent_normed)
     wide_hidden = hidden_half.astype(f32)
     hidden_scale = lax.rsqrt(jnp.mean(wide_hidden * wide_hidden, axis=-1, keepdims=True) + epsilon)
@@ -968,10 +972,15 @@
     along = jnp.mean(grad_normed * hidden_unit, axis=-1, keepdims=True)
     grad_hidden = hidden_scale * (grad_normed - hidden_unit * along)
     grad_in = (cot_half.astype(f32) + grad_hidden).astype(bf16)
-    grad_in, conv_far = tie(send_back(grad_in, place), conv_far)
+    grad_in, x_grad, rest_grad = tie(grad_in, x_grad, rest_grad)
+    grad_in = send_back(grad_in, place)
+    conv_far = reduce_plane([x_grad, rest_grad], far_steps())
+    grad_in, conv_far = tie(grad_in, conv_far)
     late = reduce_z([([plane_part([x_grad, rest_grad], 0, 0)], [*conv_near, *conv_far])])
-    for dim in range(3):
+    for dim in range(2):
         small = small + sum(moved(small, dim, by) for by in range(1, chip_dims()[dim]))
+    for bit in range((line - 1).bit_length()):
+        small = small + exchanged(small, 2**bit)
     small_other = to_partner(small)
     late_got, small_other = tie(arrivals(late), small_other)
     early_share = total([*early_kept, *early_got])

time: 567 us -> 561 us (0.989)
  waiting for transfers between devices: 190 us -> 179 us
  starting transfers between devices: 87.4 us -> 95.2 us
  other arithmetic: 61.6 us -> 68.1 us
    ppermute x12, starting transfers between devices: 9.89 us -> 19.4 us  [to_partner(): return lax.ppermute(array, 'core', [(0, 1), (1, 0)])]
    ppermute x17 -> x14, waiting for transfers between devices: 118 us -> 110 us  [moved(): return lax.ppermute(array, ('chip', 'seg'), pairs)]
    ppermute x4, waiting for transfers between devices: 39.8 us -> 32.4 us  [send_sequence(): lax.ppermute(piece, ('core', 'seg'), line_perm(turn, False))]
    ppermute x18, waiting for transfers between devices: 16.7 us -> 23.5 us  [moved_plane(): return lax.ppermute(array, ('chip', 'seg'), pairs)]
    ppermute x4, waiting for transfers between devices: 6.67 us -> 0.01 us  [send_back(): lax.ppermute(piece, ('core', 'seg'), line_perm(turn, True))]
    ppermute x17 -> x14, starting transfers between devices: 28.6 us -> 22.8 us  [moved(): return lax.ppermute(array, ('chip', 'seg'), pairs)]
    unnamed x127 -> x117, local copies, waits for them, and re-layouts: 12.6 us -> 12.7 us
  transfers between devices with their start and end apart: 57 -> 56, of which waited for: 20 -> 21; matrix products, arithmetic and copies ran while one was open for 21% -> 21% of each run, Pallas kernels for 22% -> 21%
where the time goes in v1:
time: 561 us; the launch traced here: 553 us
  waiting for transfers between devices  179 us (32%)
  Pallas kernels  118 us (21%)
  starting transfers between devices  95.2 us (17%)
  other arithmetic  68.1 us (12%)
  matrix products  54.7 us (10%)
  local copies, waits for them, and re-layouts  35 us (6%)
    ppermute x14, waiting for transfers between devices, moved(): return lax.ppermute(array, ('chip', 'seg'), pairs)  110 us
    dot_general x8, matrix products, dot(): lax.dot_general(a, b, (contract, ((), ())), preferred_element_type=f32)  54.7 us
    pallas_call x1, Pallas kernels, scan_backward(): pl.pallas_call(lambda *refs: backward_kernel(group, *refs), grid=(segs,),...  47.3 us
    ppermute x4, waiting for transfers between devices, send_sequence(): lax.ppermute(piece, ('core', 'seg'), line_perm(turn, False))  32.4 us
    ppermute x18, waiting for transfers between devices, moved_plane(): return lax.ppermute(array, ('chip', 'seg'), pairs)  23.5 us
    ppermute x14, starting transfers between devices, moved(): return lax.ppermute(array, ('chip', 'seg'), pairs)  22.8 us
    pallas_call x1, Pallas kernels, scan_forward(): pl.pallas_call(forward_kernel, grid=(segs,), out_shape=(jax.ShapeDtypeStr...  21 us
    pallas_call x2, Pallas kernels, half_products(): pl.pallas_call(lambda *refs: half_kernel(transposed, len(terms), *refs),...  20.5 us
  transfers between devices with their start and end apart: 56, of which 21 were waited for; matrix products, arithmetic and copies ran while one was open for 21% of the time, Pallas kernels for 21%

profile of v1, /device:TPU:1, one launch (start us, length us, event | category | flops | bytes accessed | tf_op | source)
XLA Modules:
  0.0 552.7 jit_solution(2597805169498014134)
XLA Ops:
  14.7 7.2 %collective-permute-done.3 = bf16[2,48,1920]{2,1,0:T(8,128)(2,1)S(1)} collective-permute-done((bf16[2,48,1920]{2,1,0:T(8,128)(2,1)S(1)}, bf16[2,48,1920]{2,1,0:T(8,128)(2,1)S(1)}, u32[]{:S(2)}, u32[]{:S(2)}) %collective-permute-start.3) | collective-permute-done | bytes 368672 | tf_op jit(solution)/shard_map/ppermute | solution.py:64
  21.9 23.5 %collective-permute-done.2 = bf16[2,48,1920]{2,1,0:T(8,128)(2,1)S(1)} collective-permute-done((bf16[2,48,1920]{2,1,0:T(8,128)(2,1)S(1)}, bf16[2,48,1920]{2,1,0:T(8,128)(2,1)S(1)}, u32[]{:S(2)}, u32[]{:S(2)}) %collective-permute-start.2) | collective-permute-done | bytes 368672 | tf_op jit(solution)/shard_map/ppermute | solution.py:64
  50.7 6.2 %collective-permute-start.7 = (bf16[256,1536]{1,0:T(8,128)(2,1)}, bf16[256,1536]{1,0:T(8,128)(2,1)}, u32[]{:S(2)}, u32[]{:S(2)}) collective-permute-start(bf16[256,1536]{1,0:T(8,128)(2,1)} %get-tuple-element.296), channel_id=1, source_target_pairs={{0,0},{1,4},{2,1},{3,5},{4,2},{5,6},{6,3},{7,7},{8,8},{9,12},{10,9... | collective-permute-start | bytes 2359304 | tf_op jit(solution)/shard_map/ppermute | solution.py:210
  56.9 15.6 %collective-permute-done.8 = bf16[256,1536]{1,0:T(8,128)(2,1)} collective-permute-done((bf16[256,1536]{1,0:T(8,128)(2,1)}, bf16[256,1536]{1,0:T(8,128)(2,1)}, u32[]{:S(2)}, u32[]{:S(2)}) %collective-permute-start.8) | collective-permute-done | bytes 786464 | tf_op jit(solution)/shard_map/ppermute | solution.py:210
  72.6 8.5 %collective-permute-done.7 = bf16[256,1536]{1,0:T(8,128)(2,1)} collective-permute-done((bf16[256,1536]{1,0:T(8,128)(2,1)}, bf16[256,1536]{1,0:T(8,128)(2,1)}, u32[]{:S(2)}, u32[]{:S(2)}) %collective-permute-start.7) | collective-permute-done | bytes 786464 | tf_op jit(solution)/shard_map/ppermute | solution.py:210
  85.6 9.8 %collective-permute-start.11 = (bf16[2,48,1536]{2,1,0:T(8,128)(2,1)S(1)}, bf16[2,48,1536]{2,1,0:T(8,128)(2,1)}, u32[]{:S(2)}, u32[]{:S(2)}) collective-permute-start(bf16[2,48,1536]{2,1,0:T(8,128)(2,1)S(1)} %pad_maximum_fusion.12), channel_id=1, source_target_pairs={{0,2},{1,3},{2,0},{3,1},{8,10},{9,11},{10,8},{11,9},{16,18},{17,19... | collective-permute-start | bytes 884744 | tf_op jit(solution)/shard_map/ppermute | solution.py:64
  95.9 5.3 collective-permute-done.12
  101.2 19.8 %collective-permute-done.11 = bf16[2,48,1536]{2,1,0:T(8,128)(2,1)} collective-permute-done((bf16[2,48,1536]{2,1,0:T(8,128)(2,1)S(1)}, bf16[2,48,1536]{2,1,0:T(8,128)(2,1)}, u32[]{:S(2)}, u32[]{:S(2)}) %collective-permute-start.11) | collective-permute-done | bytes 294944 | tf_op jit(solution)/shard_map/ppermute | solution.py:64
  125.8 5.5 collective-permute-start.16
  131.3 5.4 shard_map.143
  138.2 5.6 %shard_map.144 = (bf16[1024,1536]{1,0:T(8,128)(2,1)}, bf16[1536,1024]{1,0:T(8,128)(2,1)}) custom-call(s32[1]{0:T(128)} %bitcast.refs_0_.refs_14_.core_ref, bf16[2,256,1536]{2,1,0:T(8,128)(2,1)S(1)} %pad_maximum_fusion.1.refs_1_, bf16[2,256,1536]{2,1,0:T(8,128)(2,1)} %collective-permute-done.13.refs_2_, f32[1,1536]{1,0:T(1,128)S(1)} %reshape_reshape_squeeze.3.refs_3_), custom_call_target="tpu_custom_call" | custom-call | flops 1024 | bytes 1024 | tf_op jit(solution)/shard_map/pallas_call | solution.py:291
  143.8 11.9 %fusion.47.proj_ref.refs_0_.refs_1_.refs_4_.refs_5_ = f32[1024,1920]{1,0:T(8,128)} fusion(bf16[1024,1536]{1,0:T(8,128)(2,1)} %get-tuple-element.161, bf16[1536,1920]{1,0:T(8,128)(2,1)} %bitcast.240), kind=kOutput, calls=%fused_computation.188 | convolution fusion | flops 6039797760 | bytes 16908288 | tf_op jit(solution)/shard_map/dot_general | solution.py:264
  159.8 21.0 %shard_map.145 = (f32[1024,1536]{1,0:T(8,128)}, bf16[4,128,1536]{2,1,0:T(8,128)(2,1)S(1)}, f32[128,1536]{1,0:T(8,128)}, f32[32,128]{1,0:T(8,128)}) custom-call(f32[1024,1920]{1,0:T(8,128)} %fusion.47.proj_ref.refs_0_.refs_1_.refs_4_.refs_5_, f32[8,1920]{1,0:T(8,128)S(1)} %select_maximum_fusion.taps_ref.refs_2_.refs_6_, ...), custom_call_target="tpu_custom_call" | custom-call | flops 1024 | bytes 1024 | tf_op jit(solution)/shard_map/pallas_call | solution.py:464
  182.2 5.8 %collective-permute-done.18 = bf16[2,96,1536]{2,1,0:T(8,128)(2,1)S(1)} collective-permute-done((bf16[2,96,1536]{2,1,0:T(8,128)(2,1)S(1)}, bf16[2,96,1536]{2,1,0:T(8,128)(2,1)S(1)}, u32[]{:S(2)}, u32[]{:S(2)}) %collective-permute-start.18) | collective-permute-done | bytes 589856 | tf_op jit(solution)/shard_map/ppermute | solution.py:77
  198.7 5.2 shard_map.146
  203.9 8.0 %fusion.48 = f32[1024,1536]{1,0:T(8,128)S(1)} fusion(bf16[1024,1536]{1,0:T(8,128)(2,1)} %get-tuple-element.161, bf16[1536,1536]{1,0:T(8,128)(2,1)} %bitcast.257), kind=kOutput, calls=%fused_computation.189 | convolution fusion | flops 4831838208 | bytes 14155776 | tf_op jit(solution)/shard_map/dot_general | solution.py:264
  211.9 8.2 %collective-permute-done.19 = bf16[256,1536]{1,0:T(8,128)(2,1)} collective-permute-done((bf16[256,1536]{1,0:T(8,128)(2,1)}, bf16[256,1536]{1,0:T(8,128)(2,1)}, u32[]{:S(2)}, u32[]{:S(2)}) %collective-permute-start.19) | collective-permute-done | bytes 786464 | tf_op jit(solution)/shard_map/ppermute | solution.py:210
  225.5 5.6 %shard_map.147 = (bf16[1024,1536]{1,0:T(8,128)(2,1)S(1)}, bf16[1536,1024]{1,0:T(8,128)(2,1)}) custom-call(f32[1024,1536]{1,0:T(8,128)} %get-tuple-element.259.gated_ref, f32[1024,1]{1,0:T(8,128)S(1)} %copy.56.scale_ref, f32[1,1536]{1,0:T(1,128)S(1)} %reshape_reshape.15.gain_ref), custom_call_target="tpu_custom_call" | custom-call | flops 1024 | bytes 1024 | tf_op jit(solution)/shard_map/pallas_call | solution.py:326
  231.2 9.3 %collective-permute-done.22.refs_3_ = bf16[4,96,1536]{2,1,0:T(8,128)(2,1)} collective-permute-done((bf16[4,96,1536]{2,1,0:T(8,128)(2,1)S(1)}, bf16[4,96,1536]{2,1,0:T(8,128)(2,1)}, u32[]{:S(2)}, u32[]{:S(2)}) %collective-permute-start.22) | collective-permute-done | bytes 1179680 | tf_op jit(solution)/shard_map/ppermute | solution.py:104
  254.3 5.3 convolution_convert_fusion.2
  268.8 8.6 %shard_map.149 = (f32[2,256,1536]{2,1,0:T(8,128)S(1)}, bf16[2,256,1536]{2,1,0:T(8,128)(2,1)S(1)}) custom-call(s32[1]{0:T(128)} %bitcast.refs_0_.refs_14_.core_ref, bf16[1024,1536]{1,0:T(8,128)(2,1)} %copy-done, bf16[1536,1536]{1,0:T(8,128)(2,1)} %bitcast.246), custom_call_target="tpu_custom_call" | custom-call | flops 1024 | bytes 1024 | tf_op jit(solution)/shard_map/pallas_call | solution.py:745
  278.3 7.4 %fusion.49 = f32[1024,1536]{1,0:T(8,128)S(1)} fusion(bf16[1024,1536]{1,0:T(8,128)(2,1)S(1)} %bitcast.264, bf16[1536,1536]{1,0:T(8,128)(2,1)} %bitcast.247), kind=kOutput, calls=%fused_computation.190 | convolution fusion | flops 4831838208 | bytes 14155776 | tf_op jit(solution)/shard_map/dot_general | solution.py:264
  296.2 10.7 %fusion.11 = (f32[1024,1536]{1,0:T(8,128)}, bf16[1024,1536]{1,0:T(8,128)(2,1)S(1)}) fusion(f32[1024]{0:T(1024)S(1)} %add_multiply_fusion.1, f32[1024,1536]{1,0:T(8,128)S(1)} %bitcast.238, f32[1024,1536]{1,0:T(8,128)} %copy-done.6, f32[1536]{0:T(1024)S(1)} %mul.138, f32[1024]{0:T(1024)S(1)} %add_rsqrt_fusion, f32[1024,1536]{1,0:T(8,128)} %copy-done.5, ...), kind=kLoop, calls=%fused_computation.33 | loop fusion | flops 26738688 | bytes 34617344 | tf_op jit(solution)/shard_map/mul | solution.py:924
  309.9 5.3 convolution_convert_fusion.1
  315.2 9.2 %collective-permute-done.30 = bf16[4,96,1536]{2,1,0:T(8,128)(2,1)S(1)} collective-permute-done((bf16[4,96,1536]{2,1,0:T(8,128)(2,1)S(1)}, bf16[4,96,1536]{2,1,0:T(8,128)(2,1)S(1)}, u32[]{:S(2)}, u32[]{:S(2)}) %collective-permute-start.30) | collective-permute-done | bytes 1179680 | tf_op jit(solution)/shard_map/ppermute | solution.py:104
  335.8 47.3 %shard_map.150 = (bf16[1024,1536]{1,0:T(8,128)(2,1)}, f32[1024,128]{1,0:T(8,128)S(1)}, f32[1024,128]{1,0:T(8,128)}, f32[1024,128]{1,0:T(8,128)S(1)}, f32[8,1536]...) custom-call(f32[1024,1920]{1,0:T(8,128)} %fusion.47.proj_ref.refs_0_., ...), custom_call_target="tpu_custom_call" | custom-call | flops 1024 | bytes 1024 | tf_op jit(solution)/shard_map/pallas_call | solution.py:657
  397.9 6.7 %convolution_convert_fusion = bf16[1536,1536]{1,0:T(8,128)(2,1)} fusion(bf16[1536,1024]{1,0:T(8,128)(2,1)S(1)} %copy-done.43, bf16[1024,1536]{1,0:T(8,128)(2,1)S(1)} %copy-done.22), kind=kOutput, calls=%fused_computation | convolution fusion | flops 4834197504 | bytes 11010048 | tf_op jit(solution)/shard_map/dot_general | solution.py:264
  414.7 7.0 %fusion.50.refs_7_ = f32[1024,1536]{1,0:T(8,128)} fusion(bf16[1024,1536]{1,0:T(8,128)(2,1)S(1)} %copy-done.26, bf16[1536,1536]{1,0:T(8,128)(2,1)S(1)} %bitcast.260), kind=kOutput, calls=%fused_computation.191 | convolution fusion | flops 4831838208 | bytes 14155776 | tf_op jit(solution)/shard_map/dot_general | solution.py:264
  421.8 11.9 %shard_map.152 = (f32[2,256,1536]{2,1,0:T(8,128)S(1)}, bf16[2,256,1536]{2,1,0:T(8,128)(2,1)}) custom-call(s32[1]{0:T(128)} %bitcast.refs_0_.refs_14_.core_ref, bf16[1024,1536]{1,0:T(8,128)(2,1)} %get-tuple-element.208.refs_1_, bf16[1024,128]{1,0:T(8,128)(2,1)S(1)} %get-tuple-element.212.refs_2_, bf16[1024,128]{1,0:T(8,128)(2,1)S(1)} %convert_element_type.162.refs_3_, ...), custom_call_target="tpu_custom_call" | custom-call | flops 1024 | bytes 1024 | tf_op jit(solution)/shard_map/pallas_call | solution.py:745
  433.8 11.4 %collective-permute-done.38 = bf16[96,3072]{1,0:T(8,128)(2,1)} collective-permute-done((bf16[96,3072]{1,0:T(8,128)(2,1)}, bf16[96,3072]{1,0:T(8,128)(2,1)}, u32[]{:S(2)}, u32[]{:S(2)}) %collective-permute-start.38) | collective-permute-done | bytes 589856 | tf_op jit(solution)/shard_map/ppermute | solution.py:64
  473.9 16.7 %collective-permute-done.51 = f32[8,1664]{1,0:T(8,128)S(1)} collective-permute-done((f32[8,1664]{1,0:T(8,128)S(1)}, f32[8,1664]{1,0:T(8,128)S(1)}, u32[]{:S(2)}, u32[]{:S(2)}) %collective-permute-start.51) | collective-permute-done | bytes 53280 | tf_op jit(solution)/shard_map/ppermute | solution.py:64
  522.1 21.6 %collective-permute-done.48 = bf16[96,1792]{1,0:T(8,128)(2,1)S(1)} collective-permute-done((bf16[96,1792]{1,0:T(8,128)(2,1)S(1)}, bf16[96,1792]{1,0:T(8,128)(2,1)S(1)}, u32[]{:S(2)}, u32[]{:S(2)}) %collective-permute-start.48) | collective-permute-done | bytes 344096 | tf_op jit(solution)/shard_map/ppermute | solution.py:64
  (374 shorter events, 193.5 us)
Async XLA Ops:
  14.2 31.2 %collective-permute-start.2 = (bf16[2,48,1920]{2,1,0:T(8,128)(2,1)S(1)}, bf16[2,48,1920]{2,1,0:T(8,128)(2,1)S(1)}, u32[]{:S(2)}, u32[]{:S(2)}) collective-permute-start(bf16[2,48,1920]{2,1,0:T(8,128)(2,1)S(1)} %pad_maximum_fusion.11), channel_id=1, source_target_pairs={{0,2},{1,3},{2,0},{3,1},{8,10},{9,11},{10,8},{11,9},{16,18},{17,19... | collective-permute-start | bytes 1105928 | tf_op jit(solution)/shard_map/ppermute | solution.py:64
  14.2 31.2 %collective-permute-start.1 = (bf16[2,48,1920]{2,1,0:T(8,128)(2,1)S(1)}, bf16[2,48,1920]{2,1,0:T(8,128)(2,1)S(1)}, u32[]{:S(2)}, u32[]{:S(2)}) collective-permute-start(bf16[2,48,1920]{2,1,0:T(8,128)(2,1)S(1)} %pad_maximum_fusion.11), channel_id=1, source_target_pairs={{0,1},{1,2},{2,3},{3,0},{8,9},{9,10},{10,11},{11,8},{16,17},{17,18... | collective-permute-start | bytes 1105928 | tf_op jit(solution)/shard_map/ppermute | solution.py:64
  45.6 35.5 %collective-permute-start.6 = (bf16[4,2,48,1920]{3,2,1,0:T(8,128)(2,1)S(1)}, bf16[4,2,48,1920]{3,2,1,0:T(8,128)(2,1)S(1)}, u32[]{:S(2)}, u32[]{:S(2)}) collective-permute-start(bf16[4,2,48,1920]{3,2,1,0:T(8,128)(2,1)S(1)} %pad_maximum_fusion.5.refs_1_), channel_id=1, source_target_pairs={{0,16},{1,17},{2,18},{3,19},{8,24},{9,25},{10,26},{11,27},{16,0},{... | collective-permute-start | bytes 4423688 | tf_op jit(solution)/shard_map/ppermute | solution.py:104
  46.9 34.2 %collective-permute-start.5 = (bf16[4,2,48,1920]{3,2,1,0:T(8,128)(2,1)S(1)}, bf16[4,2,48,1920]{3,2,1,0:T(8,128)(2,1)}, u32[]{:S(2)}, u32[]{:S(2)}) collective-permute-start(bf16[4,2,48,1920]{3,2,1,0:T(8,128)(2,1)S(1)} %pad_maximum_fusion.5.refs_1_), channel_id=1, source_target_pairs={{0,8},{1,9},{2,10},{3,11},{8,0},{9,1},{10,2},{11,3},{16,24},{17,25... | collective-permute-start | bytes 4423688 | tf_op jit(solution)/shard_map/ppermute | solution.py:104
  50.7 30.4 %collective-permute-start.7 = (bf16[256,1536]{1,0:T(8,128)(2,1)}, bf16[256,1536]{1,0:T(8,128)(2,1)}, u32[]{:S(2)}, u32[]{:S(2)}) collective-permute-start(bf16[256,1536]{1,0:T(8,128)(2,1)} %get-tuple-element.296), channel_id=1, source_target_pairs={{0,0},{1,4},{2,1},{3,5},{4,2},{5,6},{6,3},{7,7},{8,8},{9,12},{10,9... | collective-permute-start | bytes 2359304 | tf_op jit(solution)/shard_map/ppermute | solution.py:210
  84.1 37.0 %collective-permute-start.13 = (bf16[2,256,1536]{2,1,0:T(8,128)(2,1)S(1)}, bf16[2,256,1536]{2,1,0:T(8,128)(2,1)}, u32[]{:S(2)}, u32[]{:S(2)}) collective-permute-start(bf16[2,256,1536]{2,1,0:T(8,128)(2,1)S(1)} %pad_maximum_fusion.1.refs_1_), channel_id=1, source_target_pairs={{0,4},{4,0},{1,5},{5,1},{2,6},{6,2},{3,7},{7,3},{8,12},{12,8},{9,1... | collective-permute-start | bytes 4718600 | tf_op jit(solution)/shard_map/ppermute | solution.py:36
  85.2 35.9 %collective-permute-start.9 = (bf16[4,2,48,1920]{3,2,1,0:T(8,128)(2,1)S(1)}, bf16[4,2,48,1920]{3,2,1,0:T(8,128)(2,1)}, u32[]{:S(2)}, u32[]{:S(2)}) collective-permute-start(bf16[4,2,48,1920]{3,2,1,0:T(8,128)(2,1)S(1)} %pad_maximum_fusion.5.refs_1_), channel_id=1, source_target_pairs={{0,24},{1,25},{2,26},{3,27},{8,16},{9,17},{10,18},{11,19},{16,8},{... | collective-permute-start | bytes 4423688 | tf_op jit(solution)/shard_map/ppermute | solution.py:104
  85.6 35.4 %collective-permute-start.11 = (bf16[2,48,1536]{2,1,0:T(8,128)(2,1)S(1)}, bf16[2,48,1536]{2,1,0:T(8,128)(2,1)}, u32[]{:S(2)}, u32[]{:S(2)}) collective-permute-start(bf16[2,48,1536]{2,1,0:T(8,128)(2,1)S(1)} %pad_maximum_fusion.12), channel_id=1, source_target_pairs={{0,2},{1,3},{2,0},{3,1},{8,10},{9,11},{10,8},{11,9},{16,18},{17,19... | collective-permute-start | bytes 884744 | tf_op jit(solution)/shard_map/ppermute | solution.py:64
  123.4 32.4 %collective-permute-start.15 = (bf16[4,2,48,1536]{3,2,1,0:T(8,128)(2,1)}, bf16[4,2,48,1536]{3,2,1,0:T(8,128)(2,1)}, u32[]{:S(2)}, u32[]{:S(2)}) collective-permute-start(bf16[4,2,48,1536]{3,2,1,0:T(8,128)(2,1)} %pad_maximum_fusion.9.refs_1_), channel_id=1, source_target_pairs={{0,16},{1,17},{2,18},{3,19},{8,24},{9,25},{10,26},{11,27},{16,0},{... | collective-permute-start | bytes 3538952 | tf_op jit(solution)/shard_map/ppermute | solution.py:104
  124.6 31.1 %collective-permute-start.14 = (bf16[4,2,48,1536]{3,2,1,0:T(8,128)(2,1)}, bf16[4,2,48,1536]{3,2,1,0:T(8,128)(2,1)}, u32[]{:S(2)}, u32[]{:S(2)}) collective-permute-start(bf16[4,2,48,1536]{3,2,1,0:T(8,128)(2,1)} %pad_maximum_fusion.9.refs_1_), channel_id=1, source_target_pairs={{0,8},{1,9},{2,10},{3,11},{8,0},{9,1},{10,2},{11,3},{16,24},{17,25... | collective-permute-start | bytes 3538952 | tf_op jit(solution)/shard_map/ppermute | solution.py:104
  125.8 29.9 %collective-permute-start.16 = (bf16[1,96,1536]{2,1,0:T(8,128)(2,1)}, bf16[1,96,1536]{2,1,0:T(8,128)(2,1)S(1)}, u32[]{:S(2)}, u32[]{:S(2)}) collective-permute-start(bf16[1,96,1536]{2,1,0:T(8,128)(2,1)} %bitcast.27), channel_id=1, source_target_pairs={{0,1},{1,0},{2,3},{3,2},{4,5},{5,4},{6,7},{7,6},{8,9},{9,8},{10,11... | collective-permute-start | bytes 884744 | tf_op jit(solution)/shard_map/ppermute | solution.py:77
  155.7 32.2 %collective-permute-start.17 = (bf16[4,2,48,1536]{3,2,1,0:T(8,128)(2,1)}, bf16[4,2,48,1536]{3,2,1,0:T(8,128)(2,1)}, u32[]{:S(2)}, u32[]{:S(2)}) collective-permute-start(bf16[4,2,48,1536]{3,2,1,0:T(8,128)(2,1)} %pad_maximum_fusion.9.refs_1_), channel_id=1, source_target_pairs={{0,24},{1,25},{2,26},{3,27},{8,16},{9,17},{10,18},{11,19},{16,8},{... | collective-permute-start | bytes 3538952 | tf_op jit(solution)/shard_map/ppermute | solution.py:104
  188.0 43.2 %collective-permute-start.23 = (bf16[4,96,1536]{2,1,0:T(8,128)(2,1)S(1)}, bf16[4,96,1536]{2,1,0:T(8,128)(2,1)}, u32[]{:S(2)}, u32[]{:S(2)}) collective-permute-start(bf16[4,96,1536]{2,1,0:T(8,128)(2,1)S(1)} %constant_dynamic-update-slice_fusion.refs_1_), channel_id=1, source_target_pairs={{0,24},{1,25},{2,26},{3,27},{8,16},{9,17},{10,18},{11,19},{16,8},{... | collective-permute-start | bytes 3538952 | tf_op jit(solution)/shard_map/ppermute | solution.py:104
  188.1 52.5 %collective-permute-start.22 = (bf16[4,96,1536]{2,1,0:T(8,128)(2,1)S(1)}, bf16[4,96,1536]{2,1,0:T(8,128)(2,1)}, u32[]{:S(2)}, u32[]{:S(2)}) collective-permute-start(bf16[4,96,1536]{2,1,0:T(8,128)(2,1)S(1)} %constant_dynamic-update-slice_fusion.refs_1_), channel_id=1, source_target_pairs={{0,16},{1,17},{2,18},{3,19},{8,24},{9,25},{10,26},{11,27},{16,0},{... | collective-permute-start | bytes 3538952 | tf_op jit(solution)/shard_map/ppermute | solution.py:104
  188.5 52.0 %collective-permute-start.21 = (bf16[4,96,1536]{2,1,0:T(8,128)(2,1)S(1)}, bf16[4,96,1536]{2,1,0:T(8,128)(2,1)}, u32[]{:S(2)}, u32[]{:S(2)}) collective-permute-start(bf16[4,96,1536]{2,1,0:T(8,128)(2,1)S(1)} %constant_dynamic-update-slice_fusion.refs_1_), channel_id=1, source_target_pairs={{0,8},{1,9},{2,10},{3,11},{8,0},{9,1},{10,2},{11,3},{16,24},{17,25... | collective-permute-start | bytes 3538952 | tf_op jit(solution)/shard_map/ppermute | solution.py:104
  192.0 39.2 %collective-permute-start.24 = (bf16[256,1536]{1,0:T(8,128)(2,1)}, bf16[256,1536]{1,0:T(8,128)(2,1)}, u32[]{:S(2)}, u32[]{:S(2)}) collective-permute-start(bf16[256,1536]{1,0:T(8,128)(2,1)} %get-tuple-element.291), channel_id=1, source_target_pairs={{0,1},{1,5},{2,0},{3,4},{4,3},{5,7},{6,2},{7,6},{8,9},{9,13},{10,8... | collective-permute-start | bytes 2359304 | tf_op jit(solution)/shard_map/ppermute | solution.py:210
  295.9 28.5 %collective-permute-start.30 = (bf16[4,96,1536]{2,1,0:T(8,128)(2,1)S(1)}, bf16[4,96,1536]{2,1,0:T(8,128)(2,1)S(1)}, u32[]{:S(2)}, u32[]{:S(2)}) collective-permute-start(bf16[4,96,1536]{2,1,0:T(8,128)(2,1)S(1)} %dynamic-slice_bitcast_fusion.7), channel_id=1, source_target_pairs={{0,24},{1,25},{2,26},{3,27},{8,16},{9,17},{10,18},{11,19},{16,8},{... | collective-permute-start | bytes 3538952 | tf_op jit(solution)/shard_map/ppermute | solution.py:104
  326.6 59.1 %collective-permute-start.33 = (bf16[4,96,1536]{2,1,0:T(8,128)(2,1)}, bf16[4,96,1536]{2,1,0:T(8,128)(2,1)}, u32[]{:S(2)}, u32[]{:S(2)}) collective-permute-start(bf16[4,96,1536]{2,1,0:T(8,128)(2,1)} %get-tuple-element.269), channel_id=1, source_target_pairs={{0,24},{1,25},{2,26},{3,27},{8,16},{9,17},{10,18},{11,19},{16,8},{... | collective-permute-start | bytes 3538952 | tf_op jit(solution)/shard_map/ppermute | solution.py:104
  326.8 58.9 %collective-permute-start.32 = (bf16[4,96,1536]{2,1,0:T(8,128)(2,1)}, bf16[4,96,1536]{2,1,0:T(8,128)(2,1)}, u32[]{:S(2)}, u32[]{:S(2)}) collective-permute-start(bf16[4,96,1536]{2,1,0:T(8,128)(2,1)} %get-tuple-element.270), channel_id=1, source_target_pairs={{0,16},{1,17},{2,18},{3,19},{8,24},{9,25},{10,26},{11,27},{16,0},{... | collective-permute-start | bytes 3538952 | tf_op jit(solution)/shard_map/ppermute | solution.py:104
  327.8 57.9 %collective-permute-start.31 = (bf16[4,96,1536]{2,1,0:T(8,128)(2,1)}, bf16[4,96,1536]{2,1,0:T(8,128)(2,1)}, u32[]{:S(2)}, u32[]{:S(2)}) collective-permute-start(bf16[4,96,1536]{2,1,0:T(8,128)(2,1)} %get-tuple-element.271), channel_id=1, source_target_pairs={{0,8},{1,9},{2,10},{3,11},{8,0},{9,1},{10,2},{11,3},{16,24},{17,25... | collective-permute-start | bytes 3538952 | tf_op jit(solution)/shard_map/ppermute | solution.py:104
  330.5 55.1 %collective-permute-start.35 = (bf16[256,1536]{1,0:T(8,128)(2,1)}, bf16[256,1536]{1,0:T(8,128)(2,1)}, u32[]{:S(2)}, u32[]{:S(2)}) collective-permute-start(bf16[256,1536]{1,0:T(8,128)(2,1)} %get-tuple-element.287), channel_id=1, source_target_pairs={{1,0},{5,1},{0,2},{4,3},{3,4},{7,5},{2,6},{6,7},{9,8},{13,9},{8,10... | collective-permute-start | bytes 2359304 | tf_op jit(solution)/shard_map/ppermute | solution.py:221
  332.6 53.0 %collective-permute-start.34 = (bf16[256,1536]{1,0:T(8,128)(2,1)}, bf16[256,1536]{1,0:T(8,128)(2,1)}, u32[]{:S(2)}, u32[]{:S(2)}) collective-permute-start(bf16[256,1536]{1,0:T(8,128)(2,1)} %get-tuple-element.288), channel_id=1, source_target_pairs={{0,0},{4,1},{1,2},{5,3},{2,4},{6,5},{3,6},{7,7},{8,8},{12,9},{9,10... | collective-permute-start | bytes 2359304 | tf_op jit(solution)/shard_map/ppermute | solution.py:221
  395.6 38.1 %collective-permute-start.39 = (bf16[96,3072]{1,0:T(8,128)(2,1)}, bf16[96,3072]{1,0:T(8,128)(2,1)}, u32[]{:S(2)}, u32[]{:S(2)}) collective-permute-start(bf16[96,3072]{1,0:T(8,128)(2,1)} %get-tuple-element.266), channel_id=1, source_target_pairs={{0,3},{1,0},{2,1},{3,2},{8,11},{9,8},{10,9},{11,10},{16,19},{17,16... | collective-permute-start | bytes 1769480 | tf_op jit(solution)/shard_map/ppermute | solution.py:64
  397.5 36.3 %collective-permute-start.37 = (bf16[96,3072]{1,0:T(8,128)(2,1)}, bf16[96,3072]{1,0:T(8,128)(2,1)}, u32[]{:S(2)}, u32[]{:S(2)}) collective-permute-start(bf16[96,3072]{1,0:T(8,128)(2,1)} %get-tuple-element.267), channel_id=1, source_target_pairs={{0,1},{1,2},{2,3},{3,0},{8,9},{9,10},{10,11},{11,8},{16,17},{17,18... | collective-permute-start | bytes 1769480 | tf_op jit(solution)/shard_map/ppermute | solution.py:64
  397.5 47.7 %collective-permute-start.38 = (bf16[96,3072]{1,0:T(8,128)(2,1)}, bf16[96,3072]{1,0:T(8,128)(2,1)}, u32[]{:S(2)}, u32[]{:S(2)}) collective-permute-start(bf16[96,3072]{1,0:T(8,128)(2,1)} %get-tuple-element.268), channel_id=1, source_target_pairs={{0,2},{1,3},{2,0},{3,1},{8,10},{9,11},{10,8},{11,9},{16,18},{17,19... | collective-permute-start | bytes 1769480 | tf_op jit(solution)/shard_map/ppermute | solution.py:64
  412.2 33.0 %collective-permute-start.40 = (bf16[4,96,1792]{2,1,0:T(8,128)(2,1)}, bf16[4,96,1792]{2,1,0:T(8,128)(2,1)}, u32[]{:S(2)}, u32[]{:S(2)}) collective-permute-start(bf16[4,96,1792]{2,1,0:T(8,128)(2,1)} %pad_maximum_fusion.6), channel_id=1, source_target_pairs={{0,8},{1,9},{2,10},{3,11},{8,0},{9,1},{10,2},{11,3},{16,24},{17,25... | collective-permute-start | bytes 4128776 | tf_op jit(solution)/shard_map/ppermute | solution.py:104
  413.5 31.6 %collective-permute-start.41 = (bf16[4,96,1792]{2,1,0:T(8,128)(2,1)}, bf16[4,96,1792]{2,1,0:T(8,128)(2,1)}, u32[]{:S(2)}, u32[]{:S(2)}) collective-permute-start(bf16[4,96,1792]{2,1,0:T(8,128)(2,1)} %pad_maximum_fusion.7), channel_id=1, source_target_pairs={{0,16},{1,17},{2,18},{3,19},{8,24},{9,25},{10,26},{11,27},{16,0},{... | collective-permute-start | bytes 4128776 | tf_op jit(solution)/shard_map/ppermute | solution.py:104
  457.7 48.8 %collective-permute-start.45 = (bf16[4,96,1792]{2,1,0:T(8,128)(2,1)S(1)}, bf16[4,96,1792]{2,1,0:T(8,128)(2,1)S(1)}, u32[]{:S(2)}, u32[]{:S(2)}) collective-permute-start(bf16[4,96,1792]{2,1,0:T(8,128)(2,1)S(1)} %pad_maximum_fusion.8), channel_id=1, source_target_pairs={{0,24},{1,25},{2,26},{3,27},{8,16},{9,17},{10,18},{11,19},{16,8},{... | collective-permute-start | bytes 4128776 | tf_op jit(solution)/shard_map/ppermute | solution.py:104
  460.5 46.0 %collective-permute-start.44 = (bf16[256,1536]{1,0:T(8,128)(2,1)}, bf16[256,1536]{1,0:T(8,128)(2,1)}, u32[]{:S(2)}, u32[]{:S(2)}) collective-permute-start(bf16[256,1536]{1,0:T(8,128)(2,1)} %get-tuple-element.281), channel_id=1, source_target_pairs={{1,0},{5,1},{0,2},{4,3},{3,4},{7,5},{2,6},{6,7},{9,8},{13,9},{8,10... | collective-permute-start | bytes 2359304 | tf_op jit(solution)/shard_map/ppermute | solution.py:221
  464.9 41.5 %collective-permute-start.43 = (bf16[256,1536]{1,0:T(8,128)(2,1)}, bf16[256,1536]{1,0:T(8,128)(2,1)}, u32[]{:S(2)}, u32[]{:S(2)}) collective-permute-start(bf16[256,1536]{1,0:T(8,128)(2,1)} %get-tuple-element.282), channel_id=1, source_target_pairs={{0,0},{4,1},{1,2},{5,3},{2,4},{6,5},{3,6},{7,7},{8,8},{12,9},{9,10... | collective-permute-start | bytes 2359304 | tf_op jit(solution)/shard_map/ppermute | solution.py:221
  514.6 29.1 %collective-permute-start.48 = (bf16[96,1792]{1,0:T(8,128)(2,1)S(1)}, bf16[96,1792]{1,0:T(8,128)(2,1)S(1)}, u32[]{:S(2)}, u32[]{:S(2)}) collective-permute-start(bf16[96,1792]{1,0:T(8,128)(2,1)S(1)} %get-tuple-element.277), channel_id=1, source_target_pairs={{0,2},{1,3},{2,0},{3,1},{8,10},{9,11},{10,8},{11,9},{16,18},{17,19... | collective-permute-start | bytes 1032200 | tf_op jit(solution)/shard_map/ppermute | solution.py:64
  514.6 29.1 %collective-permute-start.47 = (bf16[96,1792]{1,0:T(8,128)(2,1)S(1)}, bf16[96,1792]{1,0:T(8,128)(2,1)S(1)}, u32[]{:S(2)}, u32[]{:S(2)}) collective-permute-start(bf16[96,1792]{1,0:T(8,128)(2,1)S(1)} %get-tuple-element.278), channel_id=1, source_target_pairs={{0,1},{1,2},{2,3},{3,0},{8,9},{9,10},{10,11},{11,8},{16,17},{17,18... | collective-permute-start | bytes 1032200 | tf_op jit(solution)/shard_map/ppermute | solution.py:64
  (79 other events, 759.9 us)

commit v2 on v1

--- a/solution.py
+++ b/solution.py
@@ -904,14 +904,17 @@
     upstream = cot.reshape(tokens, model_width)
     by_owner = lambda grad: grad.astype(bf16).reshape(chip_dims() + (-1, grad.shape[1]))
     out_grad = by_owner(dot(mixed_turned, upstream, ((1,), (0,))))
-    out_got_near = reduce_plane([out_grad], near_steps())
+    cut = model_width // 2
+    out_first = [reduce_send([out_grad[..., :cut]], 1, 1, bf16), reduce_send([out_grad[..., cut:]], 0, 0, bf16)]
     out_matrix = whole_matrix([out_own, *out_all], False, True)
     branch, branch_sent = half_products(core, [(mixed, out_matrix, None)], seg_len, model_width, False)
     branch_sent, upstream = tie(branch_sent, upstream)
     branch_other = to_partner(branch_sent)
     grad_mixed = dot(upstream, out_matrix, ((1,), (1,)))
-    grad_mixed, out_got_near, out_grad = tie(grad_mixed, out_got_near, out_grad)
-    out_got_far = reduce_plane([out_grad], far_steps())
+    grad_mixed, out_got = tie(grad_mixed, arrivals(out_first))
+    out_second = [
+        reduce_send(kept + received, 0, dim, bf16) for (kept, received), dim in zip(arrived(out_first, out_got), (0, 1))
+    ]
     unit = gated * scale
     gain_grad = grad_mixed * gain_gate
     along = jnp.sum(gain_grad * unit, axis=1)
@@ -925,7 +928,7 @@
     sigmoid = jax.nn.sigmoid(gate_input)
     grad_gate = (grad_gated * values * (sigmoid * (1.0 + gate_input * (1.0 - sigmoid)))).astype(bf16)
     gate_grad = by_owner(dot(normed_turned, grad_gate, ((1,), (0,))))
-    gate_grad, grad_values, out_got_far = tie(gate_grad, grad_values, out_got_far)
+    gate_grad, grad_values, out_got = tie(gate_grad, grad_values, arrivals(out_second))
     gate_got = reduce_plane([gate_grad], plane_steps())
     scan = lambda later: scan_backward(
         0, core, projected, taps, head, skip, rim, later, prior, values, grad_values, seg_len
@@ -936,7 +939,7 @@
     back, gate_got, hidden_out, grad_gate = tie(back, gate_got, hidden_out, grad_gate)
     ((early_kept, early_got),) = reduce_z(
         [
-            ([plane_part([out_grad], 0, 0)], [*out_got_near, *out_got_far]),
+            *arrived(out_second, out_got),
             ([plane_part([gate_grad], 0, 0)], gate_got),
         ]
     )

time: 561 us -> 559 us (level)
  waiting for transfers between devices: 179 us -> 167 us
    ppermute x18 -> x15, waiting for transfers between devices: 23.5 us -> 9.31 us  [moved_plane(): return lax.ppermute(array, ('chip', 'seg'), pairs)]
    ppermute x14 -> x18, starting transfers between devices: 22.8 us -> 26.1 us  [moved(): return lax.ppermute(array, ('chip', 'seg'), pairs)]
    ppermute x14 -> x18, waiting for transfers between devices: 110 us -> 112 us  [moved(): return lax.ppermute(array, ('chip', 'seg'), pairs)]
    ppermute x18 -> x15, starting transfers between devices: 17.1 us -> 15.7 us  [moved_plane(): return lax.ppermute(array, ('chip', 'seg'), pairs)]
  transfers between devices with their start and end apart: 56 -> 57, of which waited for: 21 -> 20; matrix products, arithmetic and copies ran while one was open for 21% -> 22% of each run, Pallas kernels for 21% -> 21%
where the time goes in v2:
time: 559 us; the launch traced here: 550 us
  waiting for transfers between devices  167 us (30%)
  Pallas kernels  118 us (21%)
  starting transfers between devices  98.7 us (18%)
  other arithmetic  70.5 us (13%)
  matrix products  58 us (10%)
  local copies, waits for them, and re-layouts  35.5 us (6%)
    ppermute x18, waiting for transfers between devices, moved(): return lax.ppermute(array, ('chip', 'seg'), pairs)  112 us
    dot_general x8, matrix products, dot(): lax.dot_general(a, b, (contract, ((), ())), preferred_element_type=f32)  58 us
    pallas_call x1, Pallas kernels, scan_backward(): pl.pallas_call(lambda *refs: backward_kernel(group, *refs), grid=(segs,),...  47.2 us
    ppermute x4, waiting for transfers between devices, send_sequence(): lax.ppermute(piece, ('core', 'seg'), line_perm(turn, False))  32.3 us
    ppermute x18, starting transfers between devices, moved(): return lax.ppermute(array, ('chip', 'seg'), pairs)  26.1 us
    ppermute x12, starting transfers between devices, to_partner(): return lax.ppermute(array, 'core', [(0, 1), (1, 0)])  22.3 us
    pallas_call x1, Pallas kernels, scan_forward(): pl.pallas_call(forward_kernel, grid=(segs,), out_shape=(jax.ShapeDtypeStr...  21 us
    pallas_call x2, Pallas kernels, half_products(): pl.pallas_call(lambda *refs: half_kernel(transposed, len(terms), *refs),...  20.5 us
  transfers between devices with their start and end apart: 57, of which 20 were waited for; matrix products, arithmetic and copies ran while one was open for 22% of the time, Pallas kernels for 21%

profile of v2, /device:TPU:1, one launch (start us, length us, event | category | flops | bytes accessed | tf_op | source)
XLA Modules:
  0.0 550.3 jit_solution(2975791666967679146)
XLA Ops:
  14.7 7.2 %collective-permute-done.3 = bf16[2,48,1920]{2,1,0:T(8,128)(2,1)S(1)} collective-permute-done((bf16[2,48,1920]{2,1,0:T(8,128)(2,1)S(1)}, bf16[2,48,1920]{2,1,0:T(8,128)(2,1)S(1)}, u32[]{:S(2)}, u32[]{:S(2)}) %collective-permute-start.3) | collective-permute-done | bytes 368672 | tf_op jit(solution)/shard_map/ppermute | solution.py:64
  21.9 23.5 %collective-permute-done.2 = bf16[2,48,1920]{2,1,0:T(8,128)(2,1)S(1)} collective-permute-done((bf16[2,48,1920]{2,1,0:T(8,128)(2,1)S(1)}, bf16[2,48,1920]{2,1,0:T(8,128)(2,1)S(1)}, u32[]{:S(2)}, u32[]{:S(2)}) %collective-permute-start.2) | collective-permute-done | bytes 368672 | tf_op jit(solution)/shard_map/ppermute | solution.py:64
  50.7 6.2 %collective-permute-start.7 = (bf16[256,1536]{1,0:T(8,128)(2,1)}, bf16[256,1536]{1,0:T(8,128)(2,1)}, u32[]{:S(2)}, u32[]{:S(2)}) collective-permute-start(bf16[256,1536]{1,0:T(8,128)(2,1)} %get-tuple-element.296), channel_id=1, source_target_pairs={{0,0},{1,4},{2,1},{3,5},{4,2},{5,6},{6,3},{7,7},{8,8},{9,12},{10,9... | collective-permute-start | bytes 2359304 | tf_op jit(solution)/shard_map/ppermute | solution.py:210
  56.9 15.6 %collective-permute-done.8 = bf16[256,1536]{1,0:T(8,128)(2,1)} collective-permute-done((bf16[256,1536]{1,0:T(8,128)(2,1)}, bf16[256,1536]{1,0:T(8,128)(2,1)}, u32[]{:S(2)}, u32[]{:S(2)}) %collective-permute-start.8) | collective-permute-done | bytes 786464 | tf_op jit(solution)/shard_map/ppermute | solution.py:210
  72.6 8.5 %collective-permute-done.7 = bf16[256,1536]{1,0:T(8,128)(2,1)} collective-permute-done((bf16[256,1536]{1,0:T(8,128)(2,1)}, bf16[256,1536]{1,0:T(8,128)(2,1)}, u32[]{:S(2)}, u32[]{:S(2)}) %collective-permute-start.7) | collective-permute-done | bytes 786464 | tf_op jit(solution)/shard_map/ppermute | solution.py:210
  85.6 9.8 %collective-permute-start.11 = (bf16[2,48,1536]{2,1,0:T(8,128)(2,1)S(1)}, bf16[2,48,1536]{2,1,0:T(8,128)(2,1)}, u32[]{:S(2)}, u32[]{:S(2)}) collective-permute-start(bf16[2,48,1536]{2,1,0:T(8,128)(2,1)S(1)} %pad_maximum_fusion.13), channel_id=1, source_target_pairs={{0,2},{1,3},{2,0},{3,1},{8,10},{9,11},{10,8},{11,9},{16,18},{17,19... | collective-permute-start | bytes 884744 | tf_op jit(solution)/shard_map/ppermute | solution.py:64
  95.9 5.4 collective-permute-done.12
  101.3 19.8 %collective-permute-done.11 = bf16[2,48,1536]{2,1,0:T(8,128)(2,1)} collective-permute-done((bf16[2,48,1536]{2,1,0:T(8,128)(2,1)S(1)}, bf16[2,48,1536]{2,1,0:T(8,128)(2,1)}, u32[]{:S(2)}, u32[]{:S(2)}) %collective-permute-start.11) | collective-permute-done | bytes 294944 | tf_op jit(solution)/shard_map/ppermute | solution.py:64
  125.9 5.5 collective-permute-start.16
  131.4 5.4 shard_map.143
  138.3 5.6 %shard_map.144 = (bf16[1024,1536]{1,0:T(8,128)(2,1)}, bf16[1536,1024]{1,0:T(8,128)(2,1)}) custom-call(s32[1]{0:T(128)} %bitcast.refs_0_.refs_14_.core_ref, bf16[2,256,1536]{2,1,0:T(8,128)(2,1)S(1)} %pad_maximum_fusion.2.refs_1_, bf16[2,256,1536]{2,1,0:T(8,128)(2,1)} %collective-permute-done.13.refs_2_, f32[1,1536]{1,0:T(1,128)S(1)} %reshape_reshape_squeeze.3.refs_3_), custom_call_target="tpu_custom_call" | custom-call | flops 1024 | bytes 1024 | tf_op jit(solution)/shard_map/pallas_call | solution.py:291
  143.8 11.9 %fusion.41.proj_ref.refs_0_.refs_1_.refs_4_.refs_5_ = f32[1024,1920]{1,0:T(8,128)} fusion(bf16[1024,1536]{1,0:T(8,128)(2,1)} %get-tuple-element.161, bf16[1536,1920]{1,0:T(8,128)(2,1)} %bitcast.255), kind=kOutput, calls=%fused_computation.181 | convolution fusion | flops 6039797760 | bytes 16908288 | tf_op jit(solution)/shard_map/dot_general | solution.py:264
  159.9 21.0 %shard_map.145 = (f32[1024,1536]{1,0:T(8,128)}, bf16[4,128,1536]{2,1,0:T(8,128)(2,1)S(1)}, f32[128,1536]{1,0:T(8,128)}, f32[32,128]{1,0:T(8,128)}) custom-call(f32[1024,1920]{1,0:T(8,128)} %fusion.41.proj_ref.refs_0_.refs_1_.refs_4_.refs_5_, f32[8,1920]{1,0:T(8,128)S(1)} %select_maximum_fusion.taps_ref.refs_2_.refs_6_, ...), custom_call_target="tpu_custom_call" | custom-call | flops 1024 | bytes 1024 | tf_op jit(solution)/shard_map/pallas_call | solution.py:464
  182.2 5.7 %collective-permute-done.18 = bf16[2,96,1536]{2,1,0:T(8,128)(2,1)S(1)} collective-permute-done((bf16[2,96,1536]{2,1,0:T(8,128)(2,1)S(1)}, bf16[2,96,1536]{2,1,0:T(8,128)(2,1)S(1)}, u32[]{:S(2)}, u32[]{:S(2)}) %collective-permute-start.18) | collective-permute-done | bytes 589856 | tf_op jit(solution)/shard_map/ppermute | solution.py:77
  198.3 5.1 shard_map.146
  203.5 8.6 %fusion.42 = f32[1024,1536]{1,0:T(8,128)S(1)} fusion(bf16[1024,1536]{1,0:T(8,128)(2,1)} %get-tuple-element.161, bf16[1536,1536]{1,0:T(8,128)(2,1)} %bitcast.269), kind=kOutput, calls=%fused_computation.182 | convolution fusion | flops 4831838208 | bytes 14155776 | tf_op jit(solution)/shard_map/dot_general | solution.py:264
  212.1 8.1 %collective-permute-done.19 = bf16[256,1536]{1,0:T(8,128)(2,1)} collective-permute-done((bf16[256,1536]{1,0:T(8,128)(2,1)}, bf16[256,1536]{1,0:T(8,128)(2,1)}, u32[]{:S(2)}, u32[]{:S(2)}) %collective-permute-start.19) | collective-permute-done | bytes 786464 | tf_op jit(solution)/shard_map/ppermute | solution.py:210
  225.6 5.7 %shard_map.147 = (bf16[1024,1536]{1,0:T(8,128)(2,1)S(1)}, bf16[1536,1024]{1,0:T(8,128)(2,1)}) custom-call(f32[1024,1536]{1,0:T(8,128)} %get-tuple-element.259.gated_ref, f32[1024,1]{1,0:T(8,128)S(1)} %copy.56.scale_ref, f32[1,1536]{1,0:T(1,128)S(1)} %reshape_reshape.11.gain_ref), custom_call_target="tpu_custom_call" | custom-call | flops 1024 | bytes 1024 | tf_op jit(solution)/shard_map/pallas_call | solution.py:326
  231.3 9.3 %collective-permute-done.22.refs_3_ = bf16[4,96,1536]{2,1,0:T(8,128)(2,1)} collective-permute-done((bf16[4,96,1536]{2,1,0:T(8,128)(2,1)S(1)}, bf16[4,96,1536]{2,1,0:T(8,128)(2,1)}, u32[]{:S(2)}, u32[]{:S(2)}) %collective-permute-start.22) | collective-permute-done | bytes 1179680 | tf_op jit(solution)/shard_map/ppermute | solution.py:104
  254.3 5.3 convolution_convert_fusion.2
  269.5 8.6 %shard_map.149 = (f32[2,256,1536]{2,1,0:T(8,128)S(1)}, bf16[2,256,1536]{2,1,0:T(8,128)(2,1)S(1)}) custom-call(s32[1]{0:T(128)} %bitcast.refs_0_.refs_14_.core_ref, bf16[1024,1536]{1,0:T(8,128)(2,1)} %copy-done, bf16[1536,1536]{1,0:T(8,128)(2,1)} %bitcast.261), custom_call_target="tpu_custom_call" | custom-call | flops 1024 | bytes 1024 | tf_op jit(solution)/shard_map/pallas_call | solution.py:745
  278.8 7.0 %fusion.43 = f32[1024,1536]{1,0:T(8,128)S(1)} fusion(bf16[1024,1536]{1,0:T(8,128)(2,1)S(1)} %bitcast.277, bf16[1536,1536]{1,0:T(8,128)(2,1)} %bitcast.262), kind=kOutput, calls=%fused_computation.183 | convolution fusion | flops 4831838208 | bytes 14155776 | tf_op jit(solution)/shard_map/dot_general | solution.py:264
  299.1 10.6 %fusion.11 = (f32[1024,1536]{1,0:T(8,128)}, bf16[1024,1536]{1,0:T(8,128)(2,1)S(1)}) fusion(f32[1024]{0:T(1024)S(1)} %add_multiply_fusion.1, f32[1024,1536]{1,0:T(8,128)S(1)} %bitcast.253, f32[1024,1536]{1,0:T(8,128)} %copy-done.6, f32[1536]{0:T(1024)S(1)} %mul.132, f32[1024]{0:T(1024)S(1)} %add_rsqrt_fusion, f32[1024,1536]{1,0:T(8,128)} %copy-done.5, ...), kind=kLoop, calls=%fused_computation.26 | loop fusion | flops 26738688 | bytes 34617344 | tf_op jit(solution)/shard_map/mul | solution.py:927
  309.8 8.3 %convolution_convert_fusion.1 = bf16[1536,1536]{1,0:T(8,128)(2,1)S(1)} fusion(bf16[1536,1024]{1,0:T(8,128)(2,1)} %get-tuple-element.174, bf16[1024,1536]{1,0:T(8,128)(2,1)S(1)} %get-tuple-element.217), kind=kOutput, calls=%fused_computation.1 | convolution fusion | flops 4834197504 | bytes 11010048 | tf_op jit(solution)/shard_map/dot_general | solution.py:264
  331.1 47.2 %shard_map.150 = (bf16[1024,1536]{1,0:T(8,128)(2,1)}, f32[1024,128]{1,0:T(8,128)S(1)}, f32[1024,128]{1,0:T(8,128)}, f32[1024,128]{1,0:T(8,128)S(1)}, f32[8,1536]...) custom-call(f32[1024,1920]{1,0:T(8,128)} %fusion.41.proj_ref.refs_0_., ...), custom_call_target="tpu_custom_call" | custom-call | flops 1024 | bytes 1024 | tf_op jit(solution)/shard_map/pallas_call | solution.py:657
  394.8 6.8 %convolution_convert_fusion = bf16[1536,1536]{1,0:T(8,128)(2,1)} fusion(bf16[1536,1024]{1,0:T(8,128)(2,1)S(1)} %copy-done.43, bf16[1024,1536]{1,0:T(8,128)(2,1)S(1)} %copy-done.21), kind=kOutput, calls=%fused_computation | convolution fusion | flops 4834197504 | bytes 11010048 | tf_op jit(solution)/shard_map/dot_general | solution.py:264
  412.2 7.1 %fusion.44.refs_7_ = f32[1024,1536]{1,0:T(8,128)} fusion(bf16[1024,1536]{1,0:T(8,128)(2,1)S(1)} %copy-done.25, bf16[1536,1536]{1,0:T(8,128)(2,1)S(1)} %bitcast.272), kind=kOutput, calls=%fused_computation.184 | convolution fusion | flops 4831838208 | bytes 14155776 | tf_op jit(solution)/shard_map/dot_general | solution.py:264
  419.4 11.9 %shard_map.152 = (f32[2,256,1536]{2,1,0:T(8,128)S(1)}, bf16[2,256,1536]{2,1,0:T(8,128)(2,1)}) custom-call(s32[1]{0:T(128)} %bitcast.refs_0_.refs_14_.core_ref, bf16[1024,1536]{1,0:T(8,128)(2,1)} %get-tuple-element.209.refs_1_, bf16[1024,128]{1,0:T(8,128)(2,1)S(1)} %get-tuple-element.213.refs_2_, bf16[1024,128]{1,0:T(8,128)(2,1)S(1)} %convert_element_type.221.refs_3_, ...), custom_call_target="tpu_custom_call" | custom-call | flops 1024 | bytes 1024 | tf_op jit(solution)/shard_map/pallas_call | solution.py:745
  431.3 10.7 %collective-permute-done.39 = bf16[96,3072]{1,0:T(8,128)(2,1)} collective-permute-done((bf16[96,3072]{1,0:T(8,128)(2,1)}, bf16[96,3072]{1,0:T(8,128)(2,1)}, u32[]{:S(2)}, u32[]{:S(2)}) %collective-permute-start.39) | collective-permute-done | bytes 589856 | tf_op jit(solution)/shard_map/ppermute | solution.py:64
  463.7 7.3 %collective-permute-start.47 = (bf16[48,1536]{1,0:T(8,128)(2,1)}, bf16[48,1536]{1,0:T(8,128)(2,1)}, u32[]{:S(2)}, u32[]{:S(2)}) collective-permute-start(bf16[48,1536]{1,0:T(8,128)(2,1)} %get-tuple-element.316), channel_id=1, source_target_pairs={{0,4},{4,0},{1,5},{5,1},{2,6},{6,2},{3,7},{7,3},{8,12},{12,8},{9,1... | collective-permute-start | bytes 442376 | tf_op jit(solution)/shard_map/ppermute | solution.py:36
  474.1 14.0 %collective-permute-done.52 = f32[8,1664]{1,0:T(8,128)S(1)} collective-permute-done((f32[8,1664]{1,0:T(8,128)S(1)}, f32[8,1664]{1,0:T(8,128)S(1)}, u32[]{:S(2)}, u32[]{:S(2)}) %collective-permute-start.52) | collective-permute-done | bytes 53280 | tf_op jit(solution)/shard_map/ppermute | solution.py:64
  518.6 22.9 %collective-permute-done.49 = bf16[96,1792]{1,0:T(8,128)(2,1)S(1)} collective-permute-done((bf16[96,1792]{1,0:T(8,128)(2,1)S(1)}, bf16[96,1792]{1,0:T(8,128)(2,1)S(1)}, u32[]{:S(2)}, u32[]{:S(2)}) %collective-permute-start.49) | collective-permute-done | bytes 344096 | tf_op jit(solution)/shard_map/ppermute | solution.py:64
  (381 shorter events, 192.1 us)
Async XLA Ops:
  14.2 31.2 %collective-permute-start.2 = (bf16[2,48,1920]{2,1,0:T(8,128)(2,1)S(1)}, bf16[2,48,1920]{2,1,0:T(8,128)(2,1)S(1)}, u32[]{:S(2)}, u32[]{:S(2)}) collective-permute-start(bf16[2,48,1920]{2,1,0:T(8,128)(2,1)S(1)} %pad_maximum_fusion.12), channel_id=1, source_target_pairs={{0,2},{1,3},{2,0},{3,1},{8,10},{9,11},{10,8},{11,9},{16,18},{17,19... | collective-permute-start | bytes 1105928 | tf_op jit(solution)/shard_map/ppermute | solution.py:64
  14.2 31.2 %collective-permute-start.1 = (bf16[2,48,1920]{2,1,0:T(8,128)(2,1)S(1)}, bf16[2,48,1920]{2,1,0:T(8,128)(2,1)S(1)}, u32[]{:S(2)}, u32[]{:S(2)}) collective-permute-start(bf16[2,48,1920]{2,1,0:T(8,128)(2,1)S(1)} %pad_maximum_fusion.12), channel_id=1, source_target_pairs={{0,1},{1,2},{2,3},{3,0},{8,9},{9,10},{10,11},{11,8},{16,17},{17,18... | collective-permute-start | bytes 1105928 | tf_op jit(solution)/shard_map/ppermute | solution.py:64
  45.6 35.5 %collective-permute-start.6 = (bf16[4,2,48,1920]{3,2,1,0:T(8,128)(2,1)S(1)}, bf16[4,2,48,1920]{3,2,1,0:T(8,128)(2,1)S(1)}, u32[]{:S(2)}, u32[]{:S(2)}) collective-permute-start(bf16[4,2,48,1920]{3,2,1,0:T(8,128)(2,1)S(1)} %pad_maximum_fusion.6.refs_1_), channel_id=1, source_target_pairs={{0,16},{1,17},{2,18},{3,19},{8,24},{9,25},{10,26},{11,27},{16,0},{... | collective-permute-start | bytes 4423688 | tf_op jit(solution)/shard_map/ppermute | solution.py:104
  46.9 34.2 %collective-permute-start.5 = (bf16[4,2,48,1920]{3,2,1,0:T(8,128)(2,1)S(1)}, bf16[4,2,48,1920]{3,2,1,0:T(8,128)(2,1)}, u32[]{:S(2)}, u32[]{:S(2)}) collective-permute-start(bf16[4,2,48,1920]{3,2,1,0:T(8,128)(2,1)S(1)} %pad_maximum_fusion.6.refs_1_), channel_id=1, source_target_pairs={{0,8},{1,9},{2,10},{3,11},{8,0},{9,1},{10,2},{11,3},{16,24},{17,25... | collective-permute-start | bytes 4423688 | tf_op jit(solution)/shard_map/ppermute | solution.py:104
  50.7 30.4 %collective-permute-start.7 = (bf16[256,1536]{1,0:T(8,128)(2,1)}, bf16[256,1536]{1,0:T(8,128)(2,1)}, u32[]{:S(2)}, u32[]{:S(2)}) collective-permute-start(bf16[256,1536]{1,0:T(8,128)(2,1)} %get-tuple-element.296), channel_id=1, source_target_pairs={{0,0},{1,4},{2,1},{3,5},{4,2},{5,6},{6,3},{7,7},{8,8},{9,12},{10,9... | collective-permute-start | bytes 2359304 | tf_op jit(solution)/shard_map/ppermute | solution.py:210
  84.1 37.0 %collective-permute-start.13 = (bf16[2,256,1536]{2,1,0:T(8,128)(2,1)S(1)}, bf16[2,256,1536]{2,1,0:T(8,128)(2,1)}, u32[]{:S(2)}, u32[]{:S(2)}) collective-permute-start(bf16[2,256,1536]{2,1,0:T(8,128)(2,1)S(1)} %pad_maximum_fusion.2.refs_1_), channel_id=1, source_target_pairs={{0,4},{4,0},{1,5},{5,1},{2,6},{6,2},{3,7},{7,3},{8,12},{12,8},{9,1... | collective-permute-start | bytes 4718600 | tf_op jit(solution)/shard_map/ppermute | solution.py:36
  85.2 35.9 %collective-permute-start.9 = (bf16[4,2,48,1920]{3,2,1,0:T(8,128)(2,1)S(1)}, bf16[4,2,48,1920]{3,2,1,0:T(8,128)(2,1)}, u32[]{:S(2)}, u32[]{:S(2)}) collective-permute-start(bf16[4,2,48,1920]{3,2,1,0:T(8,128)(2,1)S(1)} %pad_maximum_fusion.6.refs_1_), channel_id=1, source_target_pairs={{0,24},{1,25},{2,26},{3,27},{8,16},{9,17},{10,18},{11,19},{16,8},{... | collective-permute-start | bytes 4423688 | tf_op jit(solution)/shard_map/ppermute | solution.py:104
  85.6 35.5 %collective-permute-start.11 = (bf16[2,48,1536]{2,1,0:T(8,128)(2,1)S(1)}, bf16[2,48,1536]{2,1,0:T(8,128)(2,1)}, u32[]{:S(2)}, u32[]{:S(2)}) collective-permute-start(bf16[2,48,1536]{2,1,0:T(8,128)(2,1)S(1)} %pad_maximum_fusion.13), channel_id=1, source_target_pairs={{0,2},{1,3},{2,0},{3,1},{8,10},{9,11},{10,8},{11,9},{16,18},{17,19... | collective-permute-start | bytes 884744 | tf_op jit(solution)/shard_map/ppermute | solution.py:64
  123.4 32.4 %collective-permute-start.15 = (bf16[4,2,48,1536]{3,2,1,0:T(8,128)(2,1)}, bf16[4,2,48,1536]{3,2,1,0:T(8,128)(2,1)}, u32[]{:S(2)}, u32[]{:S(2)}) collective-permute-start(bf16[4,2,48,1536]{3,2,1,0:T(8,128)(2,1)} %pad_maximum_fusion.10.refs_1_), channel_id=1, source_target_pairs={{0,16},{1,17},{2,18},{3,19},{8,24},{9,25},{10,26},{11,27},{16,0},{... | collective-permute-start | bytes 3538952 | tf_op jit(solution)/shard_map/ppermute | solution.py:104
  124.7 31.1 %collective-permute-start.14 = (bf16[4,2,48,1536]{3,2,1,0:T(8,128)(2,1)}, bf16[4,2,48,1536]{3,2,1,0:T(8,128)(2,1)}, u32[]{:S(2)}, u32[]{:S(2)}) collective-permute-start(bf16[4,2,48,1536]{3,2,1,0:T(8,128)(2,1)} %pad_maximum_fusion.10.refs_1_), channel_id=1, source_target_pairs={{0,8},{1,9},{2,10},{3,11},{8,0},{9,1},{10,2},{11,3},{16,24},{17,25... | collective-permute-start | bytes 3538952 | tf_op jit(solution)/shard_map/ppermute | solution.py:104
  125.9 29.9 %collective-permute-start.16 = (bf16[1,96,1536]{2,1,0:T(8,128)(2,1)}, bf16[1,96,1536]{2,1,0:T(8,128)(2,1)S(1)}, u32[]{:S(2)}, u32[]{:S(2)}) collective-permute-start(bf16[1,96,1536]{2,1,0:T(8,128)(2,1)} %bitcast.27), channel_id=1, source_target_pairs={{0,1},{1,0},{2,3},{3,2},{4,5},{5,4},{6,7},{7,6},{8,9},{9,8},{10,11... | collective-permute-start | bytes 884744 | tf_op jit(solution)/shard_map/ppermute | solution.py:77
  155.8 32.2 %collective-permute-start.17 = (bf16[4,2,48,1536]{3,2,1,0:T(8,128)(2,1)}, bf16[4,2,48,1536]{3,2,1,0:T(8,128)(2,1)}, u32[]{:S(2)}, u32[]{:S(2)}) collective-permute-start(bf16[4,2,48,1536]{3,2,1,0:T(8,128)(2,1)} %pad_maximum_fusion.10.refs_1_), channel_id=1, source_target_pairs={{0,24},{1,25},{2,26},{3,27},{8,16},{9,17},{10,18},{11,19},{16,8},{... | collective-permute-start | bytes 3538952 | tf_op jit(solution)/shard_map/ppermute | solution.py:104
  159.7 28.3 %collective-permute-start.18 = (bf16[2,96,1536]{2,1,0:T(8,128)(2,1)S(1)}, bf16[2,96,1536]{2,1,0:T(8,128)(2,1)S(1)}, u32[]{:S(2)}, u32[]{:S(2)}) collective-permute-start(bf16[2,96,1536]{2,1,0:T(8,128)(2,1)S(1)} %pad_maximum_fusion.11), channel_id=1, source_target_pairs={{0,2},{1,3},{2,0},{3,1},{4,6},{5,7},{6,4},{7,5},{8,10},{9,11},{10,... | collective-permute-start | bytes 1769480 | tf_op jit(solution)/shard_map/ppermute | solution.py:77
  188.0 43.3 %collective-permute-start.23 = (bf16[4,96,1536]{2,1,0:T(8,128)(2,1)S(1)}, bf16[4,96,1536]{2,1,0:T(8,128)(2,1)}, u32[]{:S(2)}, u32[]{:S(2)}) collective-permute-start(bf16[4,96,1536]{2,1,0:T(8,128)(2,1)S(1)} %constant_dynamic-update-slice_fusion.refs_1_), channel_id=1, source_target_pairs={{0,24},{1,25},{2,26},{3,27},{8,16},{9,17},{10,18},{11,19},{16,8},{... | collective-permute-start | bytes 3538952 | tf_op jit(solution)/shard_map/ppermute | solution.py:104
  188.1 52.5 %collective-permute-start.22 = (bf16[4,96,1536]{2,1,0:T(8,128)(2,1)S(1)}, bf16[4,96,1536]{2,1,0:T(8,128)(2,1)}, u32[]{:S(2)}, u32[]{:S(2)}) collective-permute-start(bf16[4,96,1536]{2,1,0:T(8,128)(2,1)S(1)} %constant_dynamic-update-slice_fusion.refs_1_), channel_id=1, source_target_pairs={{0,16},{1,17},{2,18},{3,19},{8,24},{9,25},{10,26},{11,27},{16,0},{... | collective-permute-start | bytes 3538952 | tf_op jit(solution)/shard_map/ppermute | solution.py:104
  188.6 52.0 %collective-permute-start.21 = (bf16[4,96,1536]{2,1,0:T(8,128)(2,1)S(1)}, bf16[4,96,1536]{2,1,0:T(8,128)(2,1)}, u32[]{:S(2)}, u32[]{:S(2)}) collective-permute-start(bf16[4,96,1536]{2,1,0:T(8,128)(2,1)S(1)} %constant_dynamic-update-slice_fusion.refs_1_), channel_id=1, source_target_pairs={{0,8},{1,9},{2,10},{3,11},{8,0},{9,1},{10,2},{11,3},{16,24},{17,25... | collective-permute-start | bytes 3538952 | tf_op jit(solution)/shard_map/ppermute | solution.py:104
  192.0 39.3 %collective-permute-start.24 = (bf16[256,1536]{1,0:T(8,128)(2,1)}, bf16[256,1536]{1,0:T(8,128)(2,1)}, u32[]{:S(2)}, u32[]{:S(2)}) collective-permute-start(bf16[256,1536]{1,0:T(8,128)(2,1)} %get-tuple-element.291), channel_id=1, source_target_pairs={{0,1},{1,5},{2,0},{3,4},{4,3},{5,7},{6,2},{7,6},{8,9},{9,13},{10,8... | collective-permute-start | bytes 2359304 | tf_op jit(solution)/shard_map/ppermute | solution.py:210
  322.1 59.3 %collective-permute-start.34 = (bf16[4,96,1536]{2,1,0:T(8,128)(2,1)}, bf16[4,96,1536]{2,1,0:T(8,128)(2,1)}, u32[]{:S(2)}, u32[]{:S(2)}) collective-permute-start(bf16[4,96,1536]{2,1,0:T(8,128)(2,1)} %get-tuple-element.269), channel_id=1, source_target_pairs={{0,24},{1,25},{2,26},{3,27},{8,16},{9,17},{10,18},{11,19},{16,8},{... | collective-permute-start | bytes 3538952 | tf_op jit(solution)/shard_map/ppermute | solution.py:104
  322.8 58.6 %collective-permute-start.33 = (bf16[4,96,1536]{2,1,0:T(8,128)(2,1)}, bf16[4,96,1536]{2,1,0:T(8,128)(2,1)}, u32[]{:S(2)}, u32[]{:S(2)}) collective-permute-start(bf16[4,96,1536]{2,1,0:T(8,128)(2,1)} %get-tuple-element.270), channel_id=1, source_target_pairs={{0,16},{1,17},{2,18},{3,19},{8,24},{9,25},{10,26},{11,27},{16,0},{... | collective-permute-start | bytes 3538952 | tf_op jit(solution)/shard_map/ppermute | solution.py:104
  324.0 57.5 %collective-permute-start.32 = (bf16[4,96,1536]{2,1,0:T(8,128)(2,1)}, bf16[4,96,1536]{2,1,0:T(8,128)(2,1)}, u32[]{:S(2)}, u32[]{:S(2)}) collective-permute-start(bf16[4,96,1536]{2,1,0:T(8,128)(2,1)} %get-tuple-element.271), channel_id=1, source_target_pairs={{0,8},{1,9},{2,10},{3,11},{8,0},{9,1},{10,2},{11,3},{16,24},{17,25... | collective-permute-start | bytes 3538952 | tf_op jit(solution)/shard_map/ppermute | solution.py:104
  326.1 55.3 %collective-permute-start.36 = (bf16[256,1536]{1,0:T(8,128)(2,1)}, bf16[256,1536]{1,0:T(8,128)(2,1)}, u32[]{:S(2)}, u32[]{:S(2)}) collective-permute-start(bf16[256,1536]{1,0:T(8,128)(2,1)} %get-tuple-element.287), channel_id=1, source_target_pairs={{1,0},{5,1},{0,2},{4,3},{3,4},{7,5},{2,6},{6,7},{9,8},{13,9},{8,10... | collective-permute-start | bytes 2359304 | tf_op jit(solution)/shard_map/ppermute | solution.py:221
  328.6 52.8 %collective-permute-start.35 = (bf16[256,1536]{1,0:T(8,128)(2,1)}, bf16[256,1536]{1,0:T(8,128)(2,1)}, u32[]{:S(2)}, u32[]{:S(2)}) collective-permute-start(bf16[256,1536]{1,0:T(8,128)(2,1)} %get-tuple-element.288), channel_id=1, source_target_pairs={{0,0},{4,1},{1,2},{5,3},{2,4},{6,5},{3,6},{7,7},{8,8},{12,9},{9,10... | collective-permute-start | bytes 2359304 | tf_op jit(solution)/shard_map/ppermute | solution.py:221
  393.1 38.2 %collective-permute-start.40 = (bf16[96,3072]{1,0:T(8,128)(2,1)}, bf16[96,3072]{1,0:T(8,128)(2,1)}, u32[]{:S(2)}, u32[]{:S(2)}) collective-permute-start(bf16[96,3072]{1,0:T(8,128)(2,1)} %get-tuple-element.266), channel_id=1, source_target_pairs={{0,3},{1,0},{2,1},{3,2},{8,11},{9,8},{10,9},{11,10},{16,19},{17,16... | collective-permute-start | bytes 1769480 | tf_op jit(solution)/shard_map/ppermute | solution.py:64
  394.5 47.5 %collective-permute-start.39 = (bf16[96,3072]{1,0:T(8,128)(2,1)}, bf16[96,3072]{1,0:T(8,128)(2,1)}, u32[]{:S(2)}, u32[]{:S(2)}) collective-permute-start(bf16[96,3072]{1,0:T(8,128)(2,1)} %get-tuple-element.267), channel_id=1, source_target_pairs={{0,2},{1,3},{2,0},{3,1},{8,10},{9,11},{10,8},{11,9},{16,18},{17,19... | collective-permute-start | bytes 1769480 | tf_op jit(solution)/shard_map/ppermute | solution.py:64
  394.5 47.5 %collective-permute-start.38 = (bf16[96,3072]{1,0:T(8,128)(2,1)}, bf16[96,3072]{1,0:T(8,128)(2,1)}, u32[]{:S(2)}, u32[]{:S(2)}) collective-permute-start(bf16[96,3072]{1,0:T(8,128)(2,1)} %get-tuple-element.268), channel_id=1, source_target_pairs={{0,1},{1,2},{2,3},{3,0},{8,9},{9,10},{10,11},{11,8},{16,17},{17,18... | collective-permute-start | bytes 1769480 | tf_op jit(solution)/shard_map/ppermute | solution.py:64
  409.2 32.8 %collective-permute-start.41 = (bf16[4,96,1792]{2,1,0:T(8,128)(2,1)}, bf16[4,96,1792]{2,1,0:T(8,128)(2,1)}, u32[]{:S(2)}, u32[]{:S(2)}) collective-permute-start(bf16[4,96,1792]{2,1,0:T(8,128)(2,1)} %pad_maximum_fusion.7), channel_id=1, source_target_pairs={{0,8},{1,9},{2,10},{3,11},{8,0},{9,1},{10,2},{11,3},{16,24},{17,25... | collective-permute-start | bytes 4128776 | tf_op jit(solution)/shard_map/ppermute | solution.py:104
  410.9 31.1 %collective-permute-start.42 = (bf16[4,96,1792]{2,1,0:T(8,128)(2,1)}, bf16[4,96,1792]{2,1,0:T(8,128)(2,1)}, u32[]{:S(2)}, u32[]{:S(2)}) collective-permute-start(bf16[4,96,1792]{2,1,0:T(8,128)(2,1)} %pad_maximum_fusion.8), channel_id=1, source_target_pairs={{0,16},{1,17},{2,18},{3,19},{8,24},{9,25},{10,26},{11,27},{16,0},{... | collective-permute-start | bytes 4128776 | tf_op jit(solution)/shard_map/ppermute | solution.py:104
  455.2 49.3 %collective-permute-start.46 = (bf16[4,96,1792]{2,1,0:T(8,128)(2,1)S(1)}, bf16[4,96,1792]{2,1,0:T(8,128)(2,1)S(1)}, u32[]{:S(2)}, u32[]{:S(2)}) collective-permute-start(bf16[4,96,1792]{2,1,0:T(8,128)(2,1)S(1)} %pad_maximum_fusion.9), channel_id=1, source_target_pairs={{0,24},{1,25},{2,26},{3,27},{8,16},{9,17},{10,18},{11,19},{16,8},{... | collective-permute-start | bytes 4128776 | tf_op jit(solution)/shard_map/ppermute | solution.py:104
  457.5 47.0 %collective-permute-start.45 = (bf16[256,1536]{1,0:T(8,128)(2,1)}, bf16[256,1536]{1,0:T(8,128)(2,1)}, u32[]{:S(2)}, u32[]{:S(2)}) collective-permute-start(bf16[256,1536]{1,0:T(8,128)(2,1)} %get-tuple-element.281), channel_id=1, source_target_pairs={{1,0},{5,1},{0,2},{4,3},{3,4},{7,5},{2,6},{6,7},{9,8},{13,9},{8,10... | collective-permute-start | bytes 2359304 | tf_op jit(solution)/shard_map/ppermute | solution.py:221
  460.8 43.7 %collective-permute-start.44 = (bf16[256,1536]{1,0:T(8,128)(2,1)}, bf16[256,1536]{1,0:T(8,128)(2,1)}, u32[]{:S(2)}, u32[]{:S(2)}) collective-permute-start(bf16[256,1536]{1,0:T(8,128)(2,1)} %get-tuple-element.282), channel_id=1, source_target_pairs={{0,0},{4,1},{1,2},{5,3},{2,4},{6,5},{3,6},{7,7},{8,8},{12,9},{9,10... | collective-permute-start | bytes 2359304 | tf_op jit(solution)/shard_map/ppermute | solution.py:221
  511.1 30.4 %collective-permute-start.49 = (bf16[96,1792]{1,0:T(8,128)(2,1)S(1)}, bf16[96,1792]{1,0:T(8,128)(2,1)S(1)}, u32[]{:S(2)}, u32[]{:S(2)}) collective-permute-start(bf16[96,1792]{1,0:T(8,128)(2,1)S(1)} %get-tuple-element.277), channel_id=1, source_target_pairs={{0,2},{1,3},{2,0},{3,1},{8,10},{9,11},{10,8},{11,9},{16,18},{17,19... | collective-permute-start | bytes 1032200 | tf_op jit(solution)/shard_map/ppermute | solution.py:64
  511.1 30.4 %collective-permute-start.48 = (bf16[96,1792]{1,0:T(8,128)(2,1)S(1)}, bf16[96,1792]{1,0:T(8,128)(2,1)S(1)}, u32[]{:S(2)}, u32[]{:S(2)}) collective-permute-start(bf16[96,1792]{1,0:T(8,128)(2,1)S(1)} %get-tuple-element.278), channel_id=1, source_target_pairs={{0,1},{1,2},{2,3},{3,0},{8,9},{9,10},{10,11},{11,8},{16,17},{17,18... | collective-permute-start | bytes 1032200 | tf_op jit(solution)/shard_map/ppermute | solution.py:64
  (80 other events, 781.2 us)

commit v3 on v2

--- a/solution.py
+++ b/solution.py
@@ -407,8 +407,8 @@
         total, _ = conv_parts(proj_ref[:, at], tail_ref[:, at], taps_ref[:, at])
         return total * jax.nn.sigmoid(total)
 
-    b_low = activated(HALF).astype(bf16)
-    b_turned = activated(HALF).T.astype(bf16)
+    b_values = activated(HALF)
+    b_low, b_turned = b_values.astype(bf16), b_values.T.astype(bf16)
     c_low = activated(HALF + STATE).astype(bf16)
     _, step, _, sums = step_terms(proj_ref[:, HALF + 2 * STATE :], head_ref, seg_len)
     sums_turned, step_turned = sums.T, step.T
@@ -571,13 +571,14 @@
             grad_low = jnp.where(low if side == 0 else ~low, grad_values, 0.0).astype(bf16)
             at_source = jnp.broadcast_to(sums[:, head : head + 1], (seg_len, half))
             at_token = sums_turned[head : head + 1]
-            grad_weights = dot(stepped, grad_low, ((1,), (1,)))
+            upper_weights = dot(stepped[:half], grad_low, ((1,), (1,)))
+            lower_weights = dot(stepped[half:], grad_low[half:], ((1,), (1,)))
             first = jnp.exp2(jnp.minimum(at_token[:, :half] - at_source[:half], 0.0))
             after = jnp.exp2(at_token[:, half:] - at_source[:half])
             second = jnp.exp2(jnp.minimum(at_token[:, half:] - at_source[half:], 0.0))
-            first_grad = first_grad + first * grad_weights[:half, :half]
-            later_grad = later_grad + after * grad_weights[:half, half:]
-            second_grad = second_grad + second * grad_weights[half:, half:]
+            first_grad = first_grad + first * upper_weights[:, :half]
+            later_grad = later_grad + after * upper_weights[:, half:]
+            second_grad = second_grad + second * lower_weights
             upper = jnp.concatenate([first * first_scores, after * later_scores], axis=1).astype(bf16)
             early = early + dot(upper, grad_low, ((1,), (0,)))
             late = late + dot((second * second_scores).astype(bf16), grad_low[half:], ((1,), (0,)))

time: 559 us -> 558 us (level)
  no operation moved by 1% of the time
where the time goes in v3:
time: 558 us; the launch traced here: 550 us
  waiting for transfers between devices  167 us (30%)
  Pallas kernels  118 us (21%)
  starting transfers between devices  98.7 us (18%)
  other arithmetic  70.5 us (13%)
  matrix products  58 us (10%)
  local copies, waits for them, and re-layouts  35.5 us (6%)
    ppermute x18, waiting for transfers between devices, moved(): return lax.ppermute(array, ('chip', 'seg'), pairs)  112 us
    dot_general x8, matrix products, dot(): lax.dot_general(a, b, (contract, ((), ())), preferred_element_type=f32)  58 us
    pallas_call x1, Pallas kernels, scan_backward(): pl.pallas_call(lambda *refs: backward_kernel(group, *refs), grid=(segs,),...  47 us
    ppermute x4, waiting for transfers between devices, send_sequence(): lax.ppermute(piece, ('core', 'seg'), line_perm(turn, False))  32.3 us
    ppermute x18, starting transfers between devices, moved(): return lax.ppermute(array, ('chip', 'seg'), pairs)  26.1 us
    ppermute x12, starting transfers between devices, to_partner(): return lax.ppermute(array, 'core', [(0, 1), (1, 0)])  22.4 us
    pallas_call x1, Pallas kernels, scan_forward(): pl.pallas_call(forward_kernel, grid=(segs,), out_shape=(jax.ShapeDtypeStr...  21 us
    pallas_call x2, Pallas kernels, half_products(): pl.pallas_call(lambda *refs: half_kernel(transposed, len(terms), *refs),...  20.5 us
  transfers between devices with their start and end apart: 57, of which 20 were waited for; matrix products, arithmetic and copies ran while one was open for 22% of the time, Pallas kernels for 21%

profile of v3, /device:TPU:1, one launch (start us, length us, event | category | flops | bytes accessed | tf_op | source)
XLA Modules:
  0.0 550.1 jit_solution(3655616168106096517)
XLA Ops:
  14.7 7.2 %collective-permute-done.3 = bf16[2,48,1920]{2,1,0:T(8,128)(2,1)S(1)} collective-permute-done((bf16[2,48,1920]{2,1,0:T(8,128)(2,1)S(1)}, bf16[2,48,1920]{2,1,0:T(8,128)(2,1)S(1)}, u32[]{:S(2)}, u32[]{:S(2)}) %collective-permute-start.3) | collective-permute-done | bytes 368672 | tf_op jit(solution)/shard_map/ppermute | solution.py:64
  21.9 23.5 %collective-permute-done.2 = bf16[2,48,1920]{2,1,0:T(8,128)(2,1)S(1)} collective-permute-done((bf16[2,48,1920]{2,1,0:T(8,128)(2,1)S(1)}, bf16[2,48,1920]{2,1,0:T(8,128)(2,1)S(1)}, u32[]{:S(2)}, u32[]{:S(2)}) %collective-permute-start.2) | collective-permute-done | bytes 368672 | tf_op jit(solution)/shard_map/ppermute | solution.py:64
  50.7 6.2 %collective-permute-start.7 = (bf16[256,1536]{1,0:T(8,128)(2,1)}, bf16[256,1536]{1,0:T(8,128)(2,1)}, u32[]{:S(2)}, u32[]{:S(2)}) collective-permute-start(bf16[256,1536]{1,0:T(8,128)(2,1)} %get-tuple-element.296), channel_id=1, source_target_pairs={{0,0},{1,4},{2,1},{3,5},{4,2},{5,6},{6,3},{7,7},{8,8},{9,12},{10,9... | collective-permute-start | bytes 2359304 | tf_op jit(solution)/shard_map/ppermute | solution.py:210
  56.9 15.6 %collective-permute-done.8 = bf16[256,1536]{1,0:T(8,128)(2,1)} collective-permute-done((bf16[256,1536]{1,0:T(8,128)(2,1)}, bf16[256,1536]{1,0:T(8,128)(2,1)}, u32[]{:S(2)}, u32[]{:S(2)}) %collective-permute-start.8) | collective-permute-done | bytes 786464 | tf_op jit(solution)/shard_map/ppermute | solution.py:210
  72.6 8.5 %collective-permute-done.7 = bf16[256,1536]{1,0:T(8,128)(2,1)} collective-permute-done((bf16[256,1536]{1,0:T(8,128)(2,1)}, bf16[256,1536]{1,0:T(8,128)(2,1)}, u32[]{:S(2)}, u32[]{:S(2)}) %collective-permute-start.7) | collective-permute-done | bytes 786464 | tf_op jit(solution)/shard_map/ppermute | solution.py:210
  85.6 9.8 %collective-permute-start.11 = (bf16[2,48,1536]{2,1,0:T(8,128)(2,1)S(1)}, bf16[2,48,1536]{2,1,0:T(8,128)(2,1)}, u32[]{:S(2)}, u32[]{:S(2)}) collective-permute-start(bf16[2,48,1536]{2,1,0:T(8,128)(2,1)S(1)} %pad_maximum_fusion.13), channel_id=1, source_target_pairs={{0,2},{1,3},{2,0},{3,1},{8,10},{9,11},{10,8},{11,9},{16,18},{17,19... | collective-permute-start | bytes 884744 | tf_op jit(solution)/shard_map/ppermute | solution.py:64
  95.9 5.4 collective-permute-done.12
  101.3 19.8 %collective-permute-done.11 = bf16[2,48,1536]{2,1,0:T(8,128)(2,1)} collective-permute-done((bf16[2,48,1536]{2,1,0:T(8,128)(2,1)S(1)}, bf16[2,48,1536]{2,1,0:T(8,128)(2,1)}, u32[]{:S(2)}, u32[]{:S(2)}) %collective-permute-start.11) | collective-permute-done | bytes 294944 | tf_op jit(solution)/shard_map/ppermute | solution.py:64
  125.9 5.5 collective-permute-start.16
  131.4 5.4 shard_map.143
  138.3 5.6 %shard_map.144 = (bf16[1024,1536]{1,0:T(8,128)(2,1)}, bf16[1536,1024]{1,0:T(8,128)(2,1)}) custom-call(s32[1]{0:T(128)} %bitcast.refs_0_.refs_14_.core_ref, bf16[2,256,1536]{2,1,0:T(8,128)(2,1)S(1)} %pad_maximum_fusion.2.refs_1_, bf16[2,256,1536]{2,1,0:T(8,128)(2,1)} %collective-permute-done.13.refs_2_, f32[1,1536]{1,0:T(1,128)S(1)} %reshape_reshape_squeeze.3.refs_3_), custom_call_target="tpu_custom_call" | custom-call | flops 1024 | bytes 1024 | tf_op jit(solution)/shard_map/pallas_call | solution.py:291
  143.8 11.9 %fusion.41.proj_ref.refs_0_.refs_1_.refs_4_.refs_5_ = f32[1024,1920]{1,0:T(8,128)} fusion(bf16[1024,1536]{1,0:T(8,128)(2,1)} %get-tuple-element.161, bf16[1536,1920]{1,0:T(8,128)(2,1)} %bitcast.255), kind=kOutput, calls=%fused_computation.181 | convolution fusion | flops 6039797760 | bytes 16908288 | tf_op jit(solution)/shard_map/dot_general | solution.py:264
  159.9 21.0 %shard_map.145 = (f32[1024,1536]{1,0:T(8,128)}, bf16[4,128,1536]{2,1,0:T(8,128)(2,1)S(1)}, f32[128,1536]{1,0:T(8,128)}, f32[32,128]{1,0:T(8,128)}) custom-call(f32[1024,1920]{1,0:T(8,128)} %fusion.41.proj_ref.refs_0_.refs_1_.refs_4_.refs_5_, f32[8,1920]{1,0:T(8,128)S(1)} %select_maximum_fusion.taps_ref.refs_2_.refs_6_, ...), custom_call_target="tpu_custom_call" | custom-call | flops 1024 | bytes 1024 | tf_op jit(solution)/shard_map/pallas_call | solution.py:464
  182.2 5.7 %collective-permute-done.18 = bf16[2,96,1536]{2,1,0:T(8,128)(2,1)S(1)} collective-permute-done((bf16[2,96,1536]{2,1,0:T(8,128)(2,1)S(1)}, bf16[2,96,1536]{2,1,0:T(8,128)(2,1)S(1)}, u32[]{:S(2)}, u32[]{:S(2)}) %collective-permute-start.18) | collective-permute-done | bytes 589856 | tf_op jit(solution)/shard_map/ppermute | solution.py:77
  198.3 5.1 shard_map.146
  203.5 8.6 %fusion.42 = f32[1024,1536]{1,0:T(8,128)S(1)} fusion(bf16[1024,1536]{1,0:T(8,128)(2,1)} %get-tuple-element.161, bf16[1536,1536]{1,0:T(8,128)(2,1)} %bitcast.269), kind=kOutput, calls=%fused_computation.182 | convolution fusion | flops 4831838208 | bytes 14155776 | tf_op jit(solution)/shard_map/dot_general | solution.py:264
  212.1 8.1 %collective-permute-done.19 = bf16[256,1536]{1,0:T(8,128)(2,1)} collective-permute-done((bf16[256,1536]{1,0:T(8,128)(2,1)}, bf16[256,1536]{1,0:T(8,128)(2,1)}, u32[]{:S(2)}, u32[]{:S(2)}) %collective-permute-start.19) | collective-permute-done | bytes 786464 | tf_op jit(solution)/shard_map/ppermute | solution.py:210
  225.6 5.7 %shard_map.147 = (bf16[1024,1536]{1,0:T(8,128)(2,1)S(1)}, bf16[1536,1024]{1,0:T(8,128)(2,1)}) custom-call(f32[1024,1536]{1,0:T(8,128)} %get-tuple-element.259.gated_ref, f32[1024,1]{1,0:T(8,128)S(1)} %copy.56.scale_ref, f32[1,1536]{1,0:T(1,128)S(1)} %reshape_reshape.11.gain_ref), custom_call_target="tpu_custom_call" | custom-call | flops 1024 | bytes 1024 | tf_op jit(solution)/shard_map/pallas_call | solution.py:326
  231.3 9.3 %collective-permute-done.22.refs_3_ = bf16[4,96,1536]{2,1,0:T(8,128)(2,1)} collective-permute-done((bf16[4,96,1536]{2,1,0:T(8,128)(2,1)S(1)}, bf16[4,96,1536]{2,1,0:T(8,128)(2,1)}, u32[]{:S(2)}, u32[]{:S(2)}) %collective-permute-start.22) | collective-permute-done | bytes 1179680 | tf_op jit(solution)/shard_map/ppermute | solution.py:104
  254.3 5.3 convolution_convert_fusion.2
  269.5 8.6 %shard_map.149 = (f32[2,256,1536]{2,1,0:T(8,128)S(1)}, bf16[2,256,1536]{2,1,0:T(8,128)(2,1)S(1)}) custom-call(s32[1]{0:T(128)} %bitcast.refs_0_.refs_14_.core_ref, bf16[1024,1536]{1,0:T(8,128)(2,1)} %copy-done, bf16[1536,1536]{1,0:T(8,128)(2,1)} %bitcast.261), custom_call_target="tpu_custom_call" | custom-call | flops 1024 | bytes 1024 | tf_op jit(solution)/shard_map/pallas_call | solution.py:746
  278.8 7.0 %fusion.43 = f32[1024,1536]{1,0:T(8,128)S(1)} fusion(bf16[1024,1536]{1,0:T(8,128)(2,1)S(1)} %bitcast.277, bf16[1536,1536]{1,0:T(8,128)(2,1)} %bitcast.262), kind=kOutput, calls=%fused_computation.183 | convolution fusion | flops 4831838208 | bytes 14155776 | tf_op jit(solution)/shard_map/dot_general | solution.py:264
  299.1 10.6 %fusion.11 = (f32[1024,1536]{1,0:T(8,128)}, bf16[1024,1536]{1,0:T(8,128)(2,1)S(1)}) fusion(f32[1024]{0:T(1024)S(1)} %add_multiply_fusion.1, f32[1024,1536]{1,0:T(8,128)S(1)} %bitcast.253, f32[1024,1536]{1,0:T(8,128)} %copy-done.6, f32[1536]{0:T(1024)S(1)} %mul.132, f32[1024]{0:T(1024)S(1)} %add_rsqrt_fusion, f32[1024,1536]{1,0:T(8,128)} %copy-done.5, ...), kind=kLoop, calls=%fused_computation.26 | loop fusion | flops 26738688 | bytes 34617344 | tf_op jit(solution)/shard_map/mul | solution.py:928
  309.8 8.3 %convolution_convert_fusion.1 = bf16[1536,1536]{1,0:T(8,128)(2,1)S(1)} fusion(bf16[1536,1024]{1,0:T(8,128)(2,1)} %get-tuple-element.174, bf16[1024,1536]{1,0:T(8,128)(2,1)S(1)} %get-tuple-element.217), kind=kOutput, calls=%fused_computation.1 | convolution fusion | flops 4834197504 | bytes 11010048 | tf_op jit(solution)/shard_map/dot_general | solution.py:264
  331.1 47.0 %shard_map.150 = (bf16[1024,1536]{1,0:T(8,128)(2,1)}, f32[1024,128]{1,0:T(8,128)S(1)}, f32[1024,128]{1,0:T(8,128)}, f32[1024,128]{1,0:T(8,128)S(1)}, f32[8,1536]...) custom-call(f32[1024,1920]{1,0:T(8,128)} %fusion.41.proj_ref.refs_0_., ...), custom_call_target="tpu_custom_call" | custom-call | flops 1024 | bytes 1024 | tf_op jit(solution)/shard_map/pallas_call | solution.py:658
  394.6 6.8 %convolution_convert_fusion = bf16[1536,1536]{1,0:T(8,128)(2,1)} fusion(bf16[1536,1024]{1,0:T(8,128)(2,1)S(1)} %copy-done.43, bf16[1024,1536]{1,0:T(8,128)(2,1)S(1)} %copy-done.21), kind=kOutput, calls=%fused_computation | convolution fusion | flops 4834197504 | bytes 11010048 | tf_op jit(solution)/shard_map/dot_general | solution.py:264
  412.0 7.1 %fusion.44.refs_7_ = f32[1024,1536]{1,0:T(8,128)} fusion(bf16[1024,1536]{1,0:T(8,128)(2,1)S(1)} %copy-done.25, bf16[1536,1536]{1,0:T(8,128)(2,1)S(1)} %bitcast.272), kind=kOutput, calls=%fused_computation.184 | convolution fusion | flops 4831838208 | bytes 14155776 | tf_op jit(solution)/shard_map/dot_general | solution.py:264
  419.2 11.9 %shard_map.152 = (f32[2,256,1536]{2,1,0:T(8,128)S(1)}, bf16[2,256,1536]{2,1,0:T(8,128)(2,1)}) custom-call(s32[1]{0:T(128)} %bitcast.refs_0_.refs_14_.core_ref, bf16[1024,1536]{1,0:T(8,128)(2,1)} %get-tuple-element.209.refs_1_, bf16[1024,128]{1,0:T(8,128)(2,1)S(1)} %get-tuple-element.213.refs_2_, bf16[1024,128]{1,0:T(8,128)(2,1)S(1)} %convert_element_type.221.refs_3_, ...), custom_call_target="tpu_custom_call" | custom-call | flops 1024 | bytes 1024 | tf_op jit(solution)/shard_map/pallas_call | solution.py:746
  431.1 10.7 %collective-permute-done.39 = bf16[96,3072]{1,0:T(8,128)(2,1)} collective-permute-done((bf16[96,3072]{1,0:T(8,128)(2,1)}, bf16[96,3072]{1,0:T(8,128)(2,1)}, u32[]{:S(2)}, u32[]{:S(2)}) %collective-permute-start.39) | collective-permute-done | bytes 589856 | tf_op jit(solution)/shard_map/ppermute | solution.py:64
  463.5 7.3 %collective-permute-start.47 = (bf16[48,1536]{1,0:T(8,128)(2,1)}, bf16[48,1536]{1,0:T(8,128)(2,1)}, u32[]{:S(2)}, u32[]{:S(2)}) collective-permute-start(bf16[48,1536]{1,0:T(8,128)(2,1)} %get-tuple-element.316), channel_id=1, source_target_pairs={{0,4},{4,0},{1,5},{5,1},{2,6},{6,2},{3,7},{7,3},{8,12},{12,8},{9,1... | collective-permute-start | bytes 442376 | tf_op jit(solution)/shard_map/ppermute | solution.py:36
  473.9 14.0 %collective-permute-done.52 = f32[8,1664]{1,0:T(8,128)S(1)} collective-permute-done((f32[8,1664]{1,0:T(8,128)S(1)}, f32[8,1664]{1,0:T(8,128)S(1)}, u32[]{:S(2)}, u32[]{:S(2)}) %collective-permute-start.52) | collective-permute-done | bytes 53280 | tf_op jit(solution)/shard_map/ppermute | solution.py:64
  518.4 22.9 %collective-permute-done.49 = bf16[96,1792]{1,0:T(8,128)(2,1)S(1)} collective-permute-done((bf16[96,1792]{1,0:T(8,128)(2,1)S(1)}, bf16[96,1792]{1,0:T(8,128)(2,1)S(1)}, u32[]{:S(2)}, u32[]{:S(2)}) %collective-permute-start.49) | collective-permute-done | bytes 344096 | tf_op jit(solution)/shard_map/ppermute | solution.py:64
  (381 shorter events, 192.1 us)
Async XLA Ops:
  14.2 31.2 %collective-permute-start.2 = (bf16[2,48,1920]{2,1,0:T(8,128)(2,1)S(1)}, bf16[2,48,1920]{2,1,0:T(8,128)(2,1)S(1)}, u32[]{:S(2)}, u32[]{:S(2)}) collective-permute-start(bf16[2,48,1920]{2,1,0:T(8,128)(2,1)S(1)} %pad_maximum_fusion.12), channel_id=1, source_target_pairs={{0,2},{1,3},{2,0},{3,1},{8,10},{9,11},{10,8},{11,9},{16,18},{17,19... | collective-permute-start | bytes 1105928 | tf_op jit(solution)/shard_map/ppermute | solution.py:64
  14.2 31.2 %collective-permute-start.1 = (bf16[2,48,1920]{2,1,0:T(8,128)(2,1)S(1)}, bf16[2,48,1920]{2,1,0:T(8,128)(2,1)S(1)}, u32[]{:S(2)}, u32[]{:S(2)}) collective-permute-start(bf16[2,48,1920]{2,1,0:T(8,128)(2,1)S(1)} %pad_maximum_fusion.12), channel_id=1, source_target_pairs={{0,1},{1,2},{2,3},{3,0},{8,9},{9,10},{10,11},{11,8},{16,17},{17,18... | collective-permute-start | bytes 1105928 | tf_op jit(solution)/shard_map/ppermute | solution.py:64
  45.6 35.5 %collective-permute-start.6 = (bf16[4,2,48,1920]{3,2,1,0:T(8,128)(2,1)S(1)}, bf16[4,2,48,1920]{3,2,1,0:T(8,128)(2,1)S(1)}, u32[]{:S(2)}, u32[]{:S(2)}) collective-permute-start(bf16[4,2,48,1920]{3,2,1,0:T(8,128)(2,1)S(1)} %pad_maximum_fusion.6.refs_1_), channel_id=1, source_target_pairs={{0,16},{1,17},{2,18},{3,19},{8,24},{9,25},{10,26},{11,27},{16,0},{... | collective-permute-start | bytes 4423688 | tf_op jit(solution)/shard_map/ppermute | solution.py:104
  46.9 34.2 %collective-permute-start.5 = (bf16[4,2,48,1920]{3,2,1,0:T(8,128)(2,1)S(1)}, bf16[4,2,48,1920]{3,2,1,0:T(8,128)(2,1)}, u32[]{:S(2)}, u32[]{:S(2)}) collective-permute-start(bf16[4,2,48,1920]{3,2,1,0:T(8,128)(2,1)S(1)} %pad_maximum_fusion.6.refs_1_), channel_id=1, source_target_pairs={{0,8},{1,9},{2,10},{3,11},{8,0},{9,1},{10,2},{11,3},{16,24},{17,25... | collective-permute-start | bytes 4423688 | tf_op jit(solution)/shard_map/ppermute | solution.py:104
  50.7 30.4 %collective-permute-start.7 = (bf16[256,1536]{1,0:T(8,128)(2,1)}, bf16[256,1536]{1,0:T(8,128)(2,1)}, u32[]{:S(2)}, u32[]{:S(2)}) collective-permute-start(bf16[256,1536]{1,0:T(8,128)(2,1)} %get-tuple-element.296), channel_id=1, source_target_pairs={{0,0},{1,4},{2,1},{3,5},{4,2},{5,6},{6,3},{7,7},{8,8},{9,12},{10,9... | collective-permute-start | bytes 2359304 | tf_op jit(solution)/shard_map/ppermute | solution.py:210
  84.1 37.0 %collective-permute-start.13 = (bf16[2,256,1536]{2,1,0:T(8,128)(2,1)S(1)}, bf16[2,256,1536]{2,1,0:T(8,128)(2,1)}, u32[]{:S(2)}, u32[]{:S(2)}) collective-permute-start(bf16[2,256,1536]{2,1,0:T(8,128)(2,1)S(1)} %pad_maximum_fusion.2.refs_1_), channel_id=1, source_target_pairs={{0,4},{4,0},{1,5},{5,1},{2,6},{6,2},{3,7},{7,3},{8,12},{12,8},{9,1... | collective-permute-start | bytes 4718600 | tf_op jit(solution)/shard_map/ppermute | solution.py:36
  85.2 35.9 %collective-permute-start.9 = (bf16[4,2,48,1920]{3,2,1,0:T(8,128)(2,1)S(1)}, bf16[4,2,48,1920]{3,2,1,0:T(8,128)(2,1)}, u32[]{:S(2)}, u32[]{:S(2)}) collective-permute-start(bf16[4,2,48,1920]{3,2,1,0:T(8,128)(2,1)S(1)} %pad_maximum_fusion.6.refs_1_), channel_id=1, source_target_pairs={{0,24},{1,25},{2,26},{3,27},{8,16},{9,17},{10,18},{11,19},{16,8},{... | collective-permute-start | bytes 4423688 | tf_op jit(solution)/shard_map/ppermute | solution.py:104
  85.6 35.5 %collective-permute-start.11 = (bf16[2,48,1536]{2,1,0:T(8,128)(2,1)S(1)}, bf16[2,48,1536]{2,1,0:T(8,128)(2,1)}, u32[]{:S(2)}, u32[]{:S(2)}) collective-permute-start(bf16[2,48,1536]{2,1,0:T(8,128)(2,1)S(1)} %pad_maximum_fusion.13), channel_id=1, source_target_pairs={{0,2},{1,3},{2,0},{3,1},{8,10},{9,11},{10,8},{11,9},{16,18},{17,19... | collective-permute-start | bytes 884744 | tf_op jit(solution)/shard_map/ppermute | solution.py:64
  123.4 32.4 %collective-permute-start.15 = (bf16[4,2,48,1536]{3,2,1,0:T(8,128)(2,1)}, bf16[4,2,48,1536]{3,2,1,0:T(8,128)(2,1)}, u32[]{:S(2)}, u32[]{:S(2)}) collective-permute-start(bf16[4,2,48,1536]{3,2,1,0:T(8,128)(2,1)} %pad_maximum_fusion.10.refs_1_), channel_id=1, source_target_pairs={{0,16},{1,17},{2,18},{3,19},{8,24},{9,25},{10,26},{11,27},{16,0},{... | collective-permute-start | bytes 3538952 | tf_op jit(solution)/shard_map/ppermute | solution.py:104
  124.7 31.1 %collective-permute-start.14 = (bf16[4,2,48,1536]{3,2,1,0:T(8,128)(2,1)}, bf16[4,2,48,1536]{3,2,1,0:T(8,128)(2,1)}, u32[]{:S(2)}, u32[]{:S(2)}) collective-permute-start(bf16[4,2,48,1536]{3,2,1,0:T(8,128)(2,1)} %pad_maximum_fusion.10.refs_1_), channel_id=1, source_target_pairs={{0,8},{1,9},{2,10},{3,11},{8,0},{9,1},{10,2},{11,3},{16,24},{17,25... | collective-permute-start | bytes 3538952 | tf_op jit(solution)/shard_map/ppermute | solution.py:104
  125.9 29.9 %collective-permute-start.16 = (bf16[1,96,1536]{2,1,0:T(8,128)(2,1)}, bf16[1,96,1536]{2,1,0:T(8,128)(2,1)S(1)}, u32[]{:S(2)}, u32[]{:S(2)}) collective-permute-start(bf16[1,96,1536]{2,1,0:T(8,128)(2,1)} %bitcast.27), channel_id=1, source_target_pairs={{0,1},{1,0},{2,3},{3,2},{4,5},{5,4},{6,7},{7,6},{8,9},{9,8},{10,11... | collective-permute-start | bytes 884744 | tf_op jit(solution)/shard_map/ppermute | solution.py:77
  155.8 32.2 %collective-permute-start.17 = (bf16[4,2,48,1536]{3,2,1,0:T(8,128)(2,1)}, bf16[4,2,48,1536]{3,2,1,0:T(8,128)(2,1)}, u32[]{:S(2)}, u32[]{:S(2)}) collective-permute-start(bf16[4,2,48,1536]{3,2,1,0:T(8,128)(2,1)} %pad_maximum_fusion.10.refs_1_), channel_id=1, source_target_pairs={{0,24},{1,25},{2,26},{3,27},{8,16},{9,17},{10,18},{11,19},{16,8},{... | collective-permute-start | bytes 3538952 | tf_op jit(solution)/shard_map/ppermute | solution.py:104
  159.7 28.3 %collective-permute-start.18 = (bf16[2,96,1536]{2,1,0:T(8,128)(2,1)S(1)}, bf16[2,96,1536]{2,1,0:T(8,128)(2,1)S(1)}, u32[]{:S(2)}, u32[]{:S(2)}) collective-permute-start(bf16[2,96,1536]{2,1,0:T(8,128)(2,1)S(1)} %pad_maximum_fusion.11), channel_id=1, source_target_pairs={{0,2},{1,3},{2,0},{3,1},{4,6},{5,7},{6,4},{7,5},{8,10},{9,11},{10,... | collective-permute-start | bytes 1769480 | tf_op jit(solution)/shard_map/ppermute | solution.py:77
  188.0 43.3 %collective-permute-start.23 = (bf16[4,96,1536]{2,1,0:T(8,128)(2,1)S(1)}, bf16[4,96,1536]{2,1,0:T(8,128)(2,1)}, u32[]{:S(2)}, u32[]{:S(2)}) collective-permute-start(bf16[4,96,1536]{2,1,0:T(8,128)(2,1)S(1)} %constant_dynamic-update-slice_fusion.refs_1_), channel_id=1, source_target_pairs={{0,24},{1,25},{2,26},{3,27},{8,16},{9,17},{10,18},{11,19},{16,8},{... | collective-permute-start | bytes 3538952 | tf_op jit(solution)/shard_map/ppermute | solution.py:104
  188.1 52.5 %collective-permute-start.22 = (bf16[4,96,1536]{2,1,0:T(8,128)(2,1)S(1)}, bf16[4,96,1536]{2,1,0:T(8,128)(2,1)}, u32[]{:S(2)}, u32[]{:S(2)}) collective-permute-start(bf16[4,96,1536]{2,1,0:T(8,128)(2,1)S(1)} %constant_dynamic-update-slice_fusion.refs_1_), channel_id=1, source_target_pairs={{0,16},{1,17},{2,18},{3,19},{8,24},{9,25},{10,26},{11,27},{16,0},{... | collective-permute-start | bytes 3538952 | tf_op jit(solution)/shard_map/ppermute | solution.py:104
  188.6 52.0 %collective-permute-start.21 = (bf16[4,96,1536]{2,1,0:T(8,128)(2,1)S(1)}, bf16[4,96,1536]{2,1,0:T(8,128)(2,1)}, u32[]{:S(2)}, u32[]{:S(2)}) collective-permute-start(bf16[4,96,1536]{2,1,0:T(8,128)(2,1)S(1)} %constant_dynamic-update-slice_fusion.refs_1_), channel_id=1, source_target_pairs={{0,8},{1,9},{2,10},{3,11},{8,0},{9,1},{10,2},{11,3},{16,24},{17,25... | collective-permute-start | bytes 3538952 | tf_op jit(solution)/shard_map/ppermute | solution.py:104
  192.0 39.3 %collective-permute-start.24 = (bf16[256,1536]{1,0:T(8,128)(2,1)}, bf16[256,1536]{1,0:T(8,128)(2,1)}, u32[]{:S(2)}, u32[]{:S(2)}) collective-permute-start(bf16[256,1536]{1,0:T(8,128)(2,1)} %get-tuple-element.291), channel_id=1, source_target_pairs={{0,1},{1,5},{2,0},{3,4},{4,3},{5,7},{6,2},{7,6},{8,9},{9,13},{10,8... | collective-permute-start | bytes 2359304 | tf_op jit(solution)/shard_map/ppermute | solution.py:210
  322.1 59.0 %collective-permute-start.34 = (bf16[4,96,1536]{2,1,0:T(8,128)(2,1)}, bf16[4,96,1536]{2,1,0:T(8,128)(2,1)}, u32[]{:S(2)}, u32[]{:S(2)}) collective-permute-start(bf16[4,96,1536]{2,1,0:T(8,128)(2,1)} %get-tuple-element.269), channel_id=1, source_target_pairs={{0,24},{1,25},{2,26},{3,27},{8,16},{9,17},{10,18},{11,19},{16,8},{... | collective-permute-start | bytes 3538952 | tf_op jit(solution)/shard_map/ppermute | solution.py:104
  322.8 58.4 %collective-permute-start.33 = (bf16[4,96,1536]{2,1,0:T(8,128)(2,1)}, bf16[4,96,1536]{2,1,0:T(8,128)(2,1)}, u32[]{:S(2)}, u32[]{:S(2)}) collective-permute-start(bf16[4,96,1536]{2,1,0:T(8,128)(2,1)} %get-tuple-element.270), channel_id=1, source_target_pairs={{0,16},{1,17},{2,18},{3,19},{8,24},{9,25},{10,26},{11,27},{16,0},{... | collective-permute-start | bytes 3538952 | tf_op jit(solution)/shard_map/ppermute | solution.py:104
  324.0 57.2 %collective-permute-start.32 = (bf16[4,96,1536]{2,1,0:T(8,128)(2,1)}, bf16[4,96,1536]{2,1,0:T(8,128)(2,1)}, u32[]{:S(2)}, u32[]{:S(2)}) collective-permute-start(bf16[4,96,1536]{2,1,0:T(8,128)(2,1)} %get-tuple-element.271), channel_id=1, source_target_pairs={{0,8},{1,9},{2,10},{3,11},{8,0},{9,1},{10,2},{11,3},{16,24},{17,25... | collective-permute-start | bytes 3538952 | tf_op jit(solution)/shard_map/ppermute | solution.py:104
  326.1 55.1 %collective-permute-start.36 = (bf16[256,1536]{1,0:T(8,128)(2,1)}, bf16[256,1536]{1,0:T(8,128)(2,1)}, u32[]{:S(2)}, u32[]{:S(2)}) collective-permute-start(bf16[256,1536]{1,0:T(8,128)(2,1)} %get-tuple-element.287), channel_id=1, source_target_pairs={{1,0},{5,1},{0,2},{4,3},{3,4},{7,5},{2,6},{6,7},{9,8},{13,9},{8,10... | collective-permute-start | bytes 2359304 | tf_op jit(solution)/shard_map/ppermute | solution.py:221
  328.6 52.6 %collective-permute-start.35 = (bf16[256,1536]{1,0:T(8,128)(2,1)}, bf16[256,1536]{1,0:T(8,128)(2,1)}, u32[]{:S(2)}, u32[]{:S(2)}) collective-permute-start(bf16[256,1536]{1,0:T(8,128)(2,1)} %get-tuple-element.288), channel_id=1, source_target_pairs={{0,0},{4,1},{1,2},{5,3},{2,4},{6,5},{3,6},{7,7},{8,8},{12,9},{9,10... | collective-permute-start | bytes 2359304 | tf_op jit(solution)/shard_map/ppermute | solution.py:221
  392.9 38.2 %collective-permute-start.40 = (bf16[96,3072]{1,0:T(8,128)(2,1)}, bf16[96,3072]{1,0:T(8,128)(2,1)}, u32[]{:S(2)}, u32[]{:S(2)}) collective-permute-start(bf16[96,3072]{1,0:T(8,128)(2,1)} %get-tuple-element.266), channel_id=1, source_target_pairs={{0,3},{1,0},{2,1},{3,2},{8,11},{9,8},{10,9},{11,10},{16,19},{17,16... | collective-permute-start | bytes 1769480 | tf_op jit(solution)/shard_map/ppermute | solution.py:64
  394.3 47.5 %collective-permute-start.39 = (bf16[96,3072]{1,0:T(8,128)(2,1)}, bf16[96,3072]{1,0:T(8,128)(2,1)}, u32[]{:S(2)}, u32[]{:S(2)}) collective-permute-start(bf16[96,3072]{1,0:T(8,128)(2,1)} %get-tuple-element.267), channel_id=1, source_target_pairs={{0,2},{1,3},{2,0},{3,1},{8,10},{9,11},{10,8},{11,9},{16,18},{17,19... | collective-permute-start | bytes 1769480 | tf_op jit(solution)/shard_map/ppermute | solution.py:64
  394.3 47.5 %collective-permute-start.38 = (bf16[96,3072]{1,0:T(8,128)(2,1)}, bf16[96,3072]{1,0:T(8,128)(2,1)}, u32[]{:S(2)}, u32[]{:S(2)}) collective-permute-start(bf16[96,3072]{1,0:T(8,128)(2,1)} %get-tuple-element.268), channel_id=1, source_target_pairs={{0,1},{1,2},{2,3},{3,0},{8,9},{9,10},{10,11},{11,8},{16,17},{17,18... | collective-permute-start | bytes 1769480 | tf_op jit(solution)/shard_map/ppermute | solution.py:64
  409.0 32.8 %collective-permute-start.41 = (bf16[4,96,1792]{2,1,0:T(8,128)(2,1)}, bf16[4,96,1792]{2,1,0:T(8,128)(2,1)}, u32[]{:S(2)}, u32[]{:S(2)}) collective-permute-start(bf16[4,96,1792]{2,1,0:T(8,128)(2,1)} %pad_maximum_fusion.7), channel_id=1, source_target_pairs={{0,8},{1,9},{2,10},{3,11},{8,0},{9,1},{10,2},{11,3},{16,24},{17,25... | collective-permute-start | bytes 4128776 | tf_op jit(solution)/shard_map/ppermute | solution.py:104
  410.7 31.1 %collective-permute-start.42 = (bf16[4,96,1792]{2,1,0:T(8,128)(2,1)}, bf16[4,96,1792]{2,1,0:T(8,128)(2,1)}, u32[]{:S(2)}, u32[]{:S(2)}) collective-permute-start(bf16[4,96,1792]{2,1,0:T(8,128)(2,1)} %pad_maximum_fusion.8), channel_id=1, source_target_pairs={{0,16},{1,17},{2,18},{3,19},{8,24},{9,25},{10,26},{11,27},{16,0},{... | collective-permute-start | bytes 4128776 | tf_op jit(solution)/shard_map/ppermute | solution.py:104
  455.0 49.3 %collective-permute-start.46 = (bf16[4,96,1792]{2,1,0:T(8,128)(2,1)S(1)}, bf16[4,96,1792]{2,1,0:T(8,128)(2,1)S(1)}, u32[]{:S(2)}, u32[]{:S(2)}) collective-permute-start(bf16[4,96,1792]{2,1,0:T(8,128)(2,1)S(1)} %pad_maximum_fusion.9), channel_id=1, source_target_pairs={{0,24},{1,25},{2,26},{3,27},{8,16},{9,17},{10,18},{11,19},{16,8},{... | collective-permute-start | bytes 4128776 | tf_op jit(solution)/shard_map/ppermute | solution.py:104
  457.3 47.0 %collective-permute-start.45 = (bf16[256,1536]{1,0:T(8,128)(2,1)}, bf16[256,1536]{1,0:T(8,128)(2,1)}, u32[]{:S(2)}, u32[]{:S(2)}) collective-permute-start(bf16[256,1536]{1,0:T(8,128)(2,1)} %get-tuple-element.281), channel_id=1, source_target_pairs={{1,0},{5,1},{0,2},{4,3},{3,4},{7,5},{2,6},{6,7},{9,8},{13,9},{8,10... | collective-permute-start | bytes 2359304 | tf_op jit(solution)/shard_map/ppermute | solution.py:221
  460.6 43.7 %collective-permute-start.44 = (bf16[256,1536]{1,0:T(8,128)(2,1)}, bf16[256,1536]{1,0:T(8,128)(2,1)}, u32[]{:S(2)}, u32[]{:S(2)}) collective-permute-start(bf16[256,1536]{1,0:T(8,128)(2,1)} %get-tuple-element.282), channel_id=1, source_target_pairs={{0,0},{4,1},{1,2},{5,3},{2,4},{6,5},{3,6},{7,7},{8,8},{12,9},{9,10... | collective-permute-start | bytes 2359304 | tf_op jit(solution)/shard_map/ppermute | solution.py:221
  510.9 30.4 %collective-permute-start.49 = (bf16[96,1792]{1,0:T(8,128)(2,1)S(1)}, bf16[96,1792]{1,0:T(8,128)(2,1)S(1)}, u32[]{:S(2)}, u32[]{:S(2)}) collective-permute-start(bf16[96,1792]{1,0:T(8,128)(2,1)S(1)} %get-tuple-element.277), channel_id=1, source_target_pairs={{0,2},{1,3},{2,0},{3,1},{8,10},{9,11},{10,8},{11,9},{16,18},{17,19... | collective-permute-start | bytes 1032200 | tf_op jit(solution)/shard_map/ppermute | solution.py:64
  510.9 30.4 %collective-permute-start.48 = (bf16[96,1792]{1,0:T(8,128)(2,1)S(1)}, bf16[96,1792]{1,0:T(8,128)(2,1)S(1)}, u32[]{:S(2)}, u32[]{:S(2)}) collective-permute-start(bf16[96,1792]{1,0:T(8,128)(2,1)S(1)} %get-tuple-element.278), channel_id=1, source_target_pairs={{0,1},{1,2},{2,3},{3,0},{8,9},{9,10},{10,11},{11,8},{16,17},{17,18... | collective-permute-start | bytes 1032200 | tf_op jit(solution)/shard_map/ppermute | solution.py:64
  (80 other events, 780.9 us)
